TPU v7x, 32 devices: a whole 2x2x4 slice. The times are simulated.
32 devices in a mesh: region: 16 (over z, x, core), member: 2 (over y).
Axes of the slice: x: 2, y: 2, z: 4, core: 2. Of those that a mesh axis runs over, the one named last changes fastest.
Arguments:
- state: float32 [1024, 32, 256], P('member', 'region'), may hold values from -8 to 8
- neighbours: int32 [32, 5], replicated, may hold values from 0 to 31, as said below
- obs_cell: int32 [32, 2, 64], replicated, may hold values from 0 to 255
- obs_values: float32 [32, 2, 64], replicated, may hold values from -6 to 6
- obs_var: float32 [32, 2, 64], replicated, may hold values from 0.25 to 1
Outputs:
- analysis: float32 [1024, 32, 256], P('member', 'region')
Inputs may be any that keep to these rules, and one draw needn't show every extreme that they name: `neighbours`: patch g lies in region g // 2. Each patch lists 5 different patches in some order: two of the region before its own and two of the region after it (regions wrap around), and one other patch of its own region.
All inputs are finite; a program needn't handle non-finite values.
Results may differ from a plain program's by a relative error of at most 0.0003.
Values sent between devices are 32-bit elements; how exact they have to be, the bound alone decides.
No kernel may reach another device: no remote copies, remote signals or barrier semaphores. Data moves between devices by JAX's collectives and lax.ppermute only.
A program may use at most 128 MiB of HBM per device.

v0:
```python
import functools
import math

import jax
import jax.numpy as jnp
from jax import lax
from jax.experimental import pallas as pl
from jax.experimental.pallas import tpu as pltpu
from jax.sharding import PartitionSpec as P

NBATCH = 2
HIGHEST = lax.Precision.HIGHEST
F32 = jnp.float32
BF16 = jnp.bfloat16
VMEM = pl.BlockSpec(memory_space=pltpu.VMEM)
SMEM = pl.BlockSpec(memory_space=pltpu.SMEM)
NN = (((1,), (0,)), ((), ()))
NT = (((1,), (1,)), ((), ()))
TN = (((0,), (0,)), ((), ()))
RESIDUAL = 1e-3
FACTOR_LIMIT = 24
MOST_STEPS = 15
TILE = 256
CHUNK = 128


def call(kernel, outs, ins, args, scratch=(), flops=0, limit=16, aliases=None):
    shapes = [jax.ShapeDtypeStruct(shape, dtype) for shape, dtype, _ in outs]
    moved = sum(math.prod(s.shape) * s.dtype.itemsize for s in shapes)
    moved += sum(a.size * a.dtype.itemsize for a in args)
    return pl.pallas_call(
        kernel,
        out_shape=shapes,
        in_specs=ins,
        out_specs=[space for _, _, space in outs],
        scratch_shapes=list(scratch),
        input_output_aliases=aliases or {},
        compiler_params=pltpu.CompilerParams(vmem_limit_bytes=limit * 1024 * 1024),
        cost_estimate=pl.CostEstimate(flops=flops, bytes_accessed=moved, transcendentals=0),
    )(*args)


def split(x):
    high = x.astype(BF16)
    return high, (x - high.astype(F32)).astype(BF16)


def dot(a, b, dims=NN):
    return lax.dot_general(a, b, dims, preferred_element_type=F32)


def dot3(a, b, dims=NN):
    (left,), (right,) = dims[0]
    lhs = jnp.concatenate([a[0], a[0], a[1]], axis=left)
    rhs = jnp.concatenate([b[0], b[1], b[0]], axis=right)
    return dot(lhs, rhs, dims)


def select(hot, parts, dims):
    (left,), (right,) = dims[0]
    hot = hot.astype(BF16)
    lhs = jnp.concatenate([hot] * len(parts), axis=left)
    return dot(lhs, jnp.concatenate(parts, axis=right), dims)


def split_all(x):
    high, middle = split(x)
    low = x - high.astype(F32) - middle.astype(F32)
    return high, middle, low.astype(BF16)


def step_limits():
    limits = []
    for steps in range(MOST_STEPS):
        rho = RESIDUAL
        for _ in range(steps):
            rho = math.sqrt(2.0 * rho / (1.0 + rho))
        limits.append(2.0 * rho / (1.0 - rho) if rho < 1.0 else math.inf)
    return limits


def diagonal(n, columns, first):
    row = lax.broadcasted_iota(jnp.int32, (n, columns), 0)
    column = lax.broadcasted_iota(jnp.int32, (n, columns), 1)
    return row + first == column


def selector(picks, cells, scratch):
    per_patch = picks.shape[1]
    scratch[...] = jnp.full_like(scratch, -1)
    scratch[0:1, 0:per_patch] = picks
    grid = lax.broadcasted_iota(jnp.int32, (cells, scratch.shape[1]), 0)
    hot = (grid == scratch[0:1, :]).astype(F32)
    return jnp.transpose(hot)[0:per_patch, :]


def pick_kernel(region_ref, cells_ref, state_ref, rows_ref, scratch, field_ref):
    patches, cells = state_ref.shape[1:]
    for p in range(patches):
        field_ref[p] = state_ref[:, p, :]
        hot = selector(cells_ref[pl.ds(region_ref[0] * patches + p, 1), 0, :], cells, scratch)
        rows_ref[p] = select(hot, split_all(field_ref[p]), NT)


def sort_kernel(column_ref, values_hbm, var_hbm, state_ref, *refs):
    keep_ref, send_ref, values_ref, var_ref, sems = refs[-5:]
    copies = [
        pltpu.make_async_copy(values_hbm, values_ref, sems.at[0]),
        pltpu.make_async_copy(var_hbm, var_ref, sems.at[1]),
    ]
    for copy in copies:
        copy.start()
    column = column_ref[0]
    first, second = state_ref[:, 0, :], state_ref[:, 1, :]
    keep_ref[...] = jnp.where(column == 0, first, second)
    send_ref[...] = jnp.where(column == 0, second, first)
    for copy in copies:
        copy.wait()


def table(patches, own, near_ref, values_ref, var_ref, batch, flat):
    per_patch = values_ref.shape[2]
    blocks = len(patches)
    flat[...] = jnp.ones_like(flat)
    for i, patch in enumerate(patches):
        widening = (patch == own).astype(jnp.int32)
        for j in range(near_ref.shape[0]):
            widening = widening + (near_ref[j, own] == patch).astype(jnp.int32) * (j + 2)
        flat[i : i + 1, 0:per_patch] = values_ref[pl.ds(patch, 1), batch, :]
        noise = var_ref[pl.ds(patch, 1), batch, :] * widening.astype(F32)
        flat[blocks + i : blocks + i + 1, 0:per_patch] = noise
    upright = jnp.transpose(flat[...])[0:per_patch]
    return [(upright[:, i : i + 1], upright[:, blocks + i : blocks + i + 1]) for i in range(blocks)]


def scale_block(i, piece, sources, column, members, sh_ref, sl_ref, d_ref):
    value, noise = column
    rows = [sources[which][index] for which, index, _ in piece]
    total = sum(jnp.sum(part, axis=1, keepdims=True) for part in rows)
    mean = total * (1.0 / members)
    scale = lax.rsqrt(noise * (members - 1.0))
    per_patch = value.shape[0]
    at = slice(i * per_patch, (i + 1) * per_patch)
    for part, (_, _, start) in zip(rows, piece):
        size = part.shape[1]
        lanes = slice(start * size, (start + 1) * size)
        sh_ref[at, lanes], sl_ref[at, lanes] = split((part - mean) * scale)
    d_ref[at, :] = jnp.broadcast_to((value - mean) * scale, (per_patch, d_ref.shape[1]))


def prepare_kernel(pieces, batch, members, patches_of, places, *refs):
    place_refs, refs = refs[:places], refs[places:]
    near_ref, values_ref, var_ref, ah_ref, al_ref, *refs = refs
    sources, (sh_ref, sl_ref, d_ref, g_ref, cross_ref, flat) = refs[:-6], refs[-6:]
    patches, own = patches_of(*place_refs)
    columns = table(patches[: len(pieces)], own, near_ref, values_ref, var_ref, batch, flat)
    for i, piece in enumerate(pieces):
        scale_block(i, piece, sources, columns[i], members, sh_ref, sl_ref, d_ref)
    count = len(pieces) * values_ref.shape[2]
    s = (sh_ref[0:count], sl_ref[0:count])
    g_ref[0:count, 0:count] = dot3(s, s, NT)
    cross_ref[0:count] = dot3(s, (ah_ref[...], al_ref[...]))


def factor_kernel(pieces, batch, members, chunk, patches_of, places, ready, *refs):
    place_refs, refs = refs[:places], refs[places:]
    near_ref, values_ref, var_ref, *refs = refs
    refs, (flat, eye_ref, x_ref, wa, wb) = refs[:-5], refs[-5:]
    if ready:
        refs, cross_ref = refs[:-1], refs[-1]
    refs, (sh_ref, sl_ref, d_ref, g_ref, xh_ref, xl_ref, n_ref) = refs[:-7], refs[-7:]
    if ready:
        refs, (ah_ref, al_ref) = refs[:-7], refs[-7:-5]
    sources = refs
    per_patch = values_ref.shape[2]
    blocks = len(pieces)
    patches, own = patches_of(*place_refs)
    columns = table(patches[ready:], own, near_ref, values_ref, var_ref, batch, flat)
    for i in range(ready, blocks):
        scale_block(i, pieces[i], sources, columns[i - ready], members, sh_ref, sl_ref, d_ref)
    n = sh_ref.shape[0]
    head = min(TILE, n)
    tail = n - head
    chunks = [(i, min(i + chunk, n)) for i in range(0, n, chunk)]
    left = (sh_ref[0:head], sl_ref[0:head])
    fresh = ready * per_patch
    g_ref[fresh:n, 0:head] = dot3((sh_ref[fresh:n], sl_ref[fresh:n]), left, NT)
    low = (sh_ref[head:n], sl_ref[head:n])
    g_ref[head:n, head:n] = dot3(low, low, NT)
    g_ref[0:head, head:n] = jnp.transpose(g_ref[head:n, 0:head])
    if ready:
        cross_ref[fresh:n] = dot3((sh_ref[fresh:n], sl_ref[fresh:n]), (ah_ref[...], al_ref[...]))
    g = g_ref[...]
    square = jnp.sum(jnp.sum(g * g, axis=0, keepdims=True), axis=1, keepdims=True)
    norm = jnp.sqrt(square) * (1.0 + 1e-5)
    size = square[0, 0]
    limits = step_limits()
    pairs = jnp.int32(0)
    for k in range(7, MOST_STEPS - 2, 2):
        limit = limits[k] * (1.0 - 1e-4)
        pairs = pairs + (size > limit * limit).astype(jnp.int32)
    n_ref[0] = (size > 1.6e7).astype(jnp.int32) + (size > 1e8).astype(jnp.int32)
    eye_ref[...] = diagonal(n, n, 0).astype(F32)
    eye = eye_ref[...]
    first = 2.0 / (2.0 + norm)
    rho = norm * (0.5 * first)
    rho2 = rho * rho
    weight = 2.0 / (2.0 - rho2)
    keep = 0.5 * rho2 * weight
    r = (1.0 - first) * eye - first * g
    parts = split(r)
    x = (weight * first) * (eye + r)
    x_ref[...] = x
    for i, part in enumerate(split(x)):
        wa[i, :, n : 2 * n] = part

    def store(targets, start, left, corner):
        blocks = [(slice(0, n), slice(start, start + head), left)]
        blocks.append((slice(head, n), slice(start + head, start + n), corner))
        blocks.append((slice(0, head), slice(start + head, start + n), jnp.transpose(left[head:n])))
        for rows, columns, block in blocks:
            for target, part in zip(targets, split(block)):
                target[rows, columns] = part

    def corner_of(weight, keep, left, corner):
        left = weight * left - keep * eye_ref[:, 0:head]
        return left, weight * corner - keep * eye_ref[head:n, head:n]

    left = dot3(parts, [part[:, 0:head] for part in parts])
    corner = dot3([part[head:n] for part in parts], [part[:, head:n] for part in parts])
    store((wa.at[0], wa.at[1]), 0, *corner_of(weight, keep, left, corner))

    def advance(source, target, rho2):
        weight = 2.0 / (2.0 - rho2)
        keep = 0.5 * rho2 * weight
        parts = (source[0, :, 0:n], source[1, :, 0:n])
        ends = [jnp.concatenate([source[i, :, head:n], source[i, :, n + head : 2 * n]], axis=1) for i in (0, 1)]
        left = dot3(parts, (source[0, :, 0:head], source[1, :, 0:head]))
        corners = dot3([part[head:n] for part in parts], ends)
        both = (target.at[0], target.at[1])
        store(both, 0, *corner_of(weight, keep, left, corners[:, 0:tail]))
        left = dot3(parts, (source[0, :, n : n + head], source[1, :, n : n + head]))
        left = weight * (x_ref[:, 0:head] + left)
        corner = weight * (x_ref[head:n, head:n] + corners[:, tail : 2 * tail])
        x_ref[:, 0:head] = left
        x_ref[head:n, head:n] = corner
        store(both, n, left, corner)
        return keep * keep

    rho2 = keep * keep

    def sides(source, span):
        return [source[i, span[0] : span[1], 0:n] for i in (0, 1)]

    def put(targets, start, span, block):
        for target, part in zip(targets, split(block)):
            target[span[0] : span[1], start : start + head] = part
        low = max(span[0], head)
        if low < span[1]:
            for target, part in zip(targets, split(jnp.transpose(block[low - span[0] :]))):
                target[0:head, start + low : start + span[1]] = part

    def put_corner(targets, start, block):
        for target, part in zip(targets, split(block)):
            target[head:n, start + head : start + n] = part

    def put_x(targets, start, weight, span, product):
        x = weight * (x_ref[span[0] : span[1], 0:head] + product)
        x_ref[span[0] : span[1], 0:head] = x
        put(targets, start, span, x)

    def put_x_corner(targets, start, weight, product):
        x = weight * (x_ref[head:n, head:n] + product)
        x_ref[head:n, head:n] = x
        put_corner(targets, start, x)

    waiting = None
    source, target = wa, wb
    for _ in range(5):
        weight = 2.0 / (2.0 - rho2)
        keep = 0.5 * rho2 * weight
        first = (source[0, :, 0:head], source[1, :, 0:head])
        r = []
        for k, span in enumerate(chunks):
            r.append(dot3(sides(source, span), first))
            if waiting is not None:
                put_x((source.at[0], source.at[1]), n, waiting[0], span, waiting[1][k])
        if waiting is not None:
            put_x_corner((source.at[0], source.at[1]), n, waiting[0], waiting[2])
        ends = [jnp.concatenate([source[i, :, head:n], source[i, :, n + head : 2 * n]], axis=1) for i in (0, 1)]
        corners = dot3(sides(source, (head, n)), ends)
        first = (source[0, :, n : n + head], source[1, :, n : n + head])
        both = (target.at[0], target.at[1])
        x = []
        for k, span in enumerate(chunks):
            x.append(dot3(sides(source, span), first))
            put(both, 0, span, weight * r[k] - keep * eye_ref[span[0] : span[1], 0:head])
        put_corner(both, 0, weight * corners[:, 0:tail] - keep * eye_ref[head:n, head:n])
        waiting = (weight, x, corners[:, tail : 2 * tail])
        rho2 = keep * keep
        source, target = target, source
    for k, span in enumerate(chunks):
        put_x((source.at[0], source.at[1]), n, waiting[0], span, waiting[1][k])
    put_x_corner((source.at[0], source.at[1]), n, waiting[0], waiting[2])

    def twice(_, rho2):
        return advance(target, source, advance(source, target, rho2))

    rho2 = lax.fori_loop(0, pairs, twice, rho2)
    weight = 2.0 / (2.0 - rho2)
    first = (source[0, :, n : n + head], source[1, :, n : n + head])
    done = (xh_ref, xl_ref)
    ends = [source[i, :, n + head : 2 * n] for i in (0, 1)]
    put_x_corner(done, 0, weight, dot3(sides(source, (head, n)), ends))
    x = [dot3(sides(source, span), first) for span in chunks]
    for k, span in enumerate(chunks):
        put_x(done, 0, weight, span, x[k])


def centred(fields):
    members = sum(field.shape[0] for field in fields)
    mean = sum(jnp.sum(field, axis=0, keepdims=True) for field in fields) * (1.0 / members)
    pairs = [split(field - mean) for field in fields]
    return [jnp.concatenate(parts, axis=0) for parts in zip(*pairs)], mean


def in_chunks(count, product, work):
    waiting = None
    for start in range(0, count, CHUNK):
        span = slice(start, min(start + CHUNK, count))
        result = product(span)
        if waiting is not None:
            work(*waiting)
        waiting = (span, result)
    work(*waiting)


def solve(n_ref, s, g_ref, x, anomaly, z_ref, cross_ref, parts_ref, crossed_already=False):
    n = z_ref.shape[0]

    def keep(slot, span, value):
        for i, part in enumerate(split(value)):
            parts_ref[slot, i, span] = part

    def kept(slot):
        return parts_ref[slot, 0], parts_ref[slot, 1]

    def some(parts, span):
        return [part[span] for part in parts]

    def crossed(span, value):
        cross_ref[span] = value
        keep(0, span, value)

    def solved(span, value):
        z_ref[span] = value
        keep(1, span, value)

    def left(span, value):
        keep(0, span, cross_ref[span] - z_ref[span] - value)

    def refined(span, value):
        z_ref[span] = z_ref[span] + value

    if crossed_already:
        keep(0, slice(0, n), cross_ref[...])
    else:
        in_chunks(n, lambda span: dot3(some(s, span), [part[...] for part in anomaly]), crossed)
    in_chunks(n, lambda span: dot3(some(x, span), kept(0)), solved)
    in_chunks(n, lambda span: dot3(split(g_ref[span]), kept(1)), left)
    in_chunks(n, lambda span: dot3(some(x, span), kept(0)), refined)

    def refine(_, carry):
        z = z_ref[...]
        gz = lax.dot_general(g_ref[...], z, NN, precision=HIGHEST, preferred_element_type=F32)
        z_ref[...] = z + dot3([part[...] for part in x], split(cross_ref[...] - z - gz))
        return carry

    lax.fori_loop(0, n_ref[0], refine, 0)


def gain_kernel(batch, parts, own_of, region_ref, column_ref, n_ref, cells_ref, sh_ref, sl_ref, d_ref, g_ref, *refs):
    xh_ref, xl_ref, *refs = refs
    states = refs[:parts]
    z_ref, rows_ref, scratch, anomaly_ref, cross_ref, parts_ref = refs[parts:]
    anomaly, mean = centred([state[...] for state in states])
    for i, part in enumerate(anomaly):
        anomaly_ref[i] = part
    anomaly = (anomaly_ref.at[0], anomaly_ref.at[1])
    solve(n_ref, (sh_ref, sl_ref), g_ref, (xh_ref, xl_ref), anomaly, z_ref, cross_ref, parts_ref)
    s = (sh_ref[...], sl_ref[...])
    picks = cells_ref[pl.ds(own_of(region_ref, column_ref), 1), batch, :]
    hot = selector(picks, mean.shape[1], scratch)
    zt = split(select(hot, split(z_ref[...]), NT))
    base = jnp.sum(hot * mean, axis=1, keepdims=True) + dot3(zt, split(d_ref[...]))[:, 0:1]
    picked = select(hot, [part[...] for part in anomaly], NT)
    rows_ref[...] = base + picked - 0.5 * dot3(zt, s)


def updated(field, start, s, shift, z):
    size = field.shape[0]
    return field + shift - 0.5 * dot3([h[:, start : start + size] for h in s], z, TN)


def shift_of(z, d_ref):
    return jnp.sum(z * d_ref[:, 0:1], axis=0, keepdims=True)


def update_kernel(starts, sh_ref, sl_ref, d_ref, z_ref, *refs):
    count = len(starts)
    states, outs, parts = refs[:count], refs[count : 2 * count], refs[2 * count :]
    z = z_ref[...]
    shift = shift_of(z, d_ref)
    s, zs = (sh_ref[...], sl_ref[...]), split(z)
    for start, state, out in zip(starts, states, outs):
        out[...] = updated(state[...], start, s, shift, zs)
    if parts:
        anomaly, _ = centred([out[...] for out in outs])
        for ref, part in zip(parts, anomaly):
            ref[...] = part


def last_kernel(n_ref, sh_ref, sl_ref, d_ref, g_ref, xh_ref, xl_ref, state_ref, *refs):
    cross, z_ref, out_ref, scratch_ref, parts_ref = refs if len(refs) == 5 else (None, *refs)
    given = cross is not None
    cross_ref = cross if given else scratch_ref
    anomaly = None if given else centred([state_ref[...]])[0]
    x = (xh_ref, xl_ref)
    solve(n_ref, (sh_ref, sl_ref), g_ref, x, anomaly, z_ref, cross_ref, parts_ref, given)
    z = z_ref[...]
    start = sh_ref.shape[1] - state_ref.shape[0]
    s = (sh_ref[...], sl_ref[...])
    out_ref[...] = updated(state_ref[...], start, s, shift_of(z, d_ref), split(z))


def join_kernel(column_ref, mine_ref, theirs_ref, out_ref, both, sems):
    chunks = sems.shape[0]
    size = both.shape[0] // chunks
    column = column_ref[0]
    copies = []
    for i in range(chunks):
        at = slice(i * size, (i + 1) * size)
        mine, theirs = mine_ref[at, :], theirs_ref[at, :]
        both[at, 0, :] = jnp.where(column == 0, mine, theirs)
        both[at, 1, :] = jnp.where(column == 0, theirs, mine)
        span = pl.ds(i * size, size)
        copies.append(pltpu.make_async_copy(both.at[span], out_ref.at[span], sems.at[i]))
        copies[-1].start()
    for copy in copies:
        copy.wait()


def prepare(pieces, batch, members, patches_of, place, near, values, var, anomaly, sources, n):
    width = anomaly[0].shape[1]
    outs = [
        ((n, members), BF16, VMEM),
        ((n, members), BF16, VMEM),
        ((n, 128), F32, VMEM),
        ((n, n), F32, VMEM),
        ((n, width), F32, VMEM),
    ]
    kernel = functools.partial(prepare_kernel, pieces, batch, members, patches_of, len(place))
    args = [*place, near, values, var, *anomaly, *sources]
    ins = [SMEM] * (len(place) + 1) + [VMEM] * (len(args) - len(place) - 1)
    return call(kernel, outs, ins, args, [pltpu.VMEM((128, 128), F32)], 6 * n * width * members)


def factor(pieces, batch, members, chunk, patches_of, place, near, values, var, sources, ready=0, before=()):
    per_patch = values.shape[2]
    n = len(pieces) * per_patch
    outs = [
        ((n, members), BF16, VMEM),
        ((n, members), BF16, VMEM),
        ((n, 128), F32, VMEM),
        ((n, n), F32, VMEM),
        ((n, n), BF16, VMEM),
        ((n, n), BF16, VMEM),
        ((1,), jnp.int32, SMEM),
    ]
    args = [*place, near, values, var, *sources, *before]
    aliases = {}
    if ready:
        outs.append((before[-1].shape, F32, VMEM))
        first = len(args) - 5
        aliases = {first: 0, first + 1: 1, first + 2: 2, first + 3: 3, first + 4: 7}
    scratch = [
        pltpu.VMEM((128, 128), F32),
        pltpu.VMEM((n, n), F32),
        pltpu.VMEM((n, n), F32),
        pltpu.VMEM((2, n, 2 * n), BF16),
        pltpu.VMEM((2, n, 2 * n), BF16),
    ]
    kernel = functools.partial(factor_kernel, pieces, batch, members, chunk, patches_of, len(place), ready)
    flops = 6 * n * n * members + 60 * n * n * n
    ins = [SMEM] * (len(place) + 1) + [VMEM] * (len(args) - len(place) - 1)
    return call(kernel, outs, ins, args, scratch, flops, FACTOR_LIMIT, aliases)


def solver_scratch(n, width):
    return [pltpu.VMEM((n, width), F32), pltpu.VMEM((2, 2, n, width), BF16)]


def gain(batch, own_of, place, cells, factored, states):
    sh, sl, d, g, xh, xl, more = factored[:7]
    n, members = sh.shape
    width = states[0].shape[1]
    kernel = functools.partial(gain_kernel, batch, len(states), own_of)
    outs = [((n, width), F32, VMEM), ((cells.shape[2], members), F32, VMEM)]
    ins = [SMEM] * 3 + [VMEM] * (7 + len(states))
    args = [*place, more, cells, sh, sl, d, g, xh, xl, *states]
    flops = 8 * n * members * width
    scratch = [pltpu.VMEM((8, 128), jnp.int32), pltpu.VMEM((2, members, width), BF16)]
    scratch += solver_scratch(n, width)
    return call(kernel, outs, ins, args, scratch, flops)


def update(factored, z, states, starts, more=False):
    sh, sl, d = factored[:3]
    kernel = functools.partial(update_kernel, starts)
    outs = [(state.shape, F32, VMEM) for state in states]
    if more:
        outs += [((sh.shape[1], z.shape[1]), BF16, VMEM)] * 2
    flops = 6 * sh.shape[0] * sh.shape[1] * z.shape[1]
    return call(kernel, outs, [VMEM] * (4 + len(states)), [sh, sl, d, z, *states], (), flops)


def last(factored, state):
    sh, sl, d, g, xh, xl, more, *cross = factored
    n, width = sh.shape[0], state.shape[1]
    outs = [((n, width), F32, VMEM), (state.shape, F32, VMEM)]
    args = [more, sh, sl, d, g, xh, xl, state, *cross]
    flops = 12 * sh.shape[0] * sh.shape[1] * width
    ins = [SMEM] + [VMEM] * (len(args) - 1)
    return call(last_kernel, outs, ins, args, solver_scratch(n, width), flops)


def rings(size):
    up = [(i, (i + 1) % size) for i in range(size)]
    return up, [(j, i) for i, j in up]


BOTH = ("region", "member")


def permute(x, moves, regions):
    table = []
    for region in range(regions):
        for column in range(2):
            pair, parity, to = moves(region // 2, region % 2, column)
            pair %= regions // 2
            table.append((region * 2 + column, (pair * 2 + parity) * 2 + to))
    return lax.ppermute(x, BOTH, table)


def paired(state, neighbours, obs_cell, obs_values, obs_var):
    half, _, cells = state.shape
    members = 2 * half
    regions = lax.axis_size("region")
    region, column = lax.axis_index("region"), lax.axis_index("member")
    place = (region.astype(jnp.int32)[None], column.astype(jnp.int32)[None])
    near = neighbours.T

    def own_of(region_ref, column_ref):
        return region_ref[0] * 2 + column_ref[0]

    def around(region, within):
        side = 2 * lax.rem(region, 2) - 1
        outer = lax.rem(region + regions + side, regions)
        return [r * 2 + p for p in within for r in (region, region - side, outer)]

    def patches_first(region_ref, column_ref):
        return around(region_ref[0], (0, 1)), own_of(region_ref, column_ref)

    def patches_next(region_ref, column_ref):
        column = column_ref[0]
        return around(region_ref[0], (column, 1 - column)), own_of(region_ref, column_ref)

    def across(x):
        return permute(x, lambda c, q, m: (c, q, 1 - m), regions)

    def beside(x):
        return permute(x, lambda c, q, m: (c, 1 - q, m), regions)

    def outside(x):
        return permute(x, lambda c, q, m: (c + 2 * q - 1, 1 - q, m), regions)

    anywhere = pl.BlockSpec(memory_space=pl.ANY)
    (rows,) = call(
        pick_kernel,
        [((2, obs_cell.shape[2], half), F32, VMEM)],
        [SMEM, VMEM, VMEM],
        [place[0], obs_cell, state],
        [pltpu.VMEM((8, 128), jnp.int32), pltpu.VMEM((2, half, cells), F32)],
    )
    other = across(rows)
    sources = [rows, beside(rows), outside(rows), other, beside(other), outside(other)]
    shape = ((half, cells), F32, VMEM)
    keep, send, values, var = call(
        sort_kernel,
        [shape, shape, (obs_values.shape, F32, VMEM), (obs_var.shape, F32, VMEM)],
        [SMEM, anywhere, anywhere, VMEM, anywhere],
        [place[1], obs_values, obs_var, state, other],
        [pltpu.SemaphoreType.DMA((2,))],
    )
    pieces = [[(i, (p,), 0), (3 + i, (p,), 1)] for p in range(2) for i in range(3)]
    states = [keep, across(send)]
    factored = factor(pieces, 0, members, CHUNK, patches_first, place, near, values, var, sources)
    everything = slice(None)
    low, high = (everything, slice(0, half)), (everything, slice(half, members))
    pieces = [[(i, low, 0), (i, high, 1)] for i in range(3)]
    pieces += [[(i, high, 0), (i, low, 1)] for i in range(3, 6)]
    early = 4
    for batch in range(1, NBATCH):
        z, rows = gain(batch, own_of, place, obs_cell, factored, states)
        other = across(rows)
        far = permute(rows, lambda c, q, m: (c + 2 * q - 1, 1 - q, 1 - m), regions)
        sources = [rows, beside(rows), outside(rows), other, beside(other), far]
        mine, theirs, *anomaly = update(factored, z, states, (0, half), True)
        states = [mine, theirs]
        given = (place, near, values, var)
        n = factored[0].shape[0]
        done = prepare(pieces[:early], batch, members, patches_next, *given, anomaly, sources[:early], n)
        factored = factor(
            pieces, batch, members, CHUNK, patches_next, *given, sources, early, [*anomaly, *done]
        )
    z, theirs = last(factored, states[1])
    theirs = across(theirs)
    (mine,) = update(factored, z, states[:1], (0,))
    return pl.pallas_call(
        join_kernel,
        out_shape=jax.ShapeDtypeStruct(state.shape, F32),
        in_specs=[SMEM, VMEM, VMEM],
        out_specs=anywhere,
        scratch_shapes=[pltpu.VMEM(state.shape, F32), pltpu.SemaphoreType.DMA((4,))],
        compiler_params=pltpu.CompilerParams(vmem_limit_bytes=16 * 1024 * 1024),
    )(place[1], mine, theirs)


def listed(table_ref):
    blocks = table_ref.shape[0] - 1
    return [table_ref[i] for i in range(blocks)], table_ref[blocks]


def general(state, neighbours, obs_cell, obs_values, obs_var):
    ensemble = lax.all_to_all(state, "member", split_axis=1, concat_axis=0, tiled=True)
    members, owned, cells = ensemble.shape
    regions = lax.axis_size("region")
    region_patches = owned * lax.axis_size("member")
    region = lax.axis_index("region")
    first = region * region_patches + lax.axis_index("member") * owned
    up, down = rings(regions)
    fields = [ensemble[:, p, :] for p in range(owned)]
    grid = jnp.arange(cells, dtype=jnp.int32)
    for batch in range(NBATCH):
        picks = lax.dynamic_slice_in_dim(obs_cell, first, owned, 0)[:, batch, :]
        hot = (picks[:, :, None] == grid[None, None, :]).astype(F32)
        own_rows = jnp.einsum("poc,pkc->pok", hot, jnp.stack(fields), precision=HIGHEST)
        region_rows = lax.all_gather(own_rows, "member", axis=0, tiled=True)
        before = lax.ppermute(region_rows, "region", up)
        after = lax.ppermute(region_rows, "region", down)
        beside = jnp.concatenate([before, region_rows, after], axis=0)
        new = []
        for p in range(owned):
            own = first + p
            links = lax.dynamic_index_in_dim(neighbours, own, 0, keepdims=False)
            ids = jnp.concatenate([own[None], links]).astype(jnp.int32)
            table = jnp.concatenate([ids, own[None]]).astype(jnp.int32)
            home = (ids // region_patches - region + 1) % regions
            rows = jnp.take(beside, home * region_patches + ids % region_patches, axis=0)
            pieces = [[(0, (i,), 0)] for i in range(ids.shape[0])]
            factored = factor(
                pieces, batch, members, CHUNK, listed, [table], neighbours.T, obs_values, obs_var, [rows]
            )
            new.append(last(factored, fields[p])[1])
        fields = new
    ensemble = jnp.stack(fields, axis=1)
    return lax.all_to_all(ensemble, "member", split_axis=0, concat_axis=1, tiled=True)


def on_device(state, neighbours, obs_cell, obs_values, obs_var):
    patches, links = state.shape[1], neighbours.shape[1]
    even = lax.axis_size("region") % 2 == 0
    if even and patches == 2 and lax.axis_size("member") == 2 and links + 1 == 3 * patches:
        return paired(state, neighbours, obs_cell, obs_values, obs_var)
    return general(state, neighbours, obs_cell, obs_values, obs_var)


def solution(mesh):
    in_specs = (P("member", "region", None), P(), P(), P(), P())
    out_specs = P("member", "region", None)
    return jax.shard_map(
        on_device, mesh=mesh, in_specs=in_specs, out_specs=out_specs, check_vma=False
    )
```

profile of v0, /device:TPU:0, one launch (start us, length us, event | category | flops | bytes accessed | tf_op | source)
XLA Modules:
  0.0 72.3 jit_solution(13657943913014716295)
XLA Ops:
  0.0 1.2 %copy-done = f32[512,2,256]{2,1,0:T(2,128)S(1)} copy-done((f32[512,2,256]{2,1,0:T(2,128)S(1)}, f32[512,2,256]{2,1,0:T(2,128)}, u32[]{:S(2)}) %copy-start) | copy-done | bytes 1048600
  1.2 0.8 %copy-done.2 = s32[32,2,64]{2,1,0:T(2,128)S(1)} copy-done((s32[32,2,64]{2,1,0:T(2,128)S(1)}, s32[32,2,64]{2,1,0:T(2,128)}, u32[]{:S(2)}) %copy-start.2) | copy-done | bytes 16408
  2.0 0.8 %shard_map.55.refs_5_ = f32[2,64,512]{2,1,0:T(8,128)S(1)} custom-call(s32[1]{0:T(128)} %bitcast.1.region_ref.refs_0_, s32[32,2,64]{2,1,0:T(2,128)S(1)} %copy-done.2, f32[512,2,256]{2,1,0:T(2,128)S(1)} %copy-done), custom_call_target="tpu_custom_call" | custom-call | bytes 1327108 | tf_op jit(solution)/shard_map/pallas_call | solution.py:31
  2.8 3.0 %collective-permute-start = (f32[2,64,512]{2,1,0:T(8,128)S(1)}, f32[2,64,512]{2,1,0:T(8,128)S(1)}, u32[]{:S(2)}, u32[]{:S(2)}) collective-permute-start(f32[2,64,512]{2,1,0:T(8,128)S(1)} %shard_map.55.refs_5_), channel_id=1, source_target_pairs={{0,1},{1,0},{2,3},{3,2},{4,5},{5,4},{6,7},{7,6},{8,9},{9,8},{10,11... | collective-permute-start | bytes 786440 | tf_op jit(solution)/shard_map/ppermute | solution.py:552
  5.8 3.7 %collective-permute-start.2 = (f32[2,64,512]{2,1,0:T(8,128)S(1)}, f32[2,64,512]{2,1,0:T(8,128)S(1)}, u32[]{:S(2)}, u32[]{:S(2)}) collective-permute-start(f32[2,64,512]{2,1,0:T(8,128)S(1)} %shard_map.55.refs_5_), channel_id=1, source_target_pairs={{0,30},{1,31},{2,4},{3,5},{4,2},{5,3},{6,8},{7,9},{8,6},{9,7},{10,... | collective-permute-start | bytes 786440 | tf_op jit(solution)/shard_map/ppermute | solution.py:552
  9.5 0.0 collective-permute-start.1
  9.5 2.6 %collective-permute-done.refs_0_.refs_8_ = f32[2,64,512]{2,1,0:T(8,128)S(1)} collective-permute-done((f32[2,64,512]{2,1,0:T(8,128)S(1)}, f32[2,64,512]{2,1,0:T(8,128)S(1)}, u32[]{:S(2)}, u32[]{:S(2)}) %collective-permute-start) | collective-permute-done | bytes 262176 | tf_op jit(solution)/shard_map/ppermute | solution.py:552
  12.1 3.3 %collective-permute-start.4 = (f32[2,64,512]{2,1,0:T(8,128)S(1)}, f32[2,64,512]{2,1,0:T(8,128)S(1)}, u32[]{:S(2)}, u32[]{:S(2)}) collective-permute-start(f32[2,64,512]{2,1,0:T(8,128)S(1)} %collective-permute-done.refs_0_.refs_8_), channel_id=1, source_target_pairs={{0,30},{1,31},{2,4},{3,5},{4,2},{5,3},{6,8},{7,9},{8,6},{9,7},{10,... | collective-permute-start | bytes 786440 | tf_op jit(solution)/shard_map/ppermute | solution.py:552
  15.5 0.7 shard_map.56
  16.2 0.0 copy-start.6
  16.2 1.6 %collective-permute-start.5 = (f32[512,256]{1,0:T(8,128)S(1)}, f32[512,256]{1,0:T(8,128)S(1)}, u32[]{:S(2)}, u32[]{:S(2)}) collective-permute-start(f32[512,256]{1,0:T(8,128)S(1)} %get-tuple-element.47), channel_id=1, source_target_pairs={{0,1},{1,0},{2,3},{3,2},{4,5},{5,4},{6,7},{7,6},{8,9},{9,8},{10,11... | collective-permute-start | bytes 1572872 | tf_op jit(solution)/shard_map/ppermute | solution.py:552
  17.8 0.0 collective-permute-done.2.refs_7_
  17.8 0.0 collective-permute-done.1.refs_6_
  17.8 3.0 %collective-permute-done.4.refs_10_ = f32[2,64,512]{2,1,0:T(8,128)S(1)} collective-permute-done((f32[2,64,512]{2,1,0:T(8,128)S(1)}, f32[2,64,512]{2,1,0:T(8,128)S(1)}, u32[]{:S(2)}, u32[]{:S(2)}) %collective-permute-start.4) | collective-permute-done | bytes 262176 | tf_op jit(solution)/shard_map/ppermute | solution.py:552
  20.8 7.8 %shard_map.57 = (bf16[384,1024]{1,0:T(8,128)(2,1)S(1)}, bf16[384,1024]{1,0:T(8,128)(2,1)S(1)}, f32[384,128]{1,0:T(8,128)S(1)}, f32[384,384]{1,0:T(8,128)S(1)}, b...) custom-call(s32[1]{0:T(128)} %bitcast.1.region_ref.refs_0_, s32[1]{0:T(128)} %bitcast.column_ref.refs_1_, ...), custom_call_target="tpu_custom_call" | custom-call | flops 4303355904 | bytes 4555404 | tf_op jit(solution)/shard_map/pallas_call | solution.py:31
  28.6 2.0 %collective-permute-done.5.refs_3_.refs_1_ = f32[512,256]{1,0:T(8,128)S(1)} collective-permute-done((f32[512,256]{1,0:T(8,128)S(1)}, f32[512,256]{1,0:T(8,128)S(1)}, u32[]{:S(2)}, u32[]{:S(2)}) %collective-permute-start.5) | collective-permute-done | bytes 524320 | tf_op jit(solution)/shard_map/ppermute | solution.py:552
  30.6 4.6 %shard_map.58 = (f32[384,256]{1,0:T(8,128)S(1)}, f32[64,1024]{1,0:T(8,128)S(1)}) custom-call(s32[1]{0:T(128)} %bitcast.1.region_ref.refs_0_, s32[1]{0:T(128)} %bitcast.column_ref.refs_1_, s32[1]{0:T(128)} %get-tuple-element.39.n_ref, s32[32,2,64]{2,1,0:T(2,128)S(1)} %copy-done.3, bf16[384,1024]{1,0:T(8,128)(2,1)S(1)} %get-tuple-element.40.sh_ref, ...), custom_call_target="tpu_custom_call" | custom-call | flops 805306368 | bytes 4669452 | tf_op jit(solution)/shard_map/pallas_call | solution.py:31
  35.2 1.6 %collective-permute-start.8 = (f32[64,1024]{1,0:T(8,128)S(1)}, f32[64,1024]{1,0:T(8,128)S(1)}, u32[]{:S(2)}, u32[]{:S(2)}) collective-permute-start(f32[64,1024]{1,0:T(8,128)S(1)} %get-tuple-element.48.refs_7_.refs_5_), channel_id=1, source_target_pairs={{0,1},{1,0},{2,3},{3,2},{4,5},{5,4},{6,7},{7,6},{8,9},{9,8},{10,11... | collective-permute-start | bytes 786440 | tf_op jit(solution)/shard_map/ppermute | solution.py:552
  36.8 1.0 %collective-permute-start.7 = (f32[64,1024]{1,0:T(8,128)S(1)}, f32[64,1024]{1,0:T(8,128)S(1)}, u32[]{:S(2)}, u32[]{:S(2)}) collective-permute-start(f32[64,1024]{1,0:T(8,128)S(1)} %get-tuple-element.48.refs_7_.refs_5_), channel_id=1, source_target_pairs={{0,30},{1,31},{2,4},{3,5},{4,2},{5,3},{6,8},{7,9},{8,6},{9,7},{10,... | collective-permute-start | bytes 786440 | tf_op jit(solution)/shard_map/ppermute | solution.py:552
  37.8 3.4 %collective-permute-start.10 = (f32[64,1024]{1,0:T(8,128)S(1)}, f32[64,1024]{1,0:T(8,128)S(1)}, u32[]{:S(2)}, u32[]{:S(2)}) collective-permute-start(f32[64,1024]{1,0:T(8,128)S(1)} %get-tuple-element.48.refs_7_.refs_5_), channel_id=1, source_target_pairs={{0,31},{1,30},{2,5},{3,4},{4,3},{5,2},{6,9},{7,8},{8,7},{9,6},{10,... | collective-permute-start | bytes 786440 | tf_op jit(solution)/shard_map/ppermute | solution.py:552
  41.2 2.1 %collective-permute-done.8.refs_10_.refs_8_ = f32[64,1024]{1,0:T(8,128)S(1)} collective-permute-done((f32[64,1024]{1,0:T(8,128)S(1)}, f32[64,1024]{1,0:T(8,128)S(1)}, u32[]{:S(2)}, u32[]{:S(2)}) %collective-permute-start.8) | collective-permute-done | bytes 262176 | tf_op jit(solution)/shard_map/ppermute | solution.py:552
  43.3 1.2 %shard_map.59 = (f32[512,256]{1,0:T(8,128)S(1)}, f32[512,256]{1,0:T(8,128)S(1)}, bf16[1024,256]{1,0:T(8,128)(2,1)S(1)}, bf16[1024,256]{1,0:T(8,128)(2,1)S(1)}) custom-call(bf16[384,1024]{1,0:T(8,128)(2,1)S(1)} %get-tuple-element.40.sh_ref, bf16[384,1024]{1,0:T(8,128)(2,1)S(1)} %get-tuple-element.41.sl_ref, f32[384,128]{1,0:T(8,128)S(1)} %get-tuple-element.42.d_ref, ...), custom_call_target="tpu_custom_call" | custom-call | flops 603979776 | bytes 5308416 | tf_op jit(solution)/shard_map/pallas_call | solution.py:31
  44.6 0.8 %collective-permute-done.7.refs_9_.refs_7_ = f32[64,1024]{1,0:T(8,128)S(1)} collective-permute-done((f32[64,1024]{1,0:T(8,128)S(1)}, f32[64,1024]{1,0:T(8,128)S(1)}, u32[]{:S(2)}, u32[]{:S(2)}) %collective-permute-start.7) | collective-permute-done | bytes 262176 | tf_op jit(solution)/shard_map/ppermute | solution.py:552
  45.4 0.0 collective-permute-done.6.refs_8_.refs_6_
  45.4 2.0 %shard_map.60 = (bf16[384,1024]{1,0:T(8,128)(2,1)S(1)}, bf16[384,1024]{1,0:T(8,128)(2,1)S(1)}, f32[384,128]{1,0:T(8,128)S(1)}, f32[384,384]{1,0:T(8,128)S(1)}, f32[384,256]{1,0:T(8,128)S(1)}) custom-call(s32[1]{0:T(128)} %bitcast.1.region_ref.refs_0_, s32[1]{0:T(128)} %bitcast.column_ref.refs_1_, s32[5,32]{1,0:T(8,128)S(1)} %bitcast.4, ...), custom_call_target="tpu_custom_call" | custom-call | flops 603979776 | bytes 4883080 | tf_op jit(solution)/shard_map/pallas_call | solution.py:31
  47.4 0.7 %collective-permute-done.10.refs_10_ = f32[64,1024]{1,0:T(8,128)S(1)} collective-permute-done((f32[64,1024]{1,0:T(8,128)S(1)}, f32[64,1024]{1,0:T(8,128)S(1)}, u32[]{:S(2)}, u32[]{:S(2)}) %collective-permute-start.10) | collective-permute-done | bytes 262176 | tf_op jit(solution)/shard_map/ppermute | solution.py:552
  48.1 7.0 %shard_map.61 = (bf16[384,1024]{1,0:T(8,128)(2,1)S(1)}, bf16[384,1024]{1,0:T(8,128)(2,1)S(1)}, f32[384,128]{1,0:T(8,128)S(1)}, f32[384,384]{1,0:T(8,128)S(1)}, b...) custom-call(s32[1]{0:T(128)} %bitcast.1.region_ref.refs_0_, ...), custom_call_target="tpu_custom_call", output_to_operand_aliasing={{0}: (13, {}), {1}: (14, {}), {2}: (15, {}), {3}: (16, {}),... | custom-call | flops 4303355904 | bytes 8749708 | tf_op jit(solution)/shard_map/pallas_call | solution.py:31
  55.2 2.6 %shard_map.62 = (f32[384,256]{1,0:T(8,128)S(1)}, f32[512,256]{1,0:T(8,128)S(1)}) custom-call(s32[1]{0:T(128)} %get-tuple-element.60.n_ref, bf16[384,1024]{1,0:T(8,128)(2,1)S(1)} %get-tuple-element.57.sh_ref, bf16[384,1024]{1,0:T(8,128)(2,1)S(1)} %get-tuple-element.58.sl_ref, f32[384,128]{1,0:T(8,128)S(1)} %get-tuple-element.59.d_ref, ...), custom_call_target="tpu_custom_call" | custom-call | flops 1207959552 | bytes 4784132 | tf_op jit(solution)/shard_map/pallas_call | solution.py:31
  57.8 1.6 %collective-permute-start.11 = (f32[512,256]{1,0:T(8,128)S(1)}, f32[512,256]{1,0:T(8,128)S(1)}, u32[]{:S(2)}, u32[]{:S(2)}) collective-permute-start(f32[512,256]{1,0:T(8,128)S(1)} %get-tuple-element.68), channel_id=1, source_target_pairs={{0,1},{1,0},{2,3},{3,2},{4,5},{5,4},{6,7},{7,6},{8,9},{9,8},{10,11... | collective-permute-start | bytes 1572872 | tf_op jit(solution)/shard_map/ppermute | solution.py:552
  59.3 0.6 shard_map.63.mine_ref
  59.9 11.1 %collective-permute-done.11.theirs_ref = f32[512,256]{1,0:T(8,128)S(1)} collective-permute-done((f32[512,256]{1,0:T(8,128)S(1)}, f32[512,256]{1,0:T(8,128)S(1)}, u32[]{:S(2)}, u32[]{:S(2)}) %collective-permute-start.11) | collective-permute-done | bytes 524320 | tf_op jit(solution)/shard_map/ppermute | solution.py:552
  71.0 1.1 %shard_map.64 = f32[512,2,256]{2,1,0:T(2,128)} custom-call(s32[1]{0:T(128)} %bitcast.column_ref.refs_1_, f32[512,256]{1,0:T(8,128)S(1)} %shard_map.63.mine_ref, f32[512,256]{1,0:T(8,128)S(1)} %collective-permute-done.11.theirs_ref), custom_call_target="tpu_custom_call" | custom-call | tf_op jit(solution)/shard_map/pallas_call | solution.py:629
  (16 shorter events, 0.0 us)
Async XLA Ops:
  0.0 1.2 %copy-start = (f32[512,2,256]{2,1,0:T(2,128)S(1)}, f32[512,2,256]{2,1,0:T(2,128)}, u32[]{:S(2)}) copy-start(f32[512,2,256]{2,1,0:T(2,128)} %state_ref.3) | copy-start | bytes 3145732
  1.2 0.8 %copy-start.2 = (s32[32,2,64]{2,1,0:T(2,128)S(1)}, s32[32,2,64]{2,1,0:T(2,128)}, u32[]{:S(2)}) copy-start(s32[32,2,64]{2,1,0:T(2,128)} %cells_ref.3) | copy-start | bytes 49156
  2.0 13.5 %copy-start.1 = (f32[512,2,256]{2,1,0:T(2,128)S(1)}, f32[512,2,256]{2,1,0:T(2,128)}, u32[]{:S(2)}) copy-start(f32[512,2,256]{2,1,0:T(2,128)} %state_ref.3) | copy-start | bytes 3145732
  2.0 13.5 %copy-start.4 = (f32[32,2,64]{2,1,0:T(2,128)S(1)}, f32[32,2,64]{2,1,0:T(2,128)}, u32[]{:S(2)}) copy-start(f32[32,2,64]{2,1,0:T(2,128)} %values_hbm.1) | copy-start | bytes 49156
  2.0 13.5 %copy-start.5 = (f32[32,2,64]{2,1,0:T(2,128)S(1)}, f32[32,2,64]{2,1,0:T(2,128)}, u32[]{:S(2)}) copy-start(f32[32,2,64]{2,1,0:T(2,128)} %var_hbm.1) | copy-start | bytes 49156
  2.8 9.3 %collective-permute-start = (f32[2,64,512]{2,1,0:T(8,128)S(1)}, f32[2,64,512]{2,1,0:T(8,128)S(1)}, u32[]{:S(2)}, u32[]{:S(2)}) collective-permute-start(f32[2,64,512]{2,1,0:T(8,128)S(1)} %shard_map.55.refs_5_), channel_id=1, source_target_pairs={{0,1},{1,0},{2,3},{3,2},{4,5},{5,4},{6,7},{7,6},{8,9},{9,8},{10,11... | collective-permute-start | bytes 786440 | tf_op jit(solution)/shard_map/ppermute | solution.py:552
  5.8 11.9 %collective-permute-start.2 = (f32[2,64,512]{2,1,0:T(8,128)S(1)}, f32[2,64,512]{2,1,0:T(8,128)S(1)}, u32[]{:S(2)}, u32[]{:S(2)}) collective-permute-start(f32[2,64,512]{2,1,0:T(8,128)S(1)} %shard_map.55.refs_5_), channel_id=1, source_target_pairs={{0,30},{1,31},{2,4},{3,5},{4,2},{5,3},{6,8},{7,9},{8,6},{9,7},{10,... | collective-permute-start | bytes 786440 | tf_op jit(solution)/shard_map/ppermute | solution.py:552
  9.5 8.3 %collective-permute-start.1 = (f32[2,64,512]{2,1,0:T(8,128)S(1)}, f32[2,64,512]{2,1,0:T(8,128)S(1)}, u32[]{:S(2)}, u32[]{:S(2)}) collective-permute-start(f32[2,64,512]{2,1,0:T(8,128)S(1)} %shard_map.55.refs_5_), channel_id=1, source_target_pairs={{0,2},{1,3},{2,0},{3,1},{4,6},{5,7},{6,4},{7,5},{8,10},{9,11},{10,... | collective-permute-start | bytes 786440 | tf_op jit(solution)/shard_map/ppermute | solution.py:552
  12.1 8.6 %collective-permute-start.4 = (f32[2,64,512]{2,1,0:T(8,128)S(1)}, f32[2,64,512]{2,1,0:T(8,128)S(1)}, u32[]{:S(2)}, u32[]{:S(2)}) collective-permute-start(f32[2,64,512]{2,1,0:T(8,128)S(1)} %collective-permute-done.refs_0_.refs_8_), channel_id=1, source_target_pairs={{0,30},{1,31},{2,4},{3,5},{4,2},{5,3},{6,8},{7,9},{8,6},{9,7},{10,... | collective-permute-start | bytes 786440 | tf_op jit(solution)/shard_map/ppermute | solution.py:552
  15.5 5.3 %collective-permute-start.3 = (f32[2,64,512]{2,1,0:T(8,128)S(1)}, f32[2,64,512]{2,1,0:T(8,128)S(1)}, u32[]{:S(2)}, u32[]{:S(2)}) collective-permute-start(f32[2,64,512]{2,1,0:T(8,128)S(1)} %collective-permute-done.refs_0_.refs_8_), channel_id=1, source_target_pairs={{0,2},{1,3},{2,0},{3,1},{4,6},{5,7},{6,4},{7,5},{8,10},{9,11},{10,... | collective-permute-start | bytes 786440 | tf_op jit(solution)/shard_map/ppermute | solution.py:552
  16.2 4.6 %copy-start.6 = (s32[32,5]{0,1:T(8,128)S(1)}, s32[32,5]{0,1:T(8,128)}, u32[]{:S(2)}) copy-start(s32[32,5]{0,1:T(8,128)} %param.6) | copy-start | bytes 1924
  16.2 14.4 %collective-permute-start.5 = (f32[512,256]{1,0:T(8,128)S(1)}, f32[512,256]{1,0:T(8,128)S(1)}, u32[]{:S(2)}, u32[]{:S(2)}) collective-permute-start(f32[512,256]{1,0:T(8,128)S(1)} %get-tuple-element.47), channel_id=1, source_target_pairs={{0,1},{1,0},{2,3},{3,2},{4,5},{5,4},{6,7},{7,6},{8,9},{9,8},{10,11... | collective-permute-start | bytes 1572872 | tf_op jit(solution)/shard_map/ppermute | solution.py:552
  20.8 9.8 %copy-start.3 = (s32[32,2,64]{2,1,0:T(2,128)S(1)}, s32[32,2,64]{2,1,0:T(2,128)}, u32[]{:S(2)}) copy-start(s32[32,2,64]{2,1,0:T(2,128)} %cells_ref.3) | copy-start | bytes 49156
  35.2 8.1 %collective-permute-start.8 = (f32[64,1024]{1,0:T(8,128)S(1)}, f32[64,1024]{1,0:T(8,128)S(1)}, u32[]{:S(2)}, u32[]{:S(2)}) collective-permute-start(f32[64,1024]{1,0:T(8,128)S(1)} %get-tuple-element.48.refs_7_.refs_5_), channel_id=1, source_target_pairs={{0,1},{1,0},{2,3},{3,2},{4,5},{5,4},{6,7},{7,6},{8,9},{9,8},{10,11... | collective-permute-start | bytes 786440 | tf_op jit(solution)/shard_map/ppermute | solution.py:552
  36.8 8.6 %collective-permute-start.7 = (f32[64,1024]{1,0:T(8,128)S(1)}, f32[64,1024]{1,0:T(8,128)S(1)}, u32[]{:S(2)}, u32[]{:S(2)}) collective-permute-start(f32[64,1024]{1,0:T(8,128)S(1)} %get-tuple-element.48.refs_7_.refs_5_), channel_id=1, source_target_pairs={{0,30},{1,31},{2,4},{3,5},{4,2},{5,3},{6,8},{7,9},{8,6},{9,7},{10,... | collective-permute-start | bytes 786440 | tf_op jit(solution)/shard_map/ppermute | solution.py:552
  37.8 7.6 %collective-permute-start.6 = (f32[64,1024]{1,0:T(8,128)S(1)}, f32[64,1024]{1,0:T(8,128)S(1)}, u32[]{:S(2)}, u32[]{:S(2)}) collective-permute-start(f32[64,1024]{1,0:T(8,128)S(1)} %get-tuple-element.48.refs_7_.refs_5_), channel_id=1, source_target_pairs={{0,2},{1,3},{2,0},{3,1},{4,6},{5,7},{6,4},{7,5},{8,10},{9,11},{10,... | collective-permute-start | bytes 786440 | tf_op jit(solution)/shard_map/ppermute | solution.py:552
  37.8 10.3 %collective-permute-start.10 = (f32[64,1024]{1,0:T(8,128)S(1)}, f32[64,1024]{1,0:T(8,128)S(1)}, u32[]{:S(2)}, u32[]{:S(2)}) collective-permute-start(f32[64,1024]{1,0:T(8,128)S(1)} %get-tuple-element.48.refs_7_.refs_5_), channel_id=1, source_target_pairs={{0,31},{1,30},{2,5},{3,4},{4,3},{5,2},{6,9},{7,8},{8,7},{9,6},{10,... | collective-permute-start | bytes 786440 | tf_op jit(solution)/shard_map/ppermute | solution.py:552
  43.3 4.8 %collective-permute-start.9 = (f32[64,1024]{1,0:T(8,128)S(1)}, f32[64,1024]{1,0:T(8,128)S(1)}, u32[]{:S(2)}, u32[]{:S(2)}) collective-permute-start(f32[64,1024]{1,0:T(8,128)S(1)} %collective-permute-done.8.refs_10_.refs_8_), channel_id=1, source_target_pairs={{0,2},{1,3},{2,0},{3,1},{4,6},{5,7},{6,4},{7,5},{8,10},{9,11},{10,... | collective-permute-start | bytes 786440 | tf_op jit(solution)/shard_map/ppermute | solution.py:552
  57.8 13.3 %collective-permute-start.11 = (f32[512,256]{1,0:T(8,128)S(1)}, f32[512,256]{1,0:T(8,128)S(1)}, u32[]{:S(2)}, u32[]{:S(2)}) collective-permute-start(f32[512,256]{1,0:T(8,128)S(1)} %get-tuple-element.68), channel_id=1, source_target_pairs={{0,1},{1,0},{2,3},{3,2},{4,5},{5,4},{6,7},{7,6},{8,9},{9,8},{10,11... | collective-permute-start | bytes 1572872 | tf_op jit(solution)/shard_map/ppermute | solution.py:552
where the time goes:
time: 73.5 us; the launch traced here: 72.3 us
  Pallas kernels  28.4 us (39%)
  waiting for transfers between devices  22.4 us (30%)
  starting transfers between devices  19.2 us (26%)
  local copies, waits for them, and re-layouts  2 us (3%)
    pallas_call x9, Pallas kernels, call(): pl.pallas_call(kernel, out_shape=shapes, in_specs=ins, out_specs=[space f...  27.3 us
    ppermute x12, waiting for transfers between devices, permute(): return lax.ppermute(x, BOTH, table)  22.4 us
    ppermute x12, starting transfers between devices, permute(): return lax.ppermute(x, BOTH, table)  19.2 us
    unnamed x14, local copies, waits for them, and re-layouts  2 us
  transfers between devices with their start and end apart: 12, of which 7 were waited for; matrix products, arithmetic and copies ran while one was open for 0% of the time, Pallas kernels for 17%

commit v1 on v0

--- a/solution.py
+++ b/solution.py
@@ -94,26 +94,28 @@
     return jnp.transpose(hot)[0:per_patch, :]
 
 
-def pick_kernel(region_ref, cells_ref, state_ref, rows_ref, scratch, field_ref):
-    patches, cells = state_ref.shape[1:]
-    for p in range(patches):
-        field_ref[p] = state_ref[:, p, :]
-        hot = selector(cells_ref[pl.ds(region_ref[0] * patches + p, 1), 0, :], cells, scratch)
-        rows_ref[p] = select(hot, split_all(field_ref[p]), NT)
-
-
-def sort_kernel(column_ref, values_hbm, var_hbm, state_ref, *refs):
-    keep_ref, send_ref, values_ref, var_ref, sems = refs[-5:]
+def sort_kernel(column_ref, state_ref, keep_ref, send_ref):
+    column = column_ref[0]
+    first, second = state_ref[:, 0, :], state_ref[:, 1, :]
+    keep_ref[...] = jnp.where(column == 0, first, second)
+    send_ref[...] = jnp.where(column == 0, second, first)
+
+
+def pick_kernel(region_ref, column_ref, cells_ref, keep_ref, send_ref, rows_ref, scratch):
+    column = column_ref[0]
+    for patch, field_ref in ((column, keep_ref), (1 - column, send_ref)):
+        picks = cells_ref[pl.ds(region_ref[0] * 2 + patch, 1), 0, :]
+        hot = selector(picks, field_ref.shape[1], scratch)
+        rows_ref[pl.ds(patch, 1)] = select(hot, split_all(field_ref[...]), NT)[None]
+
+
+def gate_kernel(values_hbm, var_hbm, send_ref, after_ref, out_ref, values_ref, var_ref, sems):
     copies = [
         pltpu.make_async_copy(values_hbm, values_ref, sems.at[0]),
         pltpu.make_async_copy(var_hbm, var_ref, sems.at[1]),
     ]
     for copy in copies:
         copy.start()
-    column = column_ref[0]
-    first, second = state_ref[:, 0, :], state_ref[:, 1, :]
-    keep_ref[...] = jnp.where(column == 0, first, second)
-    send_ref[...] = jnp.where(column == 0, second, first)
     for copy in copies:
         copy.wait()
 
@@ -230,18 +232,23 @@
     corner = dot3([part[head:n] for part in parts], [part[:, head:n] for part in parts])
     store((wa.at[0], wa.at[1]), 0, *corner_of(weight, keep, left, corner))
 
+    def corners_of(source):
+        ends = [
+            jnp.concatenate([source[i, head:n, 0:n], source[i, head:n, n : 2 * n]], axis=0) for i in (0, 1)
+        ]
+        return dot3(ends, (source[0, :, head:n], source[1, :, head:n]))
+
     def advance(source, target, rho2):
         weight = 2.0 / (2.0 - rho2)
         keep = 0.5 * rho2 * weight
         parts = (source[0, :, 0:n], source[1, :, 0:n])
-        ends = [jnp.concatenate([source[i, :, head:n], source[i, :, n + head : 2 * n]], axis=1) for i in (0, 1)]
         left = dot3(parts, (source[0, :, 0:head], source[1, :, 0:head]))
-        corners = dot3([part[head:n] for part in parts], ends)
+        corners = corners_of(source)
         both = (target.at[0], target.at[1])
-        store(both, 0, *corner_of(weight, keep, left, corners[:, 0:tail]))
+        store(both, 0, *corner_of(weight, keep, left, corners[0:tail]))
         left = dot3(parts, (source[0, :, n : n + head], source[1, :, n : n + head]))
         left = weight * (x_ref[:, 0:head] + left)
-        corner = weight * (x_ref[head:n, head:n] + corners[:, tail : 2 * tail])
+        corner = weight * (x_ref[head:n, head:n] + corners[tail : 2 * tail])
         x_ref[:, 0:head] = left
         x_ref[head:n, head:n] = corner
         store(both, n, left, corner)
@@ -252,11 +259,11 @@
     def sides(source, span):
         return [source[i, span[0] : span[1], 0:n] for i in (0, 1)]
 
-    def put(targets, start, span, block):
+    def put(targets, start, span, block, mirror):
         for target, part in zip(targets, split(block)):
             target[span[0] : span[1], start : start + head] = part
         low = max(span[0], head)
-        if low < span[1]:
+        if mirror and low < span[1]:
             for target, part in zip(targets, split(jnp.transpose(block[low - span[0] :]))):
                 target[0:head, start + low : start + span[1]] = part
 
@@ -264,10 +271,10 @@
         for target, part in zip(targets, split(block)):
             target[head:n, start + head : start + n] = part
 
-    def put_x(targets, start, weight, span, product):
+    def put_x(targets, start, weight, span, product, mirror=False):
         x = weight * (x_ref[span[0] : span[1], 0:head] + product)
         x_ref[span[0] : span[1], 0:head] = x
-        put(targets, start, span, x)
+        put(targets, start, span, x, mirror)
 
     def put_x_corner(targets, start, weight, product):
         x = weight * (x_ref[head:n, head:n] + product)
@@ -287,16 +294,15 @@
                 put_x((source.at[0], source.at[1]), n, waiting[0], span, waiting[1][k])
         if waiting is not None:
             put_x_corner((source.at[0], source.at[1]), n, waiting[0], waiting[2])
-        ends = [jnp.concatenate([source[i, :, head:n], source[i, :, n + head : 2 * n]], axis=1) for i in (0, 1)]
-        corners = dot3(sides(source, (head, n)), ends)
+        corners = corners_of(source)
         first = (source[0, :, n : n + head], source[1, :, n : n + head])
         both = (target.at[0], target.at[1])
         x = []
         for k, span in enumerate(chunks):
             x.append(dot3(sides(source, span), first))
-            put(both, 0, span, weight * r[k] - keep * eye_ref[span[0] : span[1], 0:head])
-        put_corner(both, 0, weight * corners[:, 0:tail] - keep * eye_ref[head:n, head:n])
-        waiting = (weight, x, corners[:, tail : 2 * tail])
+            put(both, 0, span, weight * r[k] - keep * eye_ref[span[0] : span[1], 0:head], True)
+        put_corner(both, 0, weight * corners[0:tail] - keep * eye_ref[head:n, head:n])
+        waiting = (weight, x, corners[tail : 2 * tail])
         rho2 = keep * keep
         source, target = target, source
     for k, span in enumerate(chunks):
@@ -310,11 +316,11 @@
     weight = 2.0 / (2.0 - rho2)
     first = (source[0, :, n : n + head], source[1, :, n : n + head])
     done = (xh_ref, xl_ref)
-    ends = [source[i, :, n + head : 2 * n] for i in (0, 1)]
-    put_x_corner(done, 0, weight, dot3(sides(source, (head, n)), ends))
+    ends = [source[i, head:n, n : 2 * n] for i in (0, 1)]
+    put_x_corner(done, 0, weight, dot3(ends, (source[0, :, head:n], source[1, :, head:n])))
     x = [dot3(sides(source, span), first) for span in chunks]
     for k, span in enumerate(chunks):
-        put_x(done, 0, weight, span, x[k])
+        put_x(done, 0, weight, span, x[k], True)
 
 
 def centred(fields):
@@ -335,7 +341,7 @@
     work(*waiting)
 
 
-def solve(n_ref, s, g_ref, x, anomaly, z_ref, cross_ref, parts_ref, crossed_already=False):
+def solve(n_ref, s, g_ref, x, anomaly, z_ref, cross_ref, parts_ref, crossed_already=False, between=()):
     n = z_ref.shape[0]
 
     def keep(slot, span, value):
@@ -366,9 +372,15 @@
         keep(0, slice(0, n), cross_ref[...])
     else:
         in_chunks(n, lambda span: dot3(some(s, span), [part[...] for part in anomaly]), crossed)
-    in_chunks(n, lambda span: dot3(some(x, span), kept(0)), solved)
-    in_chunks(n, lambda span: dot3(split(g_ref[span]), kept(1)), left)
-    in_chunks(n, lambda span: dot3(some(x, span), kept(0)), refined)
+    stages = [
+        (lambda span: dot3(some(x, span), kept(0)), solved),
+        (lambda span: dot3(split(g_ref[span]), kept(1)), left),
+        (lambda span: dot3(some(x, span), kept(0)), refined),
+    ]
+    for i, (product, work) in enumerate(stages):
+        for extra in between[i : i + 1]:
+            extra()
+        in_chunks(n, product, work)
 
     def refine(_, carry):
         z = z_ref[...]
@@ -387,14 +399,25 @@
     for i, part in enumerate(anomaly):
         anomaly_ref[i] = part
     anomaly = (anomaly_ref.at[0], anomaly_ref.at[1])
-    solve(n_ref, (sh_ref, sl_ref), g_ref, (xh_ref, xl_ref), anomaly, z_ref, cross_ref, parts_ref)
-    s = (sh_ref[...], sl_ref[...])
     picks = cells_ref[pl.ds(own_of(region_ref, column_ref), 1), batch, :]
     hot = selector(picks, mean.shape[1], scratch)
+    base = jnp.sum(hot * mean, axis=1, keepdims=True)
+    members = anomaly_ref.shape[1]
+    count = 3
+    size = -(-members // (count * 128)) * 128
+
+    def pick(start, stop):
+        picked = select(hot, [part[start:stop] for part in anomaly], NT)
+        rows_ref[:, start:stop] = base + picked
+
+    between = [
+        functools.partial(pick, i * size, min((i + 1) * size, members)) for i in range(count)
+    ]
+    x = (xh_ref, xl_ref)
+    solve(n_ref, (sh_ref, sl_ref), g_ref, x, anomaly, z_ref, cross_ref, parts_ref, False, between)
     zt = split(select(hot, split(z_ref[...]), NT))
-    base = jnp.sum(hot * mean, axis=1, keepdims=True) + dot3(zt, split(d_ref[...]))[:, 0:1]
-    picked = select(hot, [part[...] for part in anomaly], NT)
-    rows_ref[...] = base + picked - 0.5 * dot3(zt, s)
+    shift = dot3(zt, split(d_ref[...]))[:, 0:1]
+    rows_ref[...] = rows_ref[...] + shift - 0.5 * dot3(zt, (sh_ref[...], sl_ref[...]))
 
 
 def updated(field, start, s, shift, z):
@@ -585,22 +608,24 @@
         return permute(x, lambda c, q, m: (c + 2 * q - 1, 1 - q, m), regions)
 
     anywhere = pl.BlockSpec(memory_space=pl.ANY)
+    shape = ((half, cells), F32, VMEM)
+    keep, send = call(sort_kernel, [shape] * 2, [SMEM, VMEM], [place[1], state])
     (rows,) = call(
         pick_kernel,
         [((2, obs_cell.shape[2], half), F32, VMEM)],
-        [SMEM, VMEM, VMEM],
-        [place[0], obs_cell, state],
-        [pltpu.VMEM((8, 128), jnp.int32), pltpu.VMEM((2, half, cells), F32)],
+        [SMEM, SMEM, VMEM, VMEM, VMEM],
+        [*place, obs_cell, keep, send],
+        [pltpu.VMEM((8, 128), jnp.int32)],
     )
     other = across(rows)
     sources = [rows, beside(rows), outside(rows), other, beside(other), outside(other)]
-    shape = ((half, cells), F32, VMEM)
-    keep, send, values, var = call(
-        sort_kernel,
-        [shape, shape, (obs_values.shape, F32, VMEM), (obs_var.shape, F32, VMEM)],
-        [SMEM, anywhere, anywhere, VMEM, anywhere],
-        [place[1], obs_values, obs_var, state, other],
+    send, values, var = call(
+        gate_kernel,
+        [((half, cells), F32, anywhere), (obs_values.shape, F32, VMEM), (obs_var.shape, F32, VMEM)],
+        [anywhere] * 4,
+        [obs_values, obs_var, send, other],
         [pltpu.SemaphoreType.DMA((2,))],
+        aliases={2: 0},
     )
     pieces = [[(i, (p,), 0), (3 + i, (p,), 1)] for p in range(2) for i in range(3)]
     states = [keep, across(send)]

time: 73.5 us -> 72.6 us (0.988)
    unnamed x14 -> x10, local copies, waits for them, and re-layouts: 2 us -> 1.41 us
    pallas_call x9 -> x10, Pallas kernels: 27.3 us -> 27.1 us  [call(): pl.pallas_call(kernel, out_shape=shapes, in_specs=ins, out_specs=[space f...]
where the time goes in v1:
time: 72.6 us; the launch traced here: 71.4 us
  Pallas kernels  28.2 us (39%)
  waiting for transfers between devices  22.2 us (31%)
  starting transfers between devices  19.2 us (26%)
  local copies, waits for them, and re-layouts  1.41 us (2%)
    pallas_call x10, Pallas kernels, call(): pl.pallas_call(kernel, out_shape=shapes, in_specs=ins, out_specs=[space f...  27.1 us
    ppermute x12, waiting for transfers between devices, permute(): return lax.ppermute(x, BOTH, table)  22.2 us
    ppermute x12, starting transfers between devices, permute(): return lax.ppermute(x, BOTH, table)  19.2 us
  transfers between devices with their start and end apart: 12, of which 7 were waited for; matrix products, arithmetic and copies ran while one was open for 0% of the time, Pallas kernels for 17%

profile of v1, /device:TPU:0, one launch (start us, length us, event | category | flops | bytes accessed | tf_op | source)
XLA Modules:
  0.0 71.4 jit_solution(3411569829654032147)
XLA Ops:
  0.0 1.2 %copy-done = f32[512,2,256]{2,1,0:T(2,128)S(1)} copy-done((f32[512,2,256]{2,1,0:T(2,128)S(1)}, f32[512,2,256]{2,1,0:T(2,128)}, u32[]{:S(2)}) %copy-start) | copy-done | bytes 1048600
  1.2 0.6 shard_map.55
  1.8 0.2 copy-done.1
  2.0 0.6 shard_map.56.refs_5_
  2.6 3.0 %collective-permute-start = (f32[2,64,512]{2,1,0:T(8,128)S(1)}, f32[2,64,512]{2,1,0:T(8,128)S(1)}, u32[]{:S(2)}, u32[]{:S(2)}) collective-permute-start(f32[2,64,512]{2,1,0:T(8,128)S(1)} %shard_map.56.refs_5_), channel_id=1, source_target_pairs={{0,1},{1,0},{2,3},{3,2},{4,5},{5,4},{6,7},{7,6},{8,9},{9,8},{10,11... | collective-permute-start | bytes 786440 | tf_op jit(solution)/shard_map/ppermute | solution.py:575
  5.6 3.7 %collective-permute-start.2 = (f32[2,64,512]{2,1,0:T(8,128)S(1)}, f32[2,64,512]{2,1,0:T(8,128)S(1)}, u32[]{:S(2)}, u32[]{:S(2)}) collective-permute-start(f32[2,64,512]{2,1,0:T(8,128)S(1)} %shard_map.56.refs_5_), channel_id=1, source_target_pairs={{0,30},{1,31},{2,4},{3,5},{4,2},{5,3},{6,8},{7,9},{8,6},{9,7},{10,... | collective-permute-start | bytes 786440 | tf_op jit(solution)/shard_map/ppermute | solution.py:575
  9.3 2.6 %collective-permute-done.after_ref.refs_8_ = f32[2,64,512]{2,1,0:T(8,128)S(1)} collective-permute-done((f32[2,64,512]{2,1,0:T(8,128)S(1)}, f32[2,64,512]{2,1,0:T(8,128)S(1)}, u32[]{:S(2)}, u32[]{:S(2)}) %collective-permute-start) | collective-permute-done | bytes 262176 | tf_op jit(solution)/shard_map/ppermute | solution.py:575
  11.9 3.3 %collective-permute-start.4 = (f32[2,64,512]{2,1,0:T(8,128)S(1)}, f32[2,64,512]{2,1,0:T(8,128)S(1)}, u32[]{:S(2)}, u32[]{:S(2)}) collective-permute-start(f32[2,64,512]{2,1,0:T(8,128)S(1)} %collective-permute-done.after_ref.refs_8_), channel_id=1, source_target_pairs={{0,30},{1,31},{2,4},{3,5},{4,2},{5,3},{6,8},{7,9},{8,6},{9,7},{10,... | collective-permute-start | bytes 786440 | tf_op jit(solution)/shard_map/ppermute | solution.py:575
  15.2 0.0 collective-permute-start.3
  15.3 0.1 shard_map.57
  15.4 0.0 copy-start.4
  15.4 1.6 %collective-permute-start.5 = (f32[512,256]{1,0:T(8,128)S(1)}, f32[512,256]{1,0:T(8,128)S(1)}, u32[]{:S(2)}, u32[]{:S(2)}) collective-permute-start(f32[512,256]{1,0:T(8,128)S(1)} %get-tuple-element.49), channel_id=1, source_target_pairs={{0,1},{1,0},{2,3},{3,2},{4,5},{5,4},{6,7},{7,6},{8,9},{9,8},{10,11... | collective-permute-start | bytes 1572872 | tf_op jit(solution)/shard_map/ppermute | solution.py:575
  17.0 0.0 collective-permute-done.1.refs_6_
  17.0 3.6 %collective-permute-done.4.refs_10_ = f32[2,64,512]{2,1,0:T(8,128)S(1)} collective-permute-done((f32[2,64,512]{2,1,0:T(8,128)S(1)}, f32[2,64,512]{2,1,0:T(8,128)S(1)}, u32[]{:S(2)}, u32[]{:S(2)}) %collective-permute-start.4) | collective-permute-done | bytes 262176 | tf_op jit(solution)/shard_map/ppermute | solution.py:575
  20.5 0.0 collective-permute-done.3.refs_9_
  20.5 7.9 %shard_map.58 = (bf16[384,1024]{1,0:T(8,128)(2,1)S(1)}, bf16[384,1024]{1,0:T(8,128)(2,1)S(1)}, f32[384,128]{1,0:T(8,128)S(1)}, f32[384,384]{1,0:T(8,128)S(1)}, b...) custom-call(s32[1]{0:T(128)} %bitcast.1.region_ref.refs_0_, s32[1]{0:T(128)} %bitcast.column_ref.refs_1_, ...), custom_call_target="tpu_custom_call" | custom-call | flops 4303355904 | bytes 4555404 | tf_op jit(solution)/shard_map/pallas_call | solution.py:31
  28.4 1.3 %collective-permute-done.5.refs_3_.refs_1_ = f32[512,256]{1,0:T(8,128)S(1)} collective-permute-done((f32[512,256]{1,0:T(8,128)S(1)}, f32[512,256]{1,0:T(8,128)S(1)}, u32[]{:S(2)}, u32[]{:S(2)}) %collective-permute-start.5) | collective-permute-done | bytes 524320 | tf_op jit(solution)/shard_map/ppermute | solution.py:575
  29.8 4.2 %shard_map.59 = (f32[384,256]{1,0:T(8,128)S(1)}, f32[64,1024]{1,0:T(8,128)S(1)}) custom-call(s32[1]{0:T(128)} %bitcast.1.region_ref.refs_0_, s32[1]{0:T(128)} %bitcast.column_ref.refs_1_, s32[1]{0:T(128)} %get-tuple-element.42.n_ref, s32[32,2,64]{2,1,0:T(2,128)S(1)} %copy-done.1, bf16[384,1024]{1,0:T(8,128)(2,1)S(1)} %get-tuple-element.43.sh_ref, ...), custom_call_target="tpu_custom_call" | custom-call | flops 805306368 | bytes 4669452 | tf_op jit(solution)/shard_map/pallas_call | solution.py:31
  34.0 1.6 %collective-permute-start.8 = (f32[64,1024]{1,0:T(8,128)S(1)}, f32[64,1024]{1,0:T(8,128)S(1)}, u32[]{:S(2)}, u32[]{:S(2)}) collective-permute-start(f32[64,1024]{1,0:T(8,128)S(1)} %get-tuple-element.50.refs_7_.refs_5_), channel_id=1, source_target_pairs={{0,1},{1,0},{2,3},{3,2},{4,5},{5,4},{6,7},{7,6},{8,9},{9,8},{10,11... | collective-permute-start | bytes 786440 | tf_op jit(solution)/shard_map/ppermute | solution.py:575
  35.5 1.7 %collective-permute-start.7 = (f32[64,1024]{1,0:T(8,128)S(1)}, f32[64,1024]{1,0:T(8,128)S(1)}, u32[]{:S(2)}, u32[]{:S(2)}) collective-permute-start(f32[64,1024]{1,0:T(8,128)S(1)} %get-tuple-element.50.refs_7_.refs_5_), channel_id=1, source_target_pairs={{0,30},{1,31},{2,4},{3,5},{4,2},{5,3},{6,8},{7,9},{8,6},{9,7},{10,... | collective-permute-start | bytes 786440 | tf_op jit(solution)/shard_map/ppermute | solution.py:575
  37.3 2.7 %collective-permute-start.10 = (f32[64,1024]{1,0:T(8,128)S(1)}, f32[64,1024]{1,0:T(8,128)S(1)}, u32[]{:S(2)}, u32[]{:S(2)}) collective-permute-start(f32[64,1024]{1,0:T(8,128)S(1)} %get-tuple-element.50.refs_7_.refs_5_), channel_id=1, source_target_pairs={{0,31},{1,30},{2,5},{3,4},{4,3},{5,2},{6,9},{7,8},{8,7},{9,6},{10,... | collective-permute-start | bytes 786440 | tf_op jit(solution)/shard_map/ppermute | solution.py:575
  39.9 2.0 %collective-permute-done.8.refs_10_.refs_8_ = f32[64,1024]{1,0:T(8,128)S(1)} collective-permute-done((f32[64,1024]{1,0:T(8,128)S(1)}, f32[64,1024]{1,0:T(8,128)S(1)}, u32[]{:S(2)}, u32[]{:S(2)}) %collective-permute-start.8) | collective-permute-done | bytes 262176 | tf_op jit(solution)/shard_map/ppermute | solution.py:575
  42.0 1.2 %shard_map.60 = (f32[512,256]{1,0:T(8,128)S(1)}, f32[512,256]{1,0:T(8,128)S(1)}, bf16[1024,256]{1,0:T(8,128)(2,1)S(1)}, bf16[1024,256]{1,0:T(8,128)(2,1)S(1)}) custom-call(bf16[384,1024]{1,0:T(8,128)(2,1)S(1)} %get-tuple-element.43.sh_ref, bf16[384,1024]{1,0:T(8,128)(2,1)S(1)} %get-tuple-element.44.sl_ref, f32[384,128]{1,0:T(8,128)S(1)} %get-tuple-element.45.d_ref, ...), custom_call_target="tpu_custom_call" | custom-call | flops 603979776 | bytes 5308416 | tf_op jit(solution)/shard_map/pallas_call | solution.py:31
  43.2 0.9 %collective-permute-done.7.refs_9_.refs_7_ = f32[64,1024]{1,0:T(8,128)S(1)} collective-permute-done((f32[64,1024]{1,0:T(8,128)S(1)}, f32[64,1024]{1,0:T(8,128)S(1)}, u32[]{:S(2)}, u32[]{:S(2)}) %collective-permute-start.7) | collective-permute-done | bytes 262176 | tf_op jit(solution)/shard_map/ppermute | solution.py:575
  44.1 2.0 %shard_map.61 = (bf16[384,1024]{1,0:T(8,128)(2,1)S(1)}, bf16[384,1024]{1,0:T(8,128)(2,1)S(1)}, f32[384,128]{1,0:T(8,128)S(1)}, f32[384,384]{1,0:T(8,128)S(1)}, f32[384,256]{1,0:T(8,128)S(1)}) custom-call(s32[1]{0:T(128)} %bitcast.1.region_ref.refs_0_, s32[1]{0:T(128)} %bitcast.column_ref.refs_1_, s32[5,32]{1,0:T(8,128)S(1)} %bitcast.4, ...), custom_call_target="tpu_custom_call" | custom-call | flops 603979776 | bytes 4883080 | tf_op jit(solution)/shard_map/pallas_call | solution.py:31
  46.2 0.7 %collective-permute-done.10.refs_10_ = f32[64,1024]{1,0:T(8,128)S(1)} collective-permute-done((f32[64,1024]{1,0:T(8,128)S(1)}, f32[64,1024]{1,0:T(8,128)S(1)}, u32[]{:S(2)}, u32[]{:S(2)}) %collective-permute-start.10) | collective-permute-done | bytes 262176 | tf_op jit(solution)/shard_map/ppermute | solution.py:575
  46.9 7.2 %shard_map.62 = (bf16[384,1024]{1,0:T(8,128)(2,1)S(1)}, bf16[384,1024]{1,0:T(8,128)(2,1)S(1)}, f32[384,128]{1,0:T(8,128)S(1)}, f32[384,384]{1,0:T(8,128)S(1)}, b...) custom-call(s32[1]{0:T(128)} %bitcast.1.region_ref.refs_0_, ...), custom_call_target="tpu_custom_call", output_to_operand_aliasing={{0}: (13, {}), {1}: (14, {}), {2}: (15, {}), {3}: (16, {}),... | custom-call | flops 4303355904 | bytes 8749708 | tf_op jit(solution)/shard_map/pallas_call | solution.py:31
  54.1 2.7 %shard_map.63 = (f32[384,256]{1,0:T(8,128)S(1)}, f32[512,256]{1,0:T(8,128)S(1)}) custom-call(s32[1]{0:T(128)} %get-tuple-element.62.n_ref, bf16[384,1024]{1,0:T(8,128)(2,1)S(1)} %get-tuple-element.59.sh_ref, bf16[384,1024]{1,0:T(8,128)(2,1)S(1)} %get-tuple-element.60.sl_ref, f32[384,128]{1,0:T(8,128)S(1)} %get-tuple-element.61.d_ref, ...), custom_call_target="tpu_custom_call" | custom-call | flops 1207959552 | bytes 4784132 | tf_op jit(solution)/shard_map/pallas_call | solution.py:31
  56.8 1.6 %collective-permute-start.11 = (f32[512,256]{1,0:T(8,128)S(1)}, f32[512,256]{1,0:T(8,128)S(1)}, u32[]{:S(2)}, u32[]{:S(2)}) collective-permute-start(f32[512,256]{1,0:T(8,128)S(1)} %get-tuple-element.70), channel_id=1, source_target_pairs={{0,1},{1,0},{2,3},{3,2},{4,5},{5,4},{6,7},{7,6},{8,9},{9,8},{10,11... | collective-permute-start | bytes 1572872 | tf_op jit(solution)/shard_map/ppermute | solution.py:575
  58.4 0.6 shard_map.64.mine_ref
  59.0 11.1 %collective-permute-done.11.theirs_ref = f32[512,256]{1,0:T(8,128)S(1)} collective-permute-done((f32[512,256]{1,0:T(8,128)S(1)}, f32[512,256]{1,0:T(8,128)S(1)}, u32[]{:S(2)}, u32[]{:S(2)}) %collective-permute-start.11) | collective-permute-done | bytes 524320 | tf_op jit(solution)/shard_map/ppermute | solution.py:575
  70.1 1.1 %shard_map.65 = f32[512,2,256]{2,1,0:T(2,128)} custom-call(s32[1]{0:T(128)} %bitcast.column_ref.refs_1_, f32[512,256]{1,0:T(8,128)S(1)} %shard_map.64.mine_ref, f32[512,256]{1,0:T(8,128)S(1)} %collective-permute-done.11.theirs_ref), custom_call_target="tpu_custom_call" | custom-call | tf_op jit(solution)/shard_map/pallas_call | solution.py:654
  (13 shorter events, 0.0 us)
Async XLA Ops:
  0.0 1.2 %copy-start = (f32[512,2,256]{2,1,0:T(2,128)S(1)}, f32[512,2,256]{2,1,0:T(2,128)}, u32[]{:S(2)}) copy-start(f32[512,2,256]{2,1,0:T(2,128)} %state_ref.1) | copy-start | bytes 3145732
  1.2 0.8 %copy-start.1 = (s32[32,2,64]{2,1,0:T(2,128)S(1)}, s32[32,2,64]{2,1,0:T(2,128)}, u32[]{:S(2)}) copy-start(s32[32,2,64]{2,1,0:T(2,128)} %cells_ref.3) | copy-start | bytes 49156
  2.0 13.3 %copy-start.2 = (f32[32,2,64]{2,1,0:T(2,128)S(1)}, f32[32,2,64]{2,1,0:T(2,128)}, u32[]{:S(2)}) copy-start(f32[32,2,64]{2,1,0:T(2,128)} %values_hbm.1) | copy-start | bytes 49156
  2.0 13.3 %copy-start.3 = (f32[32,2,64]{2,1,0:T(2,128)S(1)}, f32[32,2,64]{2,1,0:T(2,128)}, u32[]{:S(2)}) copy-start(f32[32,2,64]{2,1,0:T(2,128)} %var_hbm.1) | copy-start | bytes 49156
  2.6 9.3 %collective-permute-start = (f32[2,64,512]{2,1,0:T(8,128)S(1)}, f32[2,64,512]{2,1,0:T(8,128)S(1)}, u32[]{:S(2)}, u32[]{:S(2)}) collective-permute-start(f32[2,64,512]{2,1,0:T(8,128)S(1)} %shard_map.56.refs_5_), channel_id=1, source_target_pairs={{0,1},{1,0},{2,3},{3,2},{4,5},{5,4},{6,7},{7,6},{8,9},{9,8},{10,11... | collective-permute-start | bytes 786440 | tf_op jit(solution)/shard_map/ppermute | solution.py:575
  5.6 11.3 %collective-permute-start.2 = (f32[2,64,512]{2,1,0:T(8,128)S(1)}, f32[2,64,512]{2,1,0:T(8,128)S(1)}, u32[]{:S(2)}, u32[]{:S(2)}) collective-permute-start(f32[2,64,512]{2,1,0:T(8,128)S(1)} %shard_map.56.refs_5_), channel_id=1, source_target_pairs={{0,30},{1,31},{2,4},{3,5},{4,2},{5,3},{6,8},{7,9},{8,6},{9,7},{10,... | collective-permute-start | bytes 786440 | tf_op jit(solution)/shard_map/ppermute | solution.py:575
  9.3 7.7 %collective-permute-start.1 = (f32[2,64,512]{2,1,0:T(8,128)S(1)}, f32[2,64,512]{2,1,0:T(8,128)S(1)}, u32[]{:S(2)}, u32[]{:S(2)}) collective-permute-start(f32[2,64,512]{2,1,0:T(8,128)S(1)} %shard_map.56.refs_5_), channel_id=1, source_target_pairs={{0,2},{1,3},{2,0},{3,1},{4,6},{5,7},{6,4},{7,5},{8,10},{9,11},{10,... | collective-permute-start | bytes 786440 | tf_op jit(solution)/shard_map/ppermute | solution.py:575
  11.9 8.6 %collective-permute-start.4 = (f32[2,64,512]{2,1,0:T(8,128)S(1)}, f32[2,64,512]{2,1,0:T(8,128)S(1)}, u32[]{:S(2)}, u32[]{:S(2)}) collective-permute-start(f32[2,64,512]{2,1,0:T(8,128)S(1)} %collective-permute-done.after_ref.refs_8_), channel_id=1, source_target_pairs={{0,30},{1,31},{2,4},{3,5},{4,2},{5,3},{6,8},{7,9},{8,6},{9,7},{10,... | collective-permute-start | bytes 786440 | tf_op jit(solution)/shard_map/ppermute | solution.py:575
  15.2 5.3 %collective-permute-start.3 = (f32[2,64,512]{2,1,0:T(8,128)S(1)}, f32[2,64,512]{2,1,0:T(8,128)S(1)}, u32[]{:S(2)}, u32[]{:S(2)}) collective-permute-start(f32[2,64,512]{2,1,0:T(8,128)S(1)} %collective-permute-done.after_ref.refs_8_), channel_id=1, source_target_pairs={{0,2},{1,3},{2,0},{3,1},{4,6},{5,7},{6,4},{7,5},{8,10},{9,11},{10,... | collective-permute-start | bytes 786440 | tf_op jit(solution)/shard_map/ppermute | solution.py:575
  15.4 5.2 %copy-start.4 = (s32[32,5]{0,1:T(8,128)S(1)}, s32[32,5]{0,1:T(8,128)}, u32[]{:S(2)}) copy-start(s32[32,5]{0,1:T(8,128)} %param.6) | copy-start | bytes 1924
  15.4 14.4 %collective-permute-start.5 = (f32[512,256]{1,0:T(8,128)S(1)}, f32[512,256]{1,0:T(8,128)S(1)}, u32[]{:S(2)}, u32[]{:S(2)}) collective-permute-start(f32[512,256]{1,0:T(8,128)S(1)} %get-tuple-element.49), channel_id=1, source_target_pairs={{0,1},{1,0},{2,3},{3,2},{4,5},{5,4},{6,7},{7,6},{8,9},{9,8},{10,11... | collective-permute-start | bytes 1572872 | tf_op jit(solution)/shard_map/ppermute | solution.py:575
  34.0 8.0 %collective-permute-start.8 = (f32[64,1024]{1,0:T(8,128)S(1)}, f32[64,1024]{1,0:T(8,128)S(1)}, u32[]{:S(2)}, u32[]{:S(2)}) collective-permute-start(f32[64,1024]{1,0:T(8,128)S(1)} %get-tuple-element.50.refs_7_.refs_5_), channel_id=1, source_target_pairs={{0,1},{1,0},{2,3},{3,2},{4,5},{5,4},{6,7},{7,6},{8,9},{9,8},{10,11... | collective-permute-start | bytes 786440 | tf_op jit(solution)/shard_map/ppermute | solution.py:575
  35.5 8.6 %collective-permute-start.7 = (f32[64,1024]{1,0:T(8,128)S(1)}, f32[64,1024]{1,0:T(8,128)S(1)}, u32[]{:S(2)}, u32[]{:S(2)}) collective-permute-start(f32[64,1024]{1,0:T(8,128)S(1)} %get-tuple-element.50.refs_7_.refs_5_), channel_id=1, source_target_pairs={{0,30},{1,31},{2,4},{3,5},{4,2},{5,3},{6,8},{7,9},{8,6},{9,7},{10,... | collective-permute-start | bytes 786440 | tf_op jit(solution)/shard_map/ppermute | solution.py:575
  37.3 6.9 %collective-permute-start.6 = (f32[64,1024]{1,0:T(8,128)S(1)}, f32[64,1024]{1,0:T(8,128)S(1)}, u32[]{:S(2)}, u32[]{:S(2)}) collective-permute-start(f32[64,1024]{1,0:T(8,128)S(1)} %get-tuple-element.50.refs_7_.refs_5_), channel_id=1, source_target_pairs={{0,2},{1,3},{2,0},{3,1},{4,6},{5,7},{6,4},{7,5},{8,10},{9,11},{10,... | collective-permute-start | bytes 786440 | tf_op jit(solution)/shard_map/ppermute | solution.py:575
  37.3 9.6 %collective-permute-start.10 = (f32[64,1024]{1,0:T(8,128)S(1)}, f32[64,1024]{1,0:T(8,128)S(1)}, u32[]{:S(2)}, u32[]{:S(2)}) collective-permute-start(f32[64,1024]{1,0:T(8,128)S(1)} %get-tuple-element.50.refs_7_.refs_5_), channel_id=1, source_target_pairs={{0,31},{1,30},{2,5},{3,4},{4,3},{5,2},{6,9},{7,8},{8,7},{9,6},{10,... | collective-permute-start | bytes 786440 | tf_op jit(solution)/shard_map/ppermute | solution.py:575
  42.0 4.9 %collective-permute-start.9 = (f32[64,1024]{1,0:T(8,128)S(1)}, f32[64,1024]{1,0:T(8,128)S(1)}, u32[]{:S(2)}, u32[]{:S(2)}) collective-permute-start(f32[64,1024]{1,0:T(8,128)S(1)} %collective-permute-done.8.refs_10_.refs_8_), channel_id=1, source_target_pairs={{0,2},{1,3},{2,0},{3,1},{4,6},{5,7},{6,4},{7,5},{8,10},{9,11},{10,... | collective-permute-start | bytes 786440 | tf_op jit(solution)/shard_map/ppermute | solution.py:575
  56.8 13.2 %collective-permute-start.11 = (f32[512,256]{1,0:T(8,128)S(1)}, f32[512,256]{1,0:T(8,128)S(1)}, u32[]{:S(2)}, u32[]{:S(2)}) collective-permute-start(f32[512,256]{1,0:T(8,128)S(1)} %get-tuple-element.70), channel_id=1, source_target_pairs={{0,1},{1,0},{2,3},{3,2},{4,5},{5,4},{6,7},{7,6},{8,9},{9,8},{10,11... | collective-permute-start | bytes 1572872 | tf_op jit(solution)/shard_map/ppermute | solution.py:575

commit v2 on v1

--- a/solution.py
+++ b/solution.py
@@ -150,10 +150,13 @@
     d_ref[at, :] = jnp.broadcast_to((value - mean) * scale, (per_patch, d_ref.shape[1]))
 
 
-def prepare_kernel(pieces, batch, members, patches_of, places, *refs):
+def prepare_kernel(pieces, batch, members, patches_of, places, crossing, *refs):
     place_refs, refs = refs[:places], refs[places:]
-    near_ref, values_ref, var_ref, ah_ref, al_ref, *refs = refs
-    sources, (sh_ref, sl_ref, d_ref, g_ref, cross_ref, flat) = refs[:-6], refs[-6:]
+    near_ref, values_ref, var_ref, *refs = refs
+    refs, flat = refs[:-1], refs[-1]
+    if crossing:
+        (ah_ref, al_ref, *refs), cross_ref = refs[:-1], refs[-1]
+    sources, (sh_ref, sl_ref, d_ref, g_ref) = refs[:-4], refs[-4:]
     patches, own = patches_of(*place_refs)
     columns = table(patches[: len(pieces)], own, near_ref, values_ref, var_ref, batch, flat)
     for i, piece in enumerate(pieces):
@@ -161,18 +164,21 @@
     count = len(pieces) * values_ref.shape[2]
     s = (sh_ref[0:count], sl_ref[0:count])
     g_ref[0:count, 0:count] = dot3(s, s, NT)
-    cross_ref[0:count] = dot3(s, (ah_ref[...], al_ref[...]))
-
-
-def factor_kernel(pieces, batch, members, chunk, patches_of, places, ready, *refs):
+    if crossing:
+        cross_ref[0:count] = dot3(s, (ah_ref[...], al_ref[...]))
+
+
+def factor_kernel(pieces, batch, members, chunk, patches_of, places, ready, crossing, *refs):
     place_refs, refs = refs[:places], refs[places:]
     near_ref, values_ref, var_ref, *refs = refs
     refs, (flat, eye_ref, x_ref, wa, wb) = refs[:-5], refs[-5:]
-    if ready:
+    if crossing:
         refs, cross_ref = refs[:-1], refs[-1]
     refs, (sh_ref, sl_ref, d_ref, g_ref, xh_ref, xl_ref, n_ref) = refs[:-7], refs[-7:]
-    if ready:
+    if crossing:
         refs, (ah_ref, al_ref) = refs[:-7], refs[-7:-5]
+    elif ready:
+        refs = refs[:-4]
     sources = refs
     per_patch = values_ref.shape[2]
     blocks = len(pieces)
@@ -187,10 +193,12 @@
     left = (sh_ref[0:head], sl_ref[0:head])
     fresh = ready * per_patch
     g_ref[fresh:n, 0:head] = dot3((sh_ref[fresh:n], sl_ref[fresh:n]), left, NT)
+    if 0 < fresh < head:
+        g_ref[0:fresh, fresh:head] = jnp.transpose(g_ref[fresh:head, 0:fresh])
     low = (sh_ref[head:n], sl_ref[head:n])
     g_ref[head:n, head:n] = dot3(low, low, NT)
     g_ref[0:head, head:n] = jnp.transpose(g_ref[head:n, 0:head])
-    if ready:
+    if crossing:
         cross_ref[fresh:n] = dot3((sh_ref[fresh:n], sl_ref[fresh:n]), (ah_ref[...], al_ref[...]))
     g = g_ref[...]
     square = jnp.sum(jnp.sum(g * g, axis=0, keepdims=True), axis=1, keepdims=True)
@@ -233,10 +241,8 @@
     store((wa.at[0], wa.at[1]), 0, *corner_of(weight, keep, left, corner))
 
     def corners_of(source):
-        ends = [
-            jnp.concatenate([source[i, head:n, 0:n], source[i, head:n, n : 2 * n]], axis=0) for i in (0, 1)
-        ]
-        return dot3(ends, (source[0, :, head:n], source[1, :, head:n]))
+        ends = [jnp.concatenate([source[i, :, head:n], source[i, :, n + head : 2 * n]], axis=1) for i in (0, 1)]
+        return dot3([source[i, head:n, 0:n] for i in (0, 1)], ends)
 
     def advance(source, target, rho2):
         weight = 2.0 / (2.0 - rho2)
@@ -245,10 +251,10 @@
         left = dot3(parts, (source[0, :, 0:head], source[1, :, 0:head]))
         corners = corners_of(source)
         both = (target.at[0], target.at[1])
-        store(both, 0, *corner_of(weight, keep, left, corners[0:tail]))
+        store(both, 0, *corner_of(weight, keep, left, corners[:, 0:tail]))
         left = dot3(parts, (source[0, :, n : n + head], source[1, :, n : n + head]))
         left = weight * (x_ref[:, 0:head] + left)
-        corner = weight * (x_ref[head:n, head:n] + corners[tail : 2 * tail])
+        corner = weight * (x_ref[head:n, head:n] + corners[:, tail : 2 * tail])
         x_ref[:, 0:head] = left
         x_ref[head:n, head:n] = corner
         store(both, n, left, corner)
@@ -259,11 +265,11 @@
     def sides(source, span):
         return [source[i, span[0] : span[1], 0:n] for i in (0, 1)]
 
-    def put(targets, start, span, block, mirror):
+    def put(targets, start, span, block):
         for target, part in zip(targets, split(block)):
             target[span[0] : span[1], start : start + head] = part
         low = max(span[0], head)
-        if mirror and low < span[1]:
+        if low < span[1]:
             for target, part in zip(targets, split(jnp.transpose(block[low - span[0] :]))):
                 target[0:head, start + low : start + span[1]] = part
 
@@ -271,10 +277,10 @@
         for target, part in zip(targets, split(block)):
             target[head:n, start + head : start + n] = part
 
-    def put_x(targets, start, weight, span, product, mirror=False):
+    def put_x(targets, start, weight, span, product):
         x = weight * (x_ref[span[0] : span[1], 0:head] + product)
         x_ref[span[0] : span[1], 0:head] = x
-        put(targets, start, span, x, mirror)
+        put(targets, start, span, x)
 
     def put_x_corner(targets, start, weight, product):
         x = weight * (x_ref[head:n, head:n] + product)
@@ -300,9 +306,9 @@
         x = []
         for k, span in enumerate(chunks):
             x.append(dot3(sides(source, span), first))
-            put(both, 0, span, weight * r[k] - keep * eye_ref[span[0] : span[1], 0:head], True)
-        put_corner(both, 0, weight * corners[0:tail] - keep * eye_ref[head:n, head:n])
-        waiting = (weight, x, corners[tail : 2 * tail])
+            put(both, 0, span, weight * r[k] - keep * eye_ref[span[0] : span[1], 0:head])
+        put_corner(both, 0, weight * corners[:, 0:tail] - keep * eye_ref[head:n, head:n])
+        waiting = (weight, x, corners[:, tail : 2 * tail])
         rho2 = keep * keep
         source, target = target, source
     for k, span in enumerate(chunks):
@@ -316,11 +322,11 @@
     weight = 2.0 / (2.0 - rho2)
     first = (source[0, :, n : n + head], source[1, :, n : n + head])
     done = (xh_ref, xl_ref)
-    ends = [source[i, head:n, n : 2 * n] for i in (0, 1)]
-    put_x_corner(done, 0, weight, dot3(ends, (source[0, :, head:n], source[1, :, head:n])))
+    ends = [source[i, :, n + head : 2 * n] for i in (0, 1)]
+    put_x_corner(done, 0, weight, dot3(sides(source, (head, n)), ends))
     x = [dot3(sides(source, span), first) for span in chunks]
     for k, span in enumerate(chunks):
-        put_x(done, 0, weight, span, x[k], True)
+        put_x(done, 0, weight, span, x[k])
 
 
 def centred(fields):
@@ -443,49 +449,57 @@
             ref[...] = part
 
 
-def last_kernel(n_ref, sh_ref, sl_ref, d_ref, g_ref, xh_ref, xl_ref, state_ref, *refs):
-    cross, z_ref, out_ref, scratch_ref, parts_ref = refs if len(refs) == 5 else (None, *refs)
-    given = cross is not None
-    cross_ref = cross if given else scratch_ref
+def last_kernel(given, n_ref, sh_ref, sl_ref, d_ref, g_ref, xh_ref, xl_ref, state_ref, *refs):
+    refs, (cross_ref, parts_ref) = refs[:-2], refs[-2:]
+    if given:
+        cross_ref, *refs = refs
+    z_ref, *out_refs = refs
     anomaly = None if given else centred([state_ref[...]])[0]
     x = (xh_ref, xl_ref)
     solve(n_ref, (sh_ref, sl_ref), g_ref, x, anomaly, z_ref, cross_ref, parts_ref, given)
     z = z_ref[...]
+    shift, zs = shift_of(z, d_ref), split(z)
     start = sh_ref.shape[1] - state_ref.shape[0]
     s = (sh_ref[...], sl_ref[...])
-    out_ref[...] = updated(state_ref[...], start, s, shift_of(z, d_ref), split(z))
-
-
-def join_kernel(column_ref, mine_ref, theirs_ref, out_ref, both, sems):
+    count = out_refs[0].shape[0]
+    for i, out_ref in enumerate(out_refs):
+        out_ref[...] = updated(state_ref[i * count : (i + 1) * count], start + i * count, s, shift, zs)
+
+
+def join_kernel(first, column_ref, mine_ref, theirs_ref, *refs):
+    out_ref, both, sems = refs[-3:]
     chunks = sems.shape[0]
     size = both.shape[0] // chunks
     column = column_ref[0]
     copies = []
     for i in range(chunks):
         at = slice(i * size, (i + 1) * size)
-        mine, theirs = mine_ref[at, :], theirs_ref[at, :]
+        mine, theirs = mine_ref[first + i * size : first + (i + 1) * size, :], theirs_ref[at, :]
         both[at, 0, :] = jnp.where(column == 0, mine, theirs)
         both[at, 1, :] = jnp.where(column == 0, theirs, mine)
-        span = pl.ds(i * size, size)
-        copies.append(pltpu.make_async_copy(both.at[span], out_ref.at[span], sems.at[i]))
+        target = out_ref.at[pl.ds(first + i * size, size)]
+        copies.append(pltpu.make_async_copy(both.at[pl.ds(i * size, size)], target, sems.at[i]))
         copies[-1].start()
     for copy in copies:
         copy.wait()
 
 
 def prepare(pieces, batch, members, patches_of, place, near, values, var, anomaly, sources, n):
-    width = anomaly[0].shape[1]
+    width = anomaly[0].shape[1] if anomaly else 0
     outs = [
         ((n, members), BF16, VMEM),
         ((n, members), BF16, VMEM),
         ((n, 128), F32, VMEM),
         ((n, n), F32, VMEM),
-        ((n, width), F32, VMEM),
     ]
-    kernel = functools.partial(prepare_kernel, pieces, batch, members, patches_of, len(place))
+    if anomaly:
+        outs.append(((n, width), F32, VMEM))
+    kernel = functools.partial(
+        prepare_kernel, pieces, batch, members, patches_of, len(place), bool(anomaly)
+    )
     args = [*place, near, values, var, *anomaly, *sources]
     ins = [SMEM] * (len(place) + 1) + [VMEM] * (len(args) - len(place) - 1)
-    return call(kernel, outs, ins, args, [pltpu.VMEM((128, 128), F32)], 6 * n * width * members)
+    return call(kernel, outs, ins, args, [pltpu.VMEM((128, 128), F32)], 6 * n * (width + n // 3) * members)
 
 
 def factor(pieces, batch, members, chunk, patches_of, place, near, values, var, sources, ready=0, before=()):
@@ -502,10 +516,14 @@
     ]
     args = [*place, near, values, var, *sources, *before]
     aliases = {}
+    crossing = len(before) > 4
+    if crossing:
+        outs.append((before[-1].shape, F32, VMEM))
     if ready:
-        outs.append((before[-1].shape, F32, VMEM))
-        first = len(args) - 5
-        aliases = {first: 0, first + 1: 1, first + 2: 2, first + 3: 3, first + 4: 7}
+        first = len(args) - 4 - crossing
+        aliases = {first: 0, first + 1: 1, first + 2: 2, first + 3: 3}
+        if crossing:
+            aliases[first + 4] = 7
     scratch = [
         pltpu.VMEM((128, 128), F32),
         pltpu.VMEM((n, n), F32),
@@ -513,7 +531,9 @@
         pltpu.VMEM((2, n, 2 * n), BF16),
         pltpu.VMEM((2, n, 2 * n), BF16),
     ]
-    kernel = functools.partial(factor_kernel, pieces, batch, members, chunk, patches_of, len(place), ready)
+    kernel = functools.partial(
+        factor_kernel, pieces, batch, members, chunk, patches_of, len(place), ready, crossing
+    )
     flops = 6 * n * n * members + 60 * n * n * n
     ins = [SMEM] * (len(place) + 1) + [VMEM] * (len(args) - len(place) - 1)
     return call(kernel, outs, ins, args, scratch, flops, FACTOR_LIMIT, aliases)
@@ -547,14 +567,15 @@
     return call(kernel, outs, [VMEM] * (4 + len(states)), [sh, sl, d, z, *states], (), flops)
 
 
-def last(factored, state):
+def last(factored, state, parts=1):
     sh, sl, d, g, xh, xl, more, *cross = factored
     n, width = sh.shape[0], state.shape[1]
-    outs = [((n, width), F32, VMEM), (state.shape, F32, VMEM)]
+    outs = [((n, width), F32, VMEM)] + [((state.shape[0] // parts, width), F32, VMEM)] * parts
     args = [more, sh, sl, d, g, xh, xl, state, *cross]
     flops = 12 * sh.shape[0] * sh.shape[1] * width
     ins = [SMEM] + [VMEM] * (len(args) - 1)
-    return call(last_kernel, outs, ins, args, solver_scratch(n, width), flops)
+    kernel = functools.partial(last_kernel, bool(cross))
+    return call(kernel, outs, ins, args, solver_scratch(n, width), flops)
 
 
 def rings(size):
@@ -586,17 +607,17 @@
     def own_of(region_ref, column_ref):
         return region_ref[0] * 2 + column_ref[0]
 
-    def around(region, within):
+    def around(region):
         side = 2 * lax.rem(region, 2) - 1
-        outer = lax.rem(region + regions + side, regions)
-        return [r * 2 + p for p in within for r in (region, region - side, outer)]
+        return region, region - side, lax.rem(region + regions + side, regions)
 
     def patches_first(region_ref, column_ref):
-        return around(region_ref[0], (0, 1)), own_of(region_ref, column_ref)
+        return [r * 2 + p for r in around(region_ref[0]) for p in (0, 1)], own_of(region_ref, column_ref)
 
     def patches_next(region_ref, column_ref):
         column = column_ref[0]
-        return around(region_ref[0], (column, 1 - column)), own_of(region_ref, column_ref)
+        within = (column, 1 - column)
+        return [r * 2 + p for p in within for r in around(region_ref[0])], own_of(region_ref, column_ref)
 
     def across(x):
         return permute(x, lambda c, q, m: (c, q, 1 - m), regions)
@@ -627,9 +648,13 @@
         [pltpu.SemaphoreType.DMA((2,))],
         aliases={2: 0},
     )
-    pieces = [[(i, (p,), 0), (3 + i, (p,), 1)] for p in range(2) for i in range(3)]
+    pieces = [[(i, (p,), 0), (3 + i, (p,), 1)] for i in range(3) for p in range(2)]
     states = [keep, across(send)]
-    factored = factor(pieces, 0, members, CHUNK, patches_first, place, near, values, var, sources)
+    given = (place, near, values, var)
+    n = len(pieces) * obs_cell.shape[2]
+    early = [[(0, (p,), 0), (1, (p,), 1)] for p in range(2)]
+    done = prepare(early, 0, members, patches_first, *given, (), [rows, other], n)
+    factored = factor(pieces, 0, members, CHUNK, patches_first, *given, sources, 2, done)
     everything = slice(None)
     low, high = (everything, slice(0, half)), (everything, slice(half, members))
     pieces = [[(i, low, 0), (i, high, 1)] for i in range(3)]
@@ -642,23 +667,26 @@
         sources = [rows, beside(rows), outside(rows), other, beside(other), far]
         mine, theirs, *anomaly = update(factored, z, states, (0, half), True)
         states = [mine, theirs]
-        given = (place, near, values, var)
-        n = factored[0].shape[0]
         done = prepare(pieces[:early], batch, members, patches_next, *given, anomaly, sources[:early], n)
         factored = factor(
             pieces, batch, members, CHUNK, patches_next, *given, sources, early, [*anomaly, *done]
         )
-    z, theirs = last(factored, states[1])
-    theirs = across(theirs)
+    z, *theirs = last(factored, states[1], 2)
+    theirs = [across(part) for part in theirs]
     (mine,) = update(factored, z, states[:1], (0,))
-    return pl.pallas_call(
-        join_kernel,
-        out_shape=jax.ShapeDtypeStruct(state.shape, F32),
-        in_specs=[SMEM, VMEM, VMEM],
-        out_specs=anywhere,
-        scratch_shapes=[pltpu.VMEM(state.shape, F32), pltpu.SemaphoreType.DMA((4,))],
-        compiler_params=pltpu.CompilerParams(vmem_limit_bytes=16 * 1024 * 1024),
-    )(place[1], mine, theirs)
+    joined = []
+    for part, other in enumerate(theirs):
+        count = other.shape[0]
+        (out,) = call(
+            functools.partial(join_kernel, part * count),
+            [(state.shape, F32, anywhere)],
+            [SMEM, VMEM, VMEM] + [anywhere] * len(joined),
+            [place[1], mine, other, *joined],
+            [pltpu.VMEM((count, *state.shape[1:]), F32), pltpu.SemaphoreType.DMA((2,))],
+            aliases={3: 0} if joined else {},
+        )
+        joined = [out]
+    return out
 
 
 def listed(table_ref):

time: 72.6 us -> 71.9 us (level)
  waiting for transfers between devices: 22.2 us -> 20.2 us
  Pallas kernels: 28.2 us -> 29.1 us
    ppermute x12 -> x13, waiting for transfers between devices: 22.2 us -> 20.2 us  [permute(): return lax.ppermute(x, BOTH, table)]
    pallas_call x10 -> x13, Pallas kernels: 27.1 us -> 29.1 us  [call(): pl.pallas_call(kernel, out_shape=shapes, in_specs=ins, out_specs=[space f...]
    pallas_call x1 -> x0, Pallas kernels: 1.11 us -> none  [paired(): pl.pallas_call(join_kernel, out_shape=jax.ShapeDtypeStruct(state.shape, F...]
    ppermute x12 -> x13, starting transfers between devices: 19.2 us -> 19.7 us  [permute(): return lax.ppermute(x, BOTH, table)]
  transfers between devices with their start and end apart: 12 -> 13, of which waited for: 7 -> 8; matrix products, arithmetic and copies ran while one was open for 0% -> 0% of each run, Pallas kernels for 17% -> 19%
where the time goes in v2:
time: 71.9 us; the launch traced here: 70.7 us
  Pallas kernels  29.1 us (40%)
  waiting for transfers between devices  20.2 us (28%)
  starting transfers between devices  19.7 us (27%)
  local copies, waits for them, and re-layouts  1.41 us (2%)
    pallas_call x13, Pallas kernels, call(): pl.pallas_call(kernel, out_shape=shapes, in_specs=ins, out_specs=[space f...  29.1 us
    ppermute x13, waiting for transfers between devices, permute(): return lax.ppermute(x, BOTH, table)  20.2 us
    ppermute x13, starting transfers between devices, permute(): return lax.ppermute(x, BOTH, table)  19.7 us
  transfers between devices with their start and end apart: 13, of which 8 were waited for; matrix products, arithmetic and copies ran while one was open for 0% of the time, Pallas kernels for 19%

profile of v2, /device:TPU:0, one launch (start us, length us, event | category | flops | bytes accessed | tf_op | source)
XLA Modules:
  0.0 70.7 jit_solution(14342781146956810913)
XLA Ops:
  0.0 1.2 %copy-done = f32[512,2,256]{2,1,0:T(2,128)S(1)} copy-done((f32[512,2,256]{2,1,0:T(2,128)S(1)}, f32[512,2,256]{2,1,0:T(2,128)}, u32[]{:S(2)}) %copy-start) | copy-done | bytes 1048600
  1.2 0.6 shard_map.55
  1.8 0.2 copy-done.1
  2.0 0.6 shard_map.56.refs_5_
  2.6 3.0 %collective-permute-start = (f32[2,64,512]{2,1,0:T(8,128)S(1)}, f32[2,64,512]{2,1,0:T(8,128)S(1)}, u32[]{:S(2)}, u32[]{:S(2)}) collective-permute-start(f32[2,64,512]{2,1,0:T(8,128)S(1)} %shard_map.56.refs_5_), channel_id=1, source_target_pairs={{0,1},{1,0},{2,3},{3,2},{4,5},{5,4},{6,7},{7,6},{8,9},{9,8},{10,11... | collective-permute-start | bytes 786440 | tf_op jit(solution)/shard_map/ppermute | solution.py:596
  5.6 3.7 %collective-permute-start.2 = (f32[2,64,512]{2,1,0:T(8,128)S(1)}, f32[2,64,512]{2,1,0:T(8,128)S(1)}, u32[]{:S(2)}, u32[]{:S(2)}) collective-permute-start(f32[2,64,512]{2,1,0:T(8,128)S(1)} %shard_map.56.refs_5_), channel_id=1, source_target_pairs={{0,30},{1,31},{2,4},{3,5},{4,2},{5,3},{6,8},{7,9},{8,6},{9,7},{10,... | collective-permute-start | bytes 786440 | tf_op jit(solution)/shard_map/ppermute | solution.py:596
  9.3 2.6 %collective-permute-done.after_ref.refs_6_.refs_8_ = f32[2,64,512]{2,1,0:T(8,128)S(1)} collective-permute-done((f32[2,64,512]{2,1,0:T(8,128)S(1)}, f32[2,64,512]{2,1,0:T(8,128)S(1)}, u32[]{:S(2)}, u32[]{:S(2)}) %collective-permute-start) | collective-permute-done | bytes 262176 | tf_op jit(solution)/shard_map/ppermute | solution.py:596
  11.9 3.3 %collective-permute-start.4 = (f32[2,64,512]{2,1,0:T(8,128)S(1)}, f32[2,64,512]{2,1,0:T(8,128)S(1)}, u32[]{:S(2)}, u32[]{:S(2)}) collective-permute-start(f32[2,64,512]{2,1,0:T(8,128)S(1)} %collective-permute-done.after_ref.refs_6_.refs_8_), channel_id=1, source_target_pairs={{0,30},{1,31},{2,4},{3,5},{4,2},{5,3},{6,8},{7,9},{8,6},{9,7},{10,... | collective-permute-start | bytes 786440 | tf_op jit(solution)/shard_map/ppermute | solution.py:596
  15.3 0.1 shard_map.57
  15.4 1.6 %collective-permute-start.5 = (f32[512,256]{1,0:T(8,128)S(1)}, f32[512,256]{1,0:T(8,128)S(1)}, u32[]{:S(2)}, u32[]{:S(2)}) collective-permute-start(f32[512,256]{1,0:T(8,128)S(1)} %get-tuple-element.58), channel_id=1, source_target_pairs={{0,1},{1,0},{2,3},{3,2},{4,5},{5,4},{6,7},{7,6},{8,9},{9,8},{10,11... | collective-permute-start | bytes 1572872 | tf_op jit(solution)/shard_map/ppermute | solution.py:596
  17.0 1.3 %shard_map.58 = (bf16[384,1024]{1,0:T(8,128)(2,1)S(1)}, bf16[384,1024]{1,0:T(8,128)(2,1)S(1)}, f32[384,128]{1,0:T(8,128)S(1)}, f32[384,384]{1,0:T(8,128)S(1)}) custom-call(s32[1]{0:T(128)} %bitcast.1.region_ref.refs_0_, s32[1]{0:T(128)} %bitcast.column_ref.refs_1_, s32[5,32]{1,0:T(8,128)S(1)} %bitcast.3, f32[32,2,64]{2,1,0:T(2,128)S(1)} %get-tuple-element.45.refs_3_, ...), custom_call_target="tpu_custom_call" | custom-call | flops 301989888 | bytes 2917000 | tf_op jit(solution)/shard_map/pallas_call | solution.py:31
  18.3 2.3 %collective-permute-done.4.refs_10_ = f32[2,64,512]{2,1,0:T(8,128)S(1)} collective-permute-done((f32[2,64,512]{2,1,0:T(8,128)S(1)}, f32[2,64,512]{2,1,0:T(8,128)S(1)}, u32[]{:S(2)}, u32[]{:S(2)}) %collective-permute-start.4) | collective-permute-done | bytes 262176 | tf_op jit(solution)/shard_map/ppermute | solution.py:596
  20.5 7.2 %shard_map.59 = (bf16[384,1024]{1,0:T(8,128)(2,1)S(1)}, bf16[384,1024]{1,0:T(8,128)(2,1)S(1)}, f32[384,128]{1,0:T(8,128)S(1)}, f32[384,384]{1,0:T(8,128)S(1)}, b...) custom-call(s32[1]{0:T(128)} %bitcast.1.region_ref.refs_0_, ...), custom_call_target="tpu_custom_call", output_to_operand_aliasing={{0}: (11, {}), {1}: (12, {}), {2}: (13, {}), {3}: (14, {})} | custom-call | flops 4303355904 | bytes 6914700 | tf_op jit(solution)/shard_map/pallas_call | solution.py:31
  27.8 2.0 %collective-permute-done.5.refs_3_.refs_1_ = f32[512,256]{1,0:T(8,128)S(1)} collective-permute-done((f32[512,256]{1,0:T(8,128)S(1)}, f32[512,256]{1,0:T(8,128)S(1)}, u32[]{:S(2)}, u32[]{:S(2)}) %collective-permute-start.5) | collective-permute-done | bytes 524320 | tf_op jit(solution)/shard_map/ppermute | solution.py:596
  29.8 4.2 %shard_map.60 = (f32[384,256]{1,0:T(8,128)S(1)}, f32[64,1024]{1,0:T(8,128)S(1)}) custom-call(s32[1]{0:T(128)} %bitcast.1.region_ref.refs_0_, s32[1]{0:T(128)} %bitcast.column_ref.refs_1_, s32[1]{0:T(128)} %get-tuple-element.51.n_ref, s32[32,2,64]{2,1,0:T(2,128)S(1)} %copy-done.1, bf16[384,1024]{1,0:T(8,128)(2,1)S(1)} %get-tuple-element.52.sh_ref, ...), custom_call_target="tpu_custom_call" | custom-call | flops 805306368 | bytes 4669452 | tf_op jit(solution)/shard_map/pallas_call | solution.py:31
  33.9 1.6 %collective-permute-start.8 = (f32[64,1024]{1,0:T(8,128)S(1)}, f32[64,1024]{1,0:T(8,128)S(1)}, u32[]{:S(2)}, u32[]{:S(2)}) collective-permute-start(f32[64,1024]{1,0:T(8,128)S(1)} %get-tuple-element.59.refs_7_.refs_5_), channel_id=1, source_target_pairs={{0,1},{1,0},{2,3},{3,2},{4,5},{5,4},{6,7},{7,6},{8,9},{9,8},{10,11... | collective-permute-start | bytes 786440 | tf_op jit(solution)/shard_map/ppermute | solution.py:596
  35.5 1.0 %collective-permute-start.7 = (f32[64,1024]{1,0:T(8,128)S(1)}, f32[64,1024]{1,0:T(8,128)S(1)}, u32[]{:S(2)}, u32[]{:S(2)}) collective-permute-start(f32[64,1024]{1,0:T(8,128)S(1)} %get-tuple-element.59.refs_7_.refs_5_), channel_id=1, source_target_pairs={{0,30},{1,31},{2,4},{3,5},{4,2},{5,3},{6,8},{7,9},{8,6},{9,7},{10,... | collective-permute-start | bytes 786440 | tf_op jit(solution)/shard_map/ppermute | solution.py:596
  36.6 3.3 %collective-permute-start.10 = (f32[64,1024]{1,0:T(8,128)S(1)}, f32[64,1024]{1,0:T(8,128)S(1)}, u32[]{:S(2)}, u32[]{:S(2)}) collective-permute-start(f32[64,1024]{1,0:T(8,128)S(1)} %get-tuple-element.59.refs_7_.refs_5_), channel_id=1, source_target_pairs={{0,31},{1,30},{2,5},{3,4},{4,3},{5,2},{6,9},{7,8},{8,7},{9,6},{10,... | collective-permute-start | bytes 786440 | tf_op jit(solution)/shard_map/ppermute | solution.py:596
  39.9 2.1 %collective-permute-done.8.refs_10_.refs_8_ = f32[64,1024]{1,0:T(8,128)S(1)} collective-permute-done((f32[64,1024]{1,0:T(8,128)S(1)}, f32[64,1024]{1,0:T(8,128)S(1)}, u32[]{:S(2)}, u32[]{:S(2)}) %collective-permute-start.8) | collective-permute-done | bytes 262176 | tf_op jit(solution)/shard_map/ppermute | solution.py:596
  42.1 1.3 %shard_map.61 = (f32[512,256]{1,0:T(8,128)S(1)}, f32[512,256]{1,0:T(8,128)S(1)}, bf16[1024,256]{1,0:T(8,128)(2,1)S(1)}, bf16[1024,256]{1,0:T(8,128)(2,1)S(1)}) custom-call(bf16[384,1024]{1,0:T(8,128)(2,1)S(1)} %get-tuple-element.52.sh_ref, bf16[384,1024]{1,0:T(8,128)(2,1)S(1)} %get-tuple-element.53.sl_ref, f32[384,128]{1,0:T(8,128)S(1)} %get-tuple-element.54.d_ref, ...), custom_call_target="tpu_custom_call" | custom-call | flops 603979776 | bytes 5308416 | tf_op jit(solution)/shard_map/pallas_call | solution.py:31
  43.3 0.8 %collective-permute-done.7.refs_9_.refs_7_ = f32[64,1024]{1,0:T(8,128)S(1)} collective-permute-done((f32[64,1024]{1,0:T(8,128)S(1)}, f32[64,1024]{1,0:T(8,128)S(1)}, u32[]{:S(2)}, u32[]{:S(2)}) %collective-permute-start.7) | collective-permute-done | bytes 262176 | tf_op jit(solution)/shard_map/ppermute | solution.py:596
  44.1 2.0 %shard_map.62 = (bf16[384,1024]{1,0:T(8,128)(2,1)S(1)}, bf16[384,1024]{1,0:T(8,128)(2,1)S(1)}, f32[384,128]{1,0:T(8,128)S(1)}, f32[384,384]{1,0:T(8,128)S(1)}, f32[384,256]{1,0:T(8,128)S(1)}) custom-call(s32[1]{0:T(128)} %bitcast.1.region_ref.refs_0_, s32[1]{0:T(128)} %bitcast.column_ref.refs_1_, s32[5,32]{1,0:T(8,128)S(1)} %bitcast.5, ...), custom_call_target="tpu_custom_call" | custom-call | flops 905969664 | bytes 4883080 | tf_op jit(solution)/shard_map/pallas_call | solution.py:31
  46.2 0.7 %collective-permute-done.10.refs_10_ = f32[64,1024]{1,0:T(8,128)S(1)} collective-permute-done((f32[64,1024]{1,0:T(8,128)S(1)}, f32[64,1024]{1,0:T(8,128)S(1)}, u32[]{:S(2)}, u32[]{:S(2)}) %collective-permute-start.10) | collective-permute-done | bytes 262176 | tf_op jit(solution)/shard_map/ppermute | solution.py:596
  46.9 6.8 %shard_map.63 = (bf16[384,1024]{1,0:T(8,128)(2,1)S(1)}, bf16[384,1024]{1,0:T(8,128)(2,1)S(1)}, f32[384,128]{1,0:T(8,128)S(1)}, f32[384,384]{1,0:T(8,128)S(1)}, b...) custom-call(s32[1]{0:T(128)} %bitcast.1.region_ref.refs_0_, ...), custom_call_target="tpu_custom_call", output_to_operand_aliasing={{0}: (13, {}), {1}: (14, {}), {2}: (15, {}), {3}: (16, {}),... | custom-call | flops 4303355904 | bytes 8749708 | tf_op jit(solution)/shard_map/pallas_call | solution.py:31
  53.7 2.7 %shard_map.64 = (f32[384,256]{1,0:T(8,128)S(1)}, f32[256,256]{1,0:T(8,128)S(1)}, f32[256,256]{1,0:T(8,128)S(1)}) custom-call(s32[1]{0:T(128)} %get-tuple-element.71.n_ref, bf16[384,1024]{1,0:T(8,128)(2,1)S(1)} %get-tuple-element.68.sh_ref, bf16[384,1024]{1,0:T(8,128)(2,1)S(1)} %get-tuple-element.69.sl_ref, f32[384,128]{1,0:T(8,128)S(1)} %get-tuple-element.70.d_ref, ...), custom_call_target="tpu_custom_call" | custom-call | flops 1207959552 | bytes 4784132 | tf_op jit(solution)/shard_map/pallas_call | solution.py:31
  56.4 1.6 %collective-permute-start.12 = (f32[256,256]{1,0:T(8,128)S(1)}, f32[256,256]{1,0:T(8,128)S(1)}, u32[]{:S(2)}, u32[]{:S(2)}) collective-permute-start(f32[256,256]{1,0:T(8,128)S(1)} %get-tuple-element.80), channel_id=1, source_target_pairs={{0,1},{1,0},{2,3},{3,2},{4,5},{5,4},{6,7},{7,6},{8,9},{9,8},{10,11... | collective-permute-start | bytes 786440 | tf_op jit(solution)/shard_map/ppermute | solution.py:596
  58.0 0.5 collective-permute-start.11
  58.5 0.6 shard_map.65.mine_ref
  59.0 5.0 %collective-permute-done.12.theirs_ref = f32[256,256]{1,0:T(8,128)S(1)} collective-permute-done((f32[256,256]{1,0:T(8,128)S(1)}, f32[256,256]{1,0:T(8,128)S(1)}, u32[]{:S(2)}, u32[]{:S(2)}) %collective-permute-start.12) | collective-permute-done | bytes 262176 | tf_op jit(solution)/shard_map/ppermute | solution.py:596
  64.0 0.9 %shard_map.66.refs_0_ = f32[512,2,256]{2,1,0:T(2,128)} custom-call(s32[1]{0:T(128)} %bitcast.column_ref.refs_1_, f32[512,256]{1,0:T(8,128)S(1)} %shard_map.65.mine_ref, f32[256,256]{1,0:T(8,128)S(1)} %collective-permute-done.12.theirs_ref), custom_call_target="tpu_custom_call" | custom-call | bytes 1835012 | tf_op jit(solution)/shard_map/pallas_call | solution.py:31
  64.9 4.7 %collective-permute-done.11.theirs_ref = f32[256,256]{1,0:T(8,128)S(1)} collective-permute-done((f32[256,256]{1,0:T(8,128)S(1)}, f32[256,256]{1,0:T(8,128)S(1)}, u32[]{:S(2)}, u32[]{:S(2)}) %collective-permute-start.11) | collective-permute-done | bytes 262176 | tf_op jit(solution)/shard_map/ppermute | solution.py:596
  69.6 0.9 %shard_map.67 = f32[512,2,256]{2,1,0:T(2,128)} custom-call(s32[1]{0:T(128)} %bitcast.column_ref.refs_1_, f32[512,256]{1,0:T(8,128)S(1)} %shard_map.65.mine_ref, f32[256,256]{1,0:T(8,128)S(1)} %collective-permute-done.11.theirs_ref, f32[512,2,256]{2,1,0:T(2,128)} %shard_map.66.refs_0_), custom_call_target="tpu_custom_call", output_to_operand_aliasing={{}: (3, {})} | custom-call | bytes 2883588 | tf_op jit(solution)/shard_map/pallas_call | solution.py:31
  (17 shorter events, 0.0 us)
Async XLA Ops:
  0.0 1.2 %copy-start = (f32[512,2,256]{2,1,0:T(2,128)S(1)}, f32[512,2,256]{2,1,0:T(2,128)}, u32[]{:S(2)}) copy-start(f32[512,2,256]{2,1,0:T(2,128)} %state_ref.1) | copy-start | bytes 3145732
  1.2 0.8 %copy-start.1 = (s32[32,2,64]{2,1,0:T(2,128)S(1)}, s32[32,2,64]{2,1,0:T(2,128)}, u32[]{:S(2)}) copy-start(s32[32,2,64]{2,1,0:T(2,128)} %cells_ref.3) | copy-start | bytes 49156
  2.0 13.3 %copy-start.2 = (f32[32,2,64]{2,1,0:T(2,128)S(1)}, f32[32,2,64]{2,1,0:T(2,128)}, u32[]{:S(2)}) copy-start(f32[32,2,64]{2,1,0:T(2,128)} %values_hbm.1) | copy-start | bytes 49156
  2.0 13.3 %copy-start.3 = (f32[32,2,64]{2,1,0:T(2,128)S(1)}, f32[32,2,64]{2,1,0:T(2,128)}, u32[]{:S(2)}) copy-start(f32[32,2,64]{2,1,0:T(2,128)} %var_hbm.1) | copy-start | bytes 49156
  2.6 9.3 %collective-permute-start = (f32[2,64,512]{2,1,0:T(8,128)S(1)}, f32[2,64,512]{2,1,0:T(8,128)S(1)}, u32[]{:S(2)}, u32[]{:S(2)}) collective-permute-start(f32[2,64,512]{2,1,0:T(8,128)S(1)} %shard_map.56.refs_5_), channel_id=1, source_target_pairs={{0,1},{1,0},{2,3},{3,2},{4,5},{5,4},{6,7},{7,6},{8,9},{9,8},{10,11... | collective-permute-start | bytes 786440 | tf_op jit(solution)/shard_map/ppermute | solution.py:596
  5.6 12.6 %collective-permute-start.2 = (f32[2,64,512]{2,1,0:T(8,128)S(1)}, f32[2,64,512]{2,1,0:T(8,128)S(1)}, u32[]{:S(2)}, u32[]{:S(2)}) collective-permute-start(f32[2,64,512]{2,1,0:T(8,128)S(1)} %shard_map.56.refs_5_), channel_id=1, source_target_pairs={{0,30},{1,31},{2,4},{3,5},{4,2},{5,3},{6,8},{7,9},{8,6},{9,7},{10,... | collective-permute-start | bytes 786440 | tf_op jit(solution)/shard_map/ppermute | solution.py:596
  9.3 8.9 %collective-permute-start.1 = (f32[2,64,512]{2,1,0:T(8,128)S(1)}, f32[2,64,512]{2,1,0:T(8,128)S(1)}, u32[]{:S(2)}, u32[]{:S(2)}) collective-permute-start(f32[2,64,512]{2,1,0:T(8,128)S(1)} %shard_map.56.refs_5_), channel_id=1, source_target_pairs={{0,2},{1,3},{2,0},{3,1},{4,6},{5,7},{6,4},{7,5},{8,10},{9,11},{10,... | collective-permute-start | bytes 786440 | tf_op jit(solution)/shard_map/ppermute | solution.py:596
  11.9 8.6 %collective-permute-start.4 = (f32[2,64,512]{2,1,0:T(8,128)S(1)}, f32[2,64,512]{2,1,0:T(8,128)S(1)}, u32[]{:S(2)}, u32[]{:S(2)}) collective-permute-start(f32[2,64,512]{2,1,0:T(8,128)S(1)} %collective-permute-done.after_ref.refs_6_.refs_8_), channel_id=1, source_target_pairs={{0,30},{1,31},{2,4},{3,5},{4,2},{5,3},{6,8},{7,9},{8,6},{9,7},{10,... | collective-permute-start | bytes 786440 | tf_op jit(solution)/shard_map/ppermute | solution.py:596
  15.2 5.3 %collective-permute-start.3 = (f32[2,64,512]{2,1,0:T(8,128)S(1)}, f32[2,64,512]{2,1,0:T(8,128)S(1)}, u32[]{:S(2)}, u32[]{:S(2)}) collective-permute-start(f32[2,64,512]{2,1,0:T(8,128)S(1)} %collective-permute-done.after_ref.refs_6_.refs_8_), channel_id=1, source_target_pairs={{0,2},{1,3},{2,0},{3,1},{4,6},{5,7},{6,4},{7,5},{8,10},{9,11},{10,... | collective-permute-start | bytes 786440 | tf_op jit(solution)/shard_map/ppermute | solution.py:596
  15.4 1.6 %copy-start.4 = (s32[32,5]{0,1:T(8,128)S(1)}, s32[32,5]{0,1:T(8,128)}, u32[]{:S(2)}) copy-start(s32[32,5]{0,1:T(8,128)} %param.6) | copy-start | bytes 1924
  15.4 14.4 %collective-permute-start.5 = (f32[512,256]{1,0:T(8,128)S(1)}, f32[512,256]{1,0:T(8,128)S(1)}, u32[]{:S(2)}, u32[]{:S(2)}) collective-permute-start(f32[512,256]{1,0:T(8,128)S(1)} %get-tuple-element.58), channel_id=1, source_target_pairs={{0,1},{1,0},{2,3},{3,2},{4,5},{5,4},{6,7},{7,6},{8,9},{9,8},{10,11... | collective-permute-start | bytes 1572872 | tf_op jit(solution)/shard_map/ppermute | solution.py:596
  33.9 8.1 %collective-permute-start.8 = (f32[64,1024]{1,0:T(8,128)S(1)}, f32[64,1024]{1,0:T(8,128)S(1)}, u32[]{:S(2)}, u32[]{:S(2)}) collective-permute-start(f32[64,1024]{1,0:T(8,128)S(1)} %get-tuple-element.59.refs_7_.refs_5_), channel_id=1, source_target_pairs={{0,1},{1,0},{2,3},{3,2},{4,5},{5,4},{6,7},{7,6},{8,9},{9,8},{10,11... | collective-permute-start | bytes 786440 | tf_op jit(solution)/shard_map/ppermute | solution.py:596
  35.5 8.6 %collective-permute-start.7 = (f32[64,1024]{1,0:T(8,128)S(1)}, f32[64,1024]{1,0:T(8,128)S(1)}, u32[]{:S(2)}, u32[]{:S(2)}) collective-permute-start(f32[64,1024]{1,0:T(8,128)S(1)} %get-tuple-element.59.refs_7_.refs_5_), channel_id=1, source_target_pairs={{0,30},{1,31},{2,4},{3,5},{4,2},{5,3},{6,8},{7,9},{8,6},{9,7},{10,... | collective-permute-start | bytes 786440 | tf_op jit(solution)/shard_map/ppermute | solution.py:596
  36.6 7.6 %collective-permute-start.6 = (f32[64,1024]{1,0:T(8,128)S(1)}, f32[64,1024]{1,0:T(8,128)S(1)}, u32[]{:S(2)}, u32[]{:S(2)}) collective-permute-start(f32[64,1024]{1,0:T(8,128)S(1)} %get-tuple-element.59.refs_7_.refs_5_), channel_id=1, source_target_pairs={{0,2},{1,3},{2,0},{3,1},{4,6},{5,7},{6,4},{7,5},{8,10},{9,11},{10,... | collective-permute-start | bytes 786440 | tf_op jit(solution)/shard_map/ppermute | solution.py:596
  36.6 10.3 %collective-permute-start.10 = (f32[64,1024]{1,0:T(8,128)S(1)}, f32[64,1024]{1,0:T(8,128)S(1)}, u32[]{:S(2)}, u32[]{:S(2)}) collective-permute-start(f32[64,1024]{1,0:T(8,128)S(1)} %get-tuple-element.59.refs_7_.refs_5_), channel_id=1, source_target_pairs={{0,31},{1,30},{2,5},{3,4},{4,3},{5,2},{6,9},{7,8},{8,7},{9,6},{10,... | collective-permute-start | bytes 786440 | tf_op jit(solution)/shard_map/ppermute | solution.py:596
  42.0 4.8 %collective-permute-start.9 = (f32[64,1024]{1,0:T(8,128)S(1)}, f32[64,1024]{1,0:T(8,128)S(1)}, u32[]{:S(2)}, u32[]{:S(2)}) collective-permute-start(f32[64,1024]{1,0:T(8,128)S(1)} %collective-permute-done.8.refs_10_.refs_8_), channel_id=1, source_target_pairs={{0,2},{1,3},{2,0},{3,1},{4,6},{5,7},{6,4},{7,5},{8,10},{9,11},{10,... | collective-permute-start | bytes 786440 | tf_op jit(solution)/shard_map/ppermute | solution.py:596
  56.4 7.6 %collective-permute-start.12 = (f32[256,256]{1,0:T(8,128)S(1)}, f32[256,256]{1,0:T(8,128)S(1)}, u32[]{:S(2)}, u32[]{:S(2)}) collective-permute-start(f32[256,256]{1,0:T(8,128)S(1)} %get-tuple-element.80), channel_id=1, source_target_pairs={{0,1},{1,0},{2,3},{3,2},{4,5},{5,4},{6,7},{7,6},{8,9},{9,8},{10,11... | collective-permute-start | bytes 786440 | tf_op jit(solution)/shard_map/ppermute | solution.py:596
  58.0 11.7 %collective-permute-start.11 = (f32[256,256]{1,0:T(8,128)S(1)}, f32[256,256]{1,0:T(8,128)S(1)}, u32[]{:S(2)}, u32[]{:S(2)}) collective-permute-start(f32[256,256]{1,0:T(8,128)S(1)} %get-tuple-element.79), channel_id=1, source_target_pairs={{0,1},{1,0},{2,3},{3,2},{4,5},{5,4},{6,7},{7,6},{8,9},{9,8},{10,11... | collective-permute-start | bytes 786440 | tf_op jit(solution)/shard_map/ppermute | solution.py:596

commit v3 on v2

--- a/solution.py
+++ b/solution.py
@@ -17,7 +17,9 @@
 NN = (((1,), (0,)), ((), ()))
 NT = (((1,), (1,)), ((), ()))
 TN = (((0,), (0,)), ((), ()))
-RESIDUAL = 1e-3
+RESIDUAL = 0.03
+REFINEMENTS = 2
+STEPS = 6
 FACTOR_LIMIT = 24
 MOST_STEPS = 15
 TILE = 256
@@ -206,7 +208,7 @@
     size = square[0, 0]
     limits = step_limits()
     pairs = jnp.int32(0)
-    for k in range(7, MOST_STEPS - 2, 2):
+    for k in range(STEPS, MOST_STEPS - 2, 2):
         limit = limits[k] * (1.0 - 1e-4)
         pairs = pairs + (size > limit * limit).astype(jnp.int32)
     n_ref[0] = (size > 1.6e7).astype(jnp.int32) + (size > 1e8).astype(jnp.int32)
@@ -289,7 +291,7 @@
 
     waiting = None
     source, target = wa, wb
-    for _ in range(5):
+    for _ in range(STEPS - 2):
         weight = 2.0 / (2.0 - rho2)
         keep = 0.5 * rho2 * weight
         first = (source[0, :, 0:head], source[1, :, 0:head])
@@ -372,7 +374,7 @@
         keep(0, span, cross_ref[span] - z_ref[span] - value)
 
     def refined(span, value):
-        z_ref[span] = z_ref[span] + value
+        solved(span, z_ref[span] + value)
 
     if crossed_already:
         keep(0, slice(0, n), cross_ref[...])
@@ -383,6 +385,7 @@
         (lambda span: dot3(split(g_ref[span]), kept(1)), left),
         (lambda span: dot3(some(x, span), kept(0)), refined),
     ]
+    stages += stages[1:] * (REFINEMENTS - 1)
     for i, (product, work) in enumerate(stages):
         for extra in between[i : i + 1]:
             extra()
@@ -461,9 +464,11 @@
     shift, zs = shift_of(z, d_ref), split(z)
     start = sh_ref.shape[1] - state_ref.shape[0]
     s = (sh_ref[...], sl_ref[...])
-    count = out_refs[0].shape[0]
-    for i, out_ref in enumerate(out_refs):
-        out_ref[...] = updated(state_ref[i * count : (i + 1) * count], start + i * count, s, shift, zs)
+    first = 0
+    for out_ref in out_refs:
+        stop = first + out_ref.shape[0]
+        out_ref[...] = updated(state_ref[first:stop], start + first, s, shift, zs)
+        first = stop
 
 
 def join_kernel(first, column_ref, mine_ref, theirs_ref, *refs):
@@ -567,10 +572,10 @@
     return call(kernel, outs, [VMEM] * (4 + len(states)), [sh, sl, d, z, *states], (), flops)
 
 
-def last(factored, state, parts=1):
+def last(factored, state, counts=None):
     sh, sl, d, g, xh, xl, more, *cross = factored
     n, width = sh.shape[0], state.shape[1]
-    outs = [((n, width), F32, VMEM)] + [((state.shape[0] // parts, width), F32, VMEM)] * parts
+    outs = [((n, width), F32, VMEM)] + [((count, width), F32, VMEM) for count in counts or state.shape[:1]]
     args = [more, sh, sl, d, g, xh, xl, state, *cross]
     flops = 12 * sh.shape[0] * sh.shape[1] * width
     ins = [SMEM] + [VMEM] * (len(args) - 1)
@@ -671,14 +676,15 @@
         factored = factor(
             pieces, batch, members, CHUNK, patches_next, *given, sources, early, [*anomaly, *done]
         )
-    z, *theirs = last(factored, states[1], 2)
+    most = half - half // 4
+    z, *theirs = last(factored, states[1], (most, half - most))
     theirs = [across(part) for part in theirs]
     (mine,) = update(factored, z, states[:1], (0,))
     joined = []
-    for part, other in enumerate(theirs):
+    for first, other in zip((0, most), theirs):
         count = other.shape[0]
         (out,) = call(
-            functools.partial(join_kernel, part * count),
+            functools.partial(join_kernel, first),
             [(state.shape, F32, anywhere)],
             [SMEM, VMEM, VMEM] + [anywhere] * len(joined),
             [place[1], mine, other, *joined],

time: 71.9 us -> 73.4 us (1.021)
  waiting for transfers between devices: 20.2 us -> 21.1 us
  Pallas kernels: 29.1 us -> 30 us
    pallas_call x13, Pallas kernels: 29.1 us -> 30 us  [call(): pl.pallas_call(kernel, out_shape=shapes, in_specs=ins, out_specs=[space f...]
    ppermute x13, waiting for transfers between devices: 20.2 us -> 21.1 us  [permute(): return lax.ppermute(x, BOTH, table)]
  transfers between devices with their start and end apart: 13 -> 13, of which waited for: 8 -> 8; matrix products, arithmetic and copies ran while one was open for 0% -> 0% of each run, Pallas kernels for 19% -> 18%
where the time goes in v3:
time: 73.4 us; the launch traced here: 72.4 us
  Pallas kernels  30 us (41%)
  waiting for transfers between devices  21.1 us (29%)
  starting transfers between devices  19.7 us (27%)
  local copies, waits for them, and re-layouts  1.41 us (2%)
    pallas_call x13, Pallas kernels, call(): pl.pallas_call(kernel, out_shape=shapes, in_specs=ins, out_specs=[space f...  30 us
    ppermute x13, waiting for transfers between devices, permute(): return lax.ppermute(x, BOTH, table)  21.1 us
    ppermute x13, starting transfers between devices, permute(): return lax.ppermute(x, BOTH, table)  19.7 us
  transfers between devices with their start and end apart: 13, of which 8 were waited for; matrix products, arithmetic and copies ran while one was open for 0% of the time, Pallas kernels for 18%

profile of v3, /device:TPU:0, one launch (start us, length us, event | category | flops | bytes accessed | tf_op | source)
XLA Modules:
  0.0 72.4 jit_solution(23414548103759371)
XLA Ops:
  0.0 1.2 %copy-done = f32[512,2,256]{2,1,0:T(2,128)S(1)} copy-done((f32[512,2,256]{2,1,0:T(2,128)S(1)}, f32[512,2,256]{2,1,0:T(2,128)}, u32[]{:S(2)}) %copy-start) | copy-done | bytes 1048600
  1.2 0.6 shard_map.55
  1.8 0.2 copy-done.1
  2.0 0.6 shard_map.56.refs_5_
  2.6 3.0 %collective-permute-start = (f32[2,64,512]{2,1,0:T(8,128)S(1)}, f32[2,64,512]{2,1,0:T(8,128)S(1)}, u32[]{:S(2)}, u32[]{:S(2)}) collective-permute-start(f32[2,64,512]{2,1,0:T(8,128)S(1)} %shard_map.56.refs_5_), channel_id=1, source_target_pairs={{0,1},{1,0},{2,3},{3,2},{4,5},{5,4},{6,7},{7,6},{8,9},{9,8},{10,11... | collective-permute-start | bytes 786440 | tf_op jit(solution)/shard_map/ppermute | solution.py:601
  5.6 3.7 %collective-permute-start.2 = (f32[2,64,512]{2,1,0:T(8,128)S(1)}, f32[2,64,512]{2,1,0:T(8,128)S(1)}, u32[]{:S(2)}, u32[]{:S(2)}) collective-permute-start(f32[2,64,512]{2,1,0:T(8,128)S(1)} %shard_map.56.refs_5_), channel_id=1, source_target_pairs={{0,30},{1,31},{2,4},{3,5},{4,2},{5,3},{6,8},{7,9},{8,6},{9,7},{10,... | collective-permute-start | bytes 786440 | tf_op jit(solution)/shard_map/ppermute | solution.py:601
  9.3 2.6 %collective-permute-done.after_ref.refs_6_.refs_8_ = f32[2,64,512]{2,1,0:T(8,128)S(1)} collective-permute-done((f32[2,64,512]{2,1,0:T(8,128)S(1)}, f32[2,64,512]{2,1,0:T(8,128)S(1)}, u32[]{:S(2)}, u32[]{:S(2)}) %collective-permute-start) | collective-permute-done | bytes 262176 | tf_op jit(solution)/shard_map/ppermute | solution.py:601
  11.9 3.3 %collective-permute-start.4 = (f32[2,64,512]{2,1,0:T(8,128)S(1)}, f32[2,64,512]{2,1,0:T(8,128)S(1)}, u32[]{:S(2)}, u32[]{:S(2)}) collective-permute-start(f32[2,64,512]{2,1,0:T(8,128)S(1)} %collective-permute-done.after_ref.refs_6_.refs_8_), channel_id=1, source_target_pairs={{0,30},{1,31},{2,4},{3,5},{4,2},{5,3},{6,8},{7,9},{8,6},{9,7},{10,... | collective-permute-start | bytes 786440 | tf_op jit(solution)/shard_map/ppermute | solution.py:601
  15.3 0.1 shard_map.57
  15.4 1.6 %collective-permute-start.5 = (f32[512,256]{1,0:T(8,128)S(1)}, f32[512,256]{1,0:T(8,128)S(1)}, u32[]{:S(2)}, u32[]{:S(2)}) collective-permute-start(f32[512,256]{1,0:T(8,128)S(1)} %get-tuple-element.58), channel_id=1, source_target_pairs={{0,1},{1,0},{2,3},{3,2},{4,5},{5,4},{6,7},{7,6},{8,9},{9,8},{10,11... | collective-permute-start | bytes 1572872 | tf_op jit(solution)/shard_map/ppermute | solution.py:601
  17.0 1.3 %shard_map.58 = (bf16[384,1024]{1,0:T(8,128)(2,1)S(1)}, bf16[384,1024]{1,0:T(8,128)(2,1)S(1)}, f32[384,128]{1,0:T(8,128)S(1)}, f32[384,384]{1,0:T(8,128)S(1)}) custom-call(s32[1]{0:T(128)} %bitcast.1.region_ref.refs_0_, s32[1]{0:T(128)} %bitcast.column_ref.refs_1_, s32[5,32]{1,0:T(8,128)S(1)} %bitcast.3, f32[32,2,64]{2,1,0:T(2,128)S(1)} %get-tuple-element.45.refs_3_, ...), custom_call_target="tpu_custom_call" | custom-call | flops 301989888 | bytes 2917000 | tf_op jit(solution)/shard_map/pallas_call | solution.py:33
  18.3 2.3 %collective-permute-done.4.refs_10_ = f32[2,64,512]{2,1,0:T(8,128)S(1)} collective-permute-done((f32[2,64,512]{2,1,0:T(8,128)S(1)}, f32[2,64,512]{2,1,0:T(8,128)S(1)}, u32[]{:S(2)}, u32[]{:S(2)}) %collective-permute-start.4) | collective-permute-done | bytes 262176 | tf_op jit(solution)/shard_map/ppermute | solution.py:601
  20.5 6.5 %shard_map.59 = (bf16[384,1024]{1,0:T(8,128)(2,1)S(1)}, bf16[384,1024]{1,0:T(8,128)(2,1)S(1)}, f32[384,128]{1,0:T(8,128)S(1)}, f32[384,384]{1,0:T(8,128)S(1)}, b...) custom-call(s32[1]{0:T(128)} %bitcast.1.region_ref.refs_0_, ...), custom_call_target="tpu_custom_call", output_to_operand_aliasing={{0}: (11, {}), {1}: (12, {}), {2}: (13, {}), {3}: (14, {})} | custom-call | flops 4303355904 | bytes 6914700 | tf_op jit(solution)/shard_map/pallas_call | solution.py:33
  27.1 2.7 %collective-permute-done.5.refs_3_.refs_1_ = f32[512,256]{1,0:T(8,128)S(1)} collective-permute-done((f32[512,256]{1,0:T(8,128)S(1)}, f32[512,256]{1,0:T(8,128)S(1)}, u32[]{:S(2)}, u32[]{:S(2)}) %collective-permute-start.5) | collective-permute-done | bytes 524320 | tf_op jit(solution)/shard_map/ppermute | solution.py:601
  29.8 5.1 %shard_map.60 = (f32[384,256]{1,0:T(8,128)S(1)}, f32[64,1024]{1,0:T(8,128)S(1)}) custom-call(s32[1]{0:T(128)} %bitcast.1.region_ref.refs_0_, s32[1]{0:T(128)} %bitcast.column_ref.refs_1_, s32[1]{0:T(128)} %get-tuple-element.51.n_ref, s32[32,2,64]{2,1,0:T(2,128)S(1)} %copy-done.1, bf16[384,1024]{1,0:T(8,128)(2,1)S(1)} %get-tuple-element.52.sh_ref, ...), custom_call_target="tpu_custom_call" | custom-call | flops 805306368 | bytes 4669452 | tf_op jit(solution)/shard_map/pallas_call | solution.py:33
  34.9 1.6 %collective-permute-start.8 = (f32[64,1024]{1,0:T(8,128)S(1)}, f32[64,1024]{1,0:T(8,128)S(1)}, u32[]{:S(2)}, u32[]{:S(2)}) collective-permute-start(f32[64,1024]{1,0:T(8,128)S(1)} %get-tuple-element.59.refs_7_.refs_5_), channel_id=1, source_target_pairs={{0,1},{1,0},{2,3},{3,2},{4,5},{5,4},{6,7},{7,6},{8,9},{9,8},{10,11... | collective-permute-start | bytes 786440 | tf_op jit(solution)/shard_map/ppermute | solution.py:601
  36.5 0.4 collective-permute-start.7
  36.9 4.0 %collective-permute-start.10 = (f32[64,1024]{1,0:T(8,128)S(1)}, f32[64,1024]{1,0:T(8,128)S(1)}, u32[]{:S(2)}, u32[]{:S(2)}) collective-permute-start(f32[64,1024]{1,0:T(8,128)S(1)} %get-tuple-element.59.refs_7_.refs_5_), channel_id=1, source_target_pairs={{0,31},{1,30},{2,5},{3,4},{4,3},{5,2},{6,9},{7,8},{8,7},{9,6},{10,... | collective-permute-start | bytes 786440 | tf_op jit(solution)/shard_map/ppermute | solution.py:601
  40.9 2.4 %collective-permute-done.8.refs_10_.refs_8_ = f32[64,1024]{1,0:T(8,128)S(1)} collective-permute-done((f32[64,1024]{1,0:T(8,128)S(1)}, f32[64,1024]{1,0:T(8,128)S(1)}, u32[]{:S(2)}, u32[]{:S(2)}) %collective-permute-start.8) | collective-permute-done | bytes 262176 | tf_op jit(solution)/shard_map/ppermute | solution.py:601
  43.3 1.2 %shard_map.61 = (f32[512,256]{1,0:T(8,128)S(1)}, f32[512,256]{1,0:T(8,128)S(1)}, bf16[1024,256]{1,0:T(8,128)(2,1)S(1)}, bf16[1024,256]{1,0:T(8,128)(2,1)S(1)}) custom-call(bf16[384,1024]{1,0:T(8,128)(2,1)S(1)} %get-tuple-element.52.sh_ref, bf16[384,1024]{1,0:T(8,128)(2,1)S(1)} %get-tuple-element.53.sl_ref, f32[384,128]{1,0:T(8,128)S(1)} %get-tuple-element.54.d_ref, ...), custom_call_target="tpu_custom_call" | custom-call | flops 603979776 | bytes 5308416 | tf_op jit(solution)/shard_map/pallas_call | solution.py:33
  44.5 0.6 collective-permute-done.7.refs_9_.refs_7_
  45.1 2.0 %shard_map.62 = (bf16[384,1024]{1,0:T(8,128)(2,1)S(1)}, bf16[384,1024]{1,0:T(8,128)(2,1)S(1)}, f32[384,128]{1,0:T(8,128)S(1)}, f32[384,384]{1,0:T(8,128)S(1)}, f32[384,256]{1,0:T(8,128)S(1)}) custom-call(s32[1]{0:T(128)} %bitcast.1.region_ref.refs_0_, s32[1]{0:T(128)} %bitcast.column_ref.refs_1_, s32[5,32]{1,0:T(8,128)S(1)} %bitcast.5, ...), custom_call_target="tpu_custom_call" | custom-call | flops 905969664 | bytes 4883080 | tf_op jit(solution)/shard_map/pallas_call | solution.py:33
  47.1 0.7 collective-permute-done.10.refs_10_
  47.9 6.5 %shard_map.63 = (bf16[384,1024]{1,0:T(8,128)(2,1)S(1)}, bf16[384,1024]{1,0:T(8,128)(2,1)S(1)}, f32[384,128]{1,0:T(8,128)S(1)}, f32[384,384]{1,0:T(8,128)S(1)}, b...) custom-call(s32[1]{0:T(128)} %bitcast.1.region_ref.refs_0_, ...), custom_call_target="tpu_custom_call", output_to_operand_aliasing={{0}: (13, {}), {1}: (14, {}), {2}: (15, {}), {3}: (16, {}),... | custom-call | flops 4303355904 | bytes 8749708 | tf_op jit(solution)/shard_map/pallas_call | solution.py:33
  54.3 3.6 %shard_map.64 = (f32[384,256]{1,0:T(8,128)S(1)}, f32[384,256]{1,0:T(8,128)S(1)}, f32[128,256]{1,0:T(8,128)S(1)}) custom-call(s32[1]{0:T(128)} %get-tuple-element.71.n_ref, bf16[384,1024]{1,0:T(8,128)(2,1)S(1)} %get-tuple-element.68.sh_ref, bf16[384,1024]{1,0:T(8,128)(2,1)S(1)} %get-tuple-element.69.sl_ref, f32[384,128]{1,0:T(8,128)S(1)} %get-tuple-element.70.d_ref, ...), custom_call_target="tpu_custom_call" | custom-call | flops 1207959552 | bytes 4784132 | tf_op jit(solution)/shard_map/pallas_call | solution.py:33
  58.0 1.6 %collective-permute-start.12 = (f32[384,256]{1,0:T(8,128)S(1)}, f32[384,256]{1,0:T(8,128)S(1)}, u32[]{:S(2)}, u32[]{:S(2)}) collective-permute-start(f32[384,256]{1,0:T(8,128)S(1)} %get-tuple-element.80), channel_id=1, source_target_pairs={{0,1},{1,0},{2,3},{3,2},{4,5},{5,4},{6,7},{7,6},{8,9},{9,8},{10,11... | collective-permute-start | bytes 1179656 | tf_op jit(solution)/shard_map/ppermute | solution.py:601
  59.5 0.5 collective-permute-start.11
  60.1 0.6 shard_map.65.mine_ref
  60.6 8.1 %collective-permute-done.12.theirs_ref = f32[384,256]{1,0:T(8,128)S(1)} collective-permute-done((f32[384,256]{1,0:T(8,128)S(1)}, f32[384,256]{1,0:T(8,128)S(1)}, u32[]{:S(2)}, u32[]{:S(2)}) %collective-permute-start.12) | collective-permute-done | bytes 393248 | tf_op jit(solution)/shard_map/ppermute | solution.py:601
  68.7 1.0 %shard_map.66.refs_0_ = f32[512,2,256]{2,1,0:T(2,128)} custom-call(s32[1]{0:T(128)} %bitcast.column_ref.refs_1_, f32[512,256]{1,0:T(8,128)S(1)} %shard_map.65.mine_ref, f32[384,256]{1,0:T(8,128)S(1)} %collective-permute-done.12.theirs_ref), custom_call_target="tpu_custom_call" | custom-call | bytes 1966084 | tf_op jit(solution)/shard_map/pallas_call | solution.py:33
  69.7 1.8 %collective-permute-done.11.theirs_ref = f32[128,256]{1,0:T(8,128)S(1)} collective-permute-done((f32[128,256]{1,0:T(8,128)S(1)}, f32[128,256]{1,0:T(8,128)S(1)}, u32[]{:S(2)}, u32[]{:S(2)}) %collective-permute-start.11) | collective-permute-done | bytes 131104 | tf_op jit(solution)/shard_map/ppermute | solution.py:601
  71.5 0.8 %shard_map.67 = f32[512,2,256]{2,1,0:T(2,128)} custom-call(s32[1]{0:T(128)} %bitcast.column_ref.refs_1_, f32[512,256]{1,0:T(8,128)S(1)} %shard_map.65.mine_ref, f32[128,256]{1,0:T(8,128)S(1)} %collective-permute-done.11.theirs_ref, f32[512,2,256]{2,1,0:T(2,128)} %shard_map.66.refs_0_), custom_call_target="tpu_custom_call", output_to_operand_aliasing={{}: (3, {})} | custom-call | bytes 2752516 | tf_op jit(solution)/shard_map/pallas_call | solution.py:33
  (17 shorter events, 0.0 us)
Async XLA Ops:
  0.0 1.2 %copy-start = (f32[512,2,256]{2,1,0:T(2,128)S(1)}, f32[512,2,256]{2,1,0:T(2,128)}, u32[]{:S(2)}) copy-start(f32[512,2,256]{2,1,0:T(2,128)} %state_ref.1) | copy-start | bytes 3145732
  1.2 0.8 %copy-start.1 = (s32[32,2,64]{2,1,0:T(2,128)S(1)}, s32[32,2,64]{2,1,0:T(2,128)}, u32[]{:S(2)}) copy-start(s32[32,2,64]{2,1,0:T(2,128)} %cells_ref.3) | copy-start | bytes 49156
  2.0 13.3 %copy-start.2 = (f32[32,2,64]{2,1,0:T(2,128)S(1)}, f32[32,2,64]{2,1,0:T(2,128)}, u32[]{:S(2)}) copy-start(f32[32,2,64]{2,1,0:T(2,128)} %values_hbm.1) | copy-start | bytes 49156
  2.0 13.3 %copy-start.3 = (f32[32,2,64]{2,1,0:T(2,128)S(1)}, f32[32,2,64]{2,1,0:T(2,128)}, u32[]{:S(2)}) copy-start(f32[32,2,64]{2,1,0:T(2,128)} %var_hbm.1) | copy-start | bytes 49156
  2.6 9.3 %collective-permute-start = (f32[2,64,512]{2,1,0:T(8,128)S(1)}, f32[2,64,512]{2,1,0:T(8,128)S(1)}, u32[]{:S(2)}, u32[]{:S(2)}) collective-permute-start(f32[2,64,512]{2,1,0:T(8,128)S(1)} %shard_map.56.refs_5_), channel_id=1, source_target_pairs={{0,1},{1,0},{2,3},{3,2},{4,5},{5,4},{6,7},{7,6},{8,9},{9,8},{10,11... | collective-permute-start | bytes 786440 | tf_op jit(solution)/shard_map/ppermute | solution.py:601
  5.6 12.6 %collective-permute-start.2 = (f32[2,64,512]{2,1,0:T(8,128)S(1)}, f32[2,64,512]{2,1,0:T(8,128)S(1)}, u32[]{:S(2)}, u32[]{:S(2)}) collective-permute-start(f32[2,64,512]{2,1,0:T(8,128)S(1)} %shard_map.56.refs_5_), channel_id=1, source_target_pairs={{0,30},{1,31},{2,4},{3,5},{4,2},{5,3},{6,8},{7,9},{8,6},{9,7},{10,... | collective-permute-start | bytes 786440 | tf_op jit(solution)/shard_map/ppermute | solution.py:601
  9.3 8.9 %collective-permute-start.1 = (f32[2,64,512]{2,1,0:T(8,128)S(1)}, f32[2,64,512]{2,1,0:T(8,128)S(1)}, u32[]{:S(2)}, u32[]{:S(2)}) collective-permute-start(f32[2,64,512]{2,1,0:T(8,128)S(1)} %shard_map.56.refs_5_), channel_id=1, source_target_pairs={{0,2},{1,3},{2,0},{3,1},{4,6},{5,7},{6,4},{7,5},{8,10},{9,11},{10,... | collective-permute-start | bytes 786440 | tf_op jit(solution)/shard_map/ppermute | solution.py:601
  11.9 8.6 %collective-permute-start.4 = (f32[2,64,512]{2,1,0:T(8,128)S(1)}, f32[2,64,512]{2,1,0:T(8,128)S(1)}, u32[]{:S(2)}, u32[]{:S(2)}) collective-permute-start(f32[2,64,512]{2,1,0:T(8,128)S(1)} %collective-permute-done.after_ref.refs_6_.refs_8_), channel_id=1, source_target_pairs={{0,30},{1,31},{2,4},{3,5},{4,2},{5,3},{6,8},{7,9},{8,6},{9,7},{10,... | collective-permute-start | bytes 786440 | tf_op jit(solution)/shard_map/ppermute | solution.py:601
  15.2 5.3 %collective-permute-start.3 = (f32[2,64,512]{2,1,0:T(8,128)S(1)}, f32[2,64,512]{2,1,0:T(8,128)S(1)}, u32[]{:S(2)}, u32[]{:S(2)}) collective-permute-start(f32[2,64,512]{2,1,0:T(8,128)S(1)} %collective-permute-done.after_ref.refs_6_.refs_8_), channel_id=1, source_target_pairs={{0,2},{1,3},{2,0},{3,1},{4,6},{5,7},{6,4},{7,5},{8,10},{9,11},{10,... | collective-permute-start | bytes 786440 | tf_op jit(solution)/shard_map/ppermute | solution.py:601
  15.4 1.6 %copy-start.4 = (s32[32,5]{0,1:T(8,128)S(1)}, s32[32,5]{0,1:T(8,128)}, u32[]{:S(2)}) copy-start(s32[32,5]{0,1:T(8,128)} %param.6) | copy-start | bytes 1924
  15.4 14.4 %collective-permute-start.5 = (f32[512,256]{1,0:T(8,128)S(1)}, f32[512,256]{1,0:T(8,128)S(1)}, u32[]{:S(2)}, u32[]{:S(2)}) collective-permute-start(f32[512,256]{1,0:T(8,128)S(1)} %get-tuple-element.58), channel_id=1, source_target_pairs={{0,1},{1,0},{2,3},{3,2},{4,5},{5,4},{6,7},{7,6},{8,9},{9,8},{10,11... | collective-permute-start | bytes 1572872 | tf_op jit(solution)/shard_map/ppermute | solution.py:601
  34.9 8.4 %collective-permute-start.8 = (f32[64,1024]{1,0:T(8,128)S(1)}, f32[64,1024]{1,0:T(8,128)S(1)}, u32[]{:S(2)}, u32[]{:S(2)}) collective-permute-start(f32[64,1024]{1,0:T(8,128)S(1)} %get-tuple-element.59.refs_7_.refs_5_), channel_id=1, source_target_pairs={{0,1},{1,0},{2,3},{3,2},{4,5},{5,4},{6,7},{7,6},{8,9},{9,8},{10,11... | collective-permute-start | bytes 786440 | tf_op jit(solution)/shard_map/ppermute | solution.py:601
  36.5 8.6 %collective-permute-start.7 = (f32[64,1024]{1,0:T(8,128)S(1)}, f32[64,1024]{1,0:T(8,128)S(1)}, u32[]{:S(2)}, u32[]{:S(2)}) collective-permute-start(f32[64,1024]{1,0:T(8,128)S(1)} %get-tuple-element.59.refs_7_.refs_5_), channel_id=1, source_target_pairs={{0,30},{1,31},{2,4},{3,5},{4,2},{5,3},{6,8},{7,9},{8,6},{9,7},{10,... | collective-permute-start | bytes 786440 | tf_op jit(solution)/shard_map/ppermute | solution.py:601
  36.9 8.2 %collective-permute-start.6 = (f32[64,1024]{1,0:T(8,128)S(1)}, f32[64,1024]{1,0:T(8,128)S(1)}, u32[]{:S(2)}, u32[]{:S(2)}) collective-permute-start(f32[64,1024]{1,0:T(8,128)S(1)} %get-tuple-element.59.refs_7_.refs_5_), channel_id=1, source_target_pairs={{0,2},{1,3},{2,0},{3,1},{4,6},{5,7},{6,4},{7,5},{8,10},{9,11},{10,... | collective-permute-start | bytes 786440 | tf_op jit(solution)/shard_map/ppermute | solution.py:601
  36.9 11.0 %collective-permute-start.10 = (f32[64,1024]{1,0:T(8,128)S(1)}, f32[64,1024]{1,0:T(8,128)S(1)}, u32[]{:S(2)}, u32[]{:S(2)}) collective-permute-start(f32[64,1024]{1,0:T(8,128)S(1)} %get-tuple-element.59.refs_7_.refs_5_), channel_id=1, source_target_pairs={{0,31},{1,30},{2,5},{3,4},{4,3},{5,2},{6,9},{7,8},{8,7},{9,6},{10,... | collective-permute-start | bytes 786440 | tf_op jit(solution)/shard_map/ppermute | solution.py:601
  43.3 4.6 %collective-permute-start.9 = (f32[64,1024]{1,0:T(8,128)S(1)}, f32[64,1024]{1,0:T(8,128)S(1)}, u32[]{:S(2)}, u32[]{:S(2)}) collective-permute-start(f32[64,1024]{1,0:T(8,128)S(1)} %collective-permute-done.8.refs_10_.refs_8_), channel_id=1, source_target_pairs={{0,2},{1,3},{2,0},{3,1},{4,6},{5,7},{6,4},{7,5},{8,10},{9,11},{10,... | collective-permute-start | bytes 786440 | tf_op jit(solution)/shard_map/ppermute | solution.py:601
  58.0 10.7 %collective-permute-start.12 = (f32[384,256]{1,0:T(8,128)S(1)}, f32[384,256]{1,0:T(8,128)S(1)}, u32[]{:S(2)}, u32[]{:S(2)}) collective-permute-start(f32[384,256]{1,0:T(8,128)S(1)} %get-tuple-element.80), channel_id=1, source_target_pairs={{0,1},{1,0},{2,3},{3,2},{4,5},{5,4},{6,7},{7,6},{8,9},{9,8},{10,11... | collective-permute-start | bytes 1179656 | tf_op jit(solution)/shard_map/ppermute | solution.py:601
  59.5 12.0 %collective-permute-start.11 = (f32[128,256]{1,0:T(8,128)S(1)}, f32[128,256]{1,0:T(8,128)S(1)}, u32[]{:S(2)}, u32[]{:S(2)}) collective-permute-start(f32[128,256]{1,0:T(8,128)S(1)} %get-tuple-element.79), channel_id=1, source_target_pairs={{0,1},{1,0},{2,3},{3,2},{4,5},{5,4},{6,7},{7,6},{8,9},{9,8},{10,11... | collective-permute-start | bytes 393224 | tf_op jit(solution)/shard_map/ppermute | solution.py:601

commit v4 on v2

--- a/solution.py
+++ b/solution.py
@@ -131,8 +131,11 @@
         flat[i : i + 1, 0:per_patch] = values_ref[pl.ds(patch, 1), batch, :]
         noise = var_ref[pl.ds(patch, 1), batch, :] * widening.astype(F32)
         flat[blocks + i : blocks + i + 1, 0:per_patch] = noise
-    upright = jnp.transpose(flat[...])[0:per_patch]
-    return [(upright[:, i : i + 1], upright[:, blocks + i : blocks + i + 1]) for i in range(blocks)]
+    return jnp.transpose(flat[...])[0:per_patch]
+
+
+def column_of(upright, i, blocks):
+    return upright[:, i : i + 1], upright[:, blocks + i : blocks + i + 1]
 
 
 def scale_block(i, piece, sources, column, members, sh_ref, sl_ref, d_ref):
@@ -153,14 +156,16 @@
 def prepare_kernel(pieces, batch, members, patches_of, places, crossing, *refs):
     place_refs, refs = refs[:places], refs[places:]
     near_ref, values_ref, var_ref, *refs = refs
-    refs, flat = refs[:-1], refs[-1]
+    refs, (upright_ref, flat) = refs[:-2], refs[-2:]
     if crossing:
         (ah_ref, al_ref, *refs), cross_ref = refs[:-1], refs[-1]
     sources, (sh_ref, sl_ref, d_ref, g_ref) = refs[:-4], refs[-4:]
     patches, own = patches_of(*place_refs)
-    columns = table(patches[: len(pieces)], own, near_ref, values_ref, var_ref, batch, flat)
+    upright = table(patches, own, near_ref, values_ref, var_ref, batch, flat)
+    upright_ref[...] = upright
     for i, piece in enumerate(pieces):
-        scale_block(i, piece, sources, columns[i], members, sh_ref, sl_ref, d_ref)
+        column = column_of(upright, i, len(patches))
+        scale_block(i, piece, sources, column, members, sh_ref, sl_ref, d_ref)
     count = len(pieces) * values_ref.shape[2]
     s = (sh_ref[0:count], sl_ref[0:count])
     g_ref[0:count, 0:count] = dot3(s, s, NT)
@@ -169,8 +174,11 @@
 
 
 def factor_kernel(pieces, batch, members, chunk, patches_of, places, ready, crossing, *refs):
-    place_refs, refs = refs[:places], refs[places:]
-    near_ref, values_ref, var_ref, *refs = refs
+    if ready:
+        upright_ref, *refs = refs
+    else:
+        place_refs, refs = refs[:places], refs[places:]
+        near_ref, values_ref, var_ref, *refs = refs
     refs, (flat, eye_ref, x_ref, wa, wb) = refs[:-5], refs[-5:]
     if crossing:
         refs, cross_ref = refs[:-1], refs[-1]
@@ -180,12 +188,16 @@
     elif ready:
         refs = refs[:-4]
     sources = refs
-    per_patch = values_ref.shape[2]
     blocks = len(pieces)
-    patches, own = patches_of(*place_refs)
-    columns = table(patches[ready:], own, near_ref, values_ref, var_ref, batch, flat)
+    if ready:
+        upright = upright_ref[...]
+    else:
+        patches, own = patches_of(*place_refs)
+        upright = table(patches, own, near_ref, values_ref, var_ref, batch, flat)
+    per_patch = upright.shape[0]
     for i in range(ready, blocks):
-        scale_block(i, pieces[i], sources, columns[i - ready], members, sh_ref, sl_ref, d_ref)
+        column = column_of(upright, i, blocks)
+        scale_block(i, pieces[i], sources, column, members, sh_ref, sl_ref, d_ref)
     n = sh_ref.shape[0]
     head = min(TILE, n)
     tail = n - head
@@ -217,9 +229,7 @@
     rho2 = rho * rho
     weight = 2.0 / (2.0 - rho2)
     keep = 0.5 * rho2 * weight
-    r = (1.0 - first) * eye - first * g
-    parts = split(r)
-    x = (weight * first) * (eye + r)
+    x = (weight * first * (2.0 - first)) * eye - (weight * first * first) * g
     x_ref[...] = x
     for i, part in enumerate(split(x)):
         wa[i, :, n : 2 * n] = part
@@ -236,9 +246,15 @@
         left = weight * left - keep * eye_ref[:, 0:head]
         return left, weight * corner - keep * eye_ref[head:n, head:n]
 
-    left = dot3(parts, [part[:, 0:head] for part in parts])
-    corner = dot3([part[head:n] for part in parts], [part[:, head:n] for part in parts])
-    store((wa.at[0], wa.at[1]), 0, *corner_of(weight, keep, left, corner))
+    parts = split(g)
+    square_left = dot3(parts, [part[:, 0:head] for part in parts])
+    square_corner = dot3([part[head:n] for part in parts], [part[:, head:n] for part in parts])
+    two = weight * first * first
+    one = -2.0 * weight * first * (1.0 - first)
+    none = weight * (1.0 - first) * (1.0 - first) - keep
+    left = two * square_left + one * g[:, 0:head] + none * eye[:, 0:head]
+    corner = two * square_corner + one * g[head:n, head:n] + none * eye[head:n, head:n]
+    store((wa.at[0], wa.at[1]), 0, left, corner)
 
     def corners_of(source):
         ends = [jnp.concatenate([source[i, :, head:n], source[i, :, n + head : 2 * n]], axis=1) for i in (0, 1)]
@@ -494,6 +510,7 @@
     ]
     if anomaly:
         outs.append(((n, width), F32, VMEM))
+    outs.append(((values.shape[2], 128), F32, VMEM))
     kernel = functools.partial(
         prepare_kernel, pieces, batch, members, patches_of, len(place), bool(anomaly)
     )
@@ -514,7 +531,13 @@
         ((n, n), BF16, VMEM),
         ((1,), jnp.int32, SMEM),
     ]
-    args = [*place, near, values, var, *sources, *before]
+    if ready:
+        *before, upright = before
+        args = [upright, *sources, *before]
+        ins = [VMEM] * len(args)
+    else:
+        args = [*place, near, values, var, *sources]
+        ins = [SMEM] * (len(place) + 1) + [VMEM] * (2 + len(sources))
     aliases = {}
     crossing = len(before) > 4
     if crossing:
@@ -535,7 +558,6 @@
         factor_kernel, pieces, batch, members, chunk, patches_of, len(place), ready, crossing
     )
     flops = 6 * n * n * members + 60 * n * n * n
-    ins = [SMEM] * (len(place) + 1) + [VMEM] * (len(args) - len(place) - 1)
     return call(kernel, outs, ins, args, scratch, flops, FACTOR_LIMIT, aliases)
 
 

time: 71.9 us -> 70.8 us (0.985)
  Pallas kernels: 29.1 us -> 27 us
  waiting for transfers between devices: 20.2 us -> 21.5 us
    pallas_call x13, Pallas kernels: 29.1 us -> 27 us  [call(): pl.pallas_call(kernel, out_shape=shapes, in_specs=ins, out_specs=[space f...]
    ppermute x13, waiting for transfers between devices: 20.2 us -> 21.5 us  [permute(): return lax.ppermute(x, BOTH, table)]
  transfers between devices with their start and end apart: 13 -> 13, of which waited for: 8 -> 8; matrix products, arithmetic and copies ran while one was open for 0% -> 0% of each run, Pallas kernels for 19% -> 18%
where the time goes in v4:
time: 70.8 us; the launch traced here: 69.9 us
  Pallas kernels  27 us (38%)
  waiting for transfers between devices  21.5 us (30%)
  starting transfers between devices  19.7 us (28%)
  local copies, waits for them, and re-layouts  1.41 us (2%)
    pallas_call x13, Pallas kernels, call(): pl.pallas_call(kernel, out_shape=shapes, in_specs=ins, out_specs=[space f...  27 us
    ppermute x13, waiting for transfers between devices, permute(): return lax.ppermute(x, BOTH, table)  21.5 us
    ppermute x13, starting transfers between devices, permute(): return lax.ppermute(x, BOTH, table)  19.7 us
  transfers between devices with their start and end apart: 13, of which 8 were waited for; matrix products, arithmetic and copies ran while one was open for 0% of the time, Pallas kernels for 18%

profile of v4, /device:TPU:0, one launch (start us, length us, event | category | flops | bytes accessed | tf_op | source)
XLA Modules:
  0.0 69.9 jit_solution(11116182883598883120)
XLA Ops:
  0.0 1.2 %copy-done = f32[512,2,256]{2,1,0:T(2,128)S(1)} copy-done((f32[512,2,256]{2,1,0:T(2,128)S(1)}, f32[512,2,256]{2,1,0:T(2,128)}, u32[]{:S(2)}) %copy-start) | copy-done | bytes 1048600
  1.2 0.6 shard_map.55
  1.8 0.2 copy-done.1
  2.0 0.6 shard_map.56.refs_5_.refs_1_
  2.6 3.0 %collective-permute-start = (f32[2,64,512]{2,1,0:T(8,128)S(1)}, f32[2,64,512]{2,1,0:T(8,128)S(1)}, u32[]{:S(2)}, u32[]{:S(2)}) collective-permute-start(f32[2,64,512]{2,1,0:T(8,128)S(1)} %shard_map.56.refs_5_.refs_1_), channel_id=1, source_target_pairs={{0,1},{1,0},{2,3},{3,2},{4,5},{5,4},{6,7},{7,6},{8,9},{9,8},{10,11... | collective-permute-start | bytes 786440 | tf_op jit(solution)/shard_map/ppermute | solution.py:618
  5.6 3.7 %collective-permute-start.2 = (f32[2,64,512]{2,1,0:T(8,128)S(1)}, f32[2,64,512]{2,1,0:T(8,128)S(1)}, u32[]{:S(2)}, u32[]{:S(2)}) collective-permute-start(f32[2,64,512]{2,1,0:T(8,128)S(1)} %shard_map.56.refs_5_.refs_1_), channel_id=1, source_target_pairs={{0,30},{1,31},{2,4},{3,5},{4,2},{5,3},{6,8},{7,9},{8,6},{9,7},{10,... | collective-permute-start | bytes 786440 | tf_op jit(solution)/shard_map/ppermute | solution.py:618
  9.3 2.6 %collective-permute-done.after_ref.refs_6_.refs_4_ = f32[2,64,512]{2,1,0:T(8,128)S(1)} collective-permute-done((f32[2,64,512]{2,1,0:T(8,128)S(1)}, f32[2,64,512]{2,1,0:T(8,128)S(1)}, u32[]{:S(2)}, u32[]{:S(2)}) %collective-permute-start) | collective-permute-done | bytes 262176 | tf_op jit(solution)/shard_map/ppermute | solution.py:618
  11.9 3.3 %collective-permute-start.4 = (f32[2,64,512]{2,1,0:T(8,128)S(1)}, f32[2,64,512]{2,1,0:T(8,128)S(1)}, u32[]{:S(2)}, u32[]{:S(2)}) collective-permute-start(f32[2,64,512]{2,1,0:T(8,128)S(1)} %collective-permute-done.after_ref.refs_6_.refs_4_), channel_id=1, source_target_pairs={{0,30},{1,31},{2,4},{3,5},{4,2},{5,3},{6,8},{7,9},{8,6},{9,7},{10,... | collective-permute-start | bytes 786440 | tf_op jit(solution)/shard_map/ppermute | solution.py:618
  15.3 0.1 shard_map.57
  15.4 1.6 %collective-permute-start.5 = (f32[512,256]{1,0:T(8,128)S(1)}, f32[512,256]{1,0:T(8,128)S(1)}, u32[]{:S(2)}, u32[]{:S(2)}) collective-permute-start(f32[512,256]{1,0:T(8,128)S(1)} %get-tuple-element.61), channel_id=1, source_target_pairs={{0,1},{1,0},{2,3},{3,2},{4,5},{5,4},{6,7},{7,6},{8,9},{9,8},{10,11... | collective-permute-start | bytes 1572872 | tf_op jit(solution)/shard_map/ppermute | solution.py:618
  17.0 1.3 %shard_map.58 = (bf16[384,1024]{1,0:T(8,128)(2,1)S(1)}, bf16[384,1024]{1,0:T(8,128)(2,1)S(1)}, f32[384,128]{1,0:T(8,128)S(1)}, f32[384,384]{1,0:T(8,128)S(1)}, f32[64,128]{1,0:T(8,128)S(1)}) custom-call(s32[1]{0:T(128)} %bitcast.1.region_ref.refs_0_, s32[1]{0:T(128)} %bitcast.column_ref.refs_1_, s32[5,32]{1,0:T(8,128)S(1)} %bitcast.3, ...), custom_call_target="tpu_custom_call" | custom-call | flops 301989888 | bytes 2949768 | tf_op jit(solution)/shard_map/pallas_call | solution.py:31
  18.3 2.2 %collective-permute-done.4.refs_6_ = f32[2,64,512]{2,1,0:T(8,128)S(1)} collective-permute-done((f32[2,64,512]{2,1,0:T(8,128)S(1)}, f32[2,64,512]{2,1,0:T(8,128)S(1)}, u32[]{:S(2)}, u32[]{:S(2)}) %collective-permute-start.4) | collective-permute-done | bytes 262176 | tf_op jit(solution)/shard_map/ppermute | solution.py:618
  20.5 6.2 %shard_map.59 = (bf16[384,1024]{1,0:T(8,128)(2,1)S(1)}, bf16[384,1024]{1,0:T(8,128)(2,1)S(1)}, f32[384,128]{1,0:T(8,128)S(1)}, f32[384,384]{1,0:T(8,128)S(1)}, b...) custom-call(f32[64,128]{1,0:T(8,128)S(1)} %get-tuple-element.49.refs, ...), custom_call_target="tpu_custom_call", output_to_operand_aliasing={{0}: (7, {}), {1}: (8, {}), {2}: (9, {}), {3}: (10, {})} | custom-call | flops 4303355904 | bytes 6914052 | tf_op jit(solution)/shard_map/pallas_call | solution.py:31
  26.8 3.0 %collective-permute-done.5.refs_3_.refs_1_ = f32[512,256]{1,0:T(8,128)S(1)} collective-permute-done((f32[512,256]{1,0:T(8,128)S(1)}, f32[512,256]{1,0:T(8,128)S(1)}, u32[]{:S(2)}, u32[]{:S(2)}) %collective-permute-start.5) | collective-permute-done | bytes 524320 | tf_op jit(solution)/shard_map/ppermute | solution.py:618
  29.8 4.1 %shard_map.60 = (f32[384,256]{1,0:T(8,128)S(1)}, f32[64,1024]{1,0:T(8,128)S(1)}) custom-call(s32[1]{0:T(128)} %bitcast.1.region_ref.refs_0_, s32[1]{0:T(128)} %bitcast.column_ref.refs_1_, s32[1]{0:T(128)} %get-tuple-element.57.n_ref, s32[32,2,64]{2,1,0:T(2,128)S(1)} %copy-done.1, bf16[384,1024]{1,0:T(8,128)(2,1)S(1)} %get-tuple-element.54.sh_ref, ...), custom_call_target="tpu_custom_call" | custom-call | flops 805306368 | bytes 4669452 | tf_op jit(solution)/shard_map/pallas_call | solution.py:31
  33.9 1.6 %collective-permute-start.8 = (f32[64,1024]{1,0:T(8,128)S(1)}, f32[64,1024]{1,0:T(8,128)S(1)}, u32[]{:S(2)}, u32[]{:S(2)}) collective-permute-start(f32[64,1024]{1,0:T(8,128)S(1)} %get-tuple-element.65.refs_7_.refs_1_), channel_id=1, source_target_pairs={{0,1},{1,0},{2,3},{3,2},{4,5},{5,4},{6,7},{7,6},{8,9},{9,8},{10,11... | collective-permute-start | bytes 786440 | tf_op jit(solution)/shard_map/ppermute | solution.py:618
  35.5 0.1 collective-permute-start.7
  35.6 4.2 %collective-permute-start.10 = (f32[64,1024]{1,0:T(8,128)S(1)}, f32[64,1024]{1,0:T(8,128)S(1)}, u32[]{:S(2)}, u32[]{:S(2)}) collective-permute-start(f32[64,1024]{1,0:T(8,128)S(1)} %get-tuple-element.65.refs_7_.refs_1_), channel_id=1, source_target_pairs={{0,31},{1,30},{2,5},{3,4},{4,3},{5,2},{6,9},{7,8},{8,7},{9,6},{10,... | collective-permute-start | bytes 786440 | tf_op jit(solution)/shard_map/ppermute | solution.py:618
  39.9 2.4 %collective-permute-done.8.refs_10_.refs_4_ = f32[64,1024]{1,0:T(8,128)S(1)} collective-permute-done((f32[64,1024]{1,0:T(8,128)S(1)}, f32[64,1024]{1,0:T(8,128)S(1)}, u32[]{:S(2)}, u32[]{:S(2)}) %collective-permute-start.8) | collective-permute-done | bytes 262176 | tf_op jit(solution)/shard_map/ppermute | solution.py:618
  42.3 1.2 %shard_map.61 = (f32[512,256]{1,0:T(8,128)S(1)}, f32[512,256]{1,0:T(8,128)S(1)}, bf16[1024,256]{1,0:T(8,128)(2,1)S(1)}, bf16[1024,256]{1,0:T(8,128)(2,1)S(1)}) custom-call(bf16[384,1024]{1,0:T(8,128)(2,1)S(1)} %get-tuple-element.54.sh_ref, bf16[384,1024]{1,0:T(8,128)(2,1)S(1)} %get-tuple-element.55.sl_ref, f32[384,128]{1,0:T(8,128)S(1)} %get-tuple-element.56.d_ref, ...), custom_call_target="tpu_custom_call" | custom-call | flops 603979776 | bytes 5308416 | tf_op jit(solution)/shard_map/pallas_call | solution.py:31
  43.5 0.6 collective-permute-done.7.refs_9_.refs_3_
  44.1 2.1 %shard_map.62 = (bf16[384,1024]{1,0:T(8,128)(2,1)S(1)}, bf16[384,1024]{1,0:T(8,128)(2,1)S(1)}, f32[384,128]{1,0:T(8,128)S(1)}, f32[384,384]{1,0:T(8,128)S(1)}, f...) custom-call(s32[1]{0:T(128)} %bitcast.1.region_ref.refs_0_, s32[1]{0:T(128)} %bitcast.column_ref.refs_1_, ...), custom_call_target="tpu_custom_call" | custom-call | flops 905969664 | bytes 4915848 | tf_op jit(solution)/shard_map/pallas_call | solution.py:31
  46.2 0.7 collective-permute-done.10.refs_6_
  46.8 5.8 %shard_map.63 = (bf16[384,1024]{1,0:T(8,128)(2,1)S(1)}, bf16[384,1024]{1,0:T(8,128)(2,1)S(1)}, f32[384,128]{1,0:T(8,128)S(1)}, f32[384,384]{1,0:T(8,128)S(1)}, b...) custom-call(f32[64,128]{1,0:T(8,128)S(1)} %get-tuple-element.66.refs, ...), custom_call_target="tpu_custom_call", output_to_operand_aliasing={{0}: (9, {}), {1}: (10, {}), {2}: (11, {}), {3}: (12, {}), ... | custom-call | flops 4303355904 | bytes 8749060 | tf_op jit(solution)/shard_map/pallas_call | solution.py:31
  52.6 2.6 %shard_map.64 = (f32[384,256]{1,0:T(8,128)S(1)}, f32[256,256]{1,0:T(8,128)S(1)}, f32[256,256]{1,0:T(8,128)S(1)}) custom-call(s32[1]{0:T(128)} %get-tuple-element.75.n_ref, bf16[384,1024]{1,0:T(8,128)(2,1)S(1)} %get-tuple-element.72.sh_ref, bf16[384,1024]{1,0:T(8,128)(2,1)S(1)} %get-tuple-element.73.sl_ref, f32[384,128]{1,0:T(8,128)S(1)} %get-tuple-element.74.d_ref, ...), custom_call_target="tpu_custom_call" | custom-call | flops 1207959552 | bytes 4784132 | tf_op jit(solution)/shard_map/pallas_call | solution.py:31
  55.3 1.6 %collective-permute-start.12 = (f32[256,256]{1,0:T(8,128)S(1)}, f32[256,256]{1,0:T(8,128)S(1)}, u32[]{:S(2)}, u32[]{:S(2)}) collective-permute-start(f32[256,256]{1,0:T(8,128)S(1)} %get-tuple-element.84), channel_id=1, source_target_pairs={{0,1},{1,0},{2,3},{3,2},{4,5},{5,4},{6,7},{7,6},{8,9},{9,8},{10,11... | collective-permute-start | bytes 786440 | tf_op jit(solution)/shard_map/ppermute | solution.py:618
  56.9 0.5 collective-permute-start.11
  57.4 0.6 shard_map.65.mine_ref
  57.9 5.3 %collective-permute-done.12.theirs_ref = f32[256,256]{1,0:T(8,128)S(1)} collective-permute-done((f32[256,256]{1,0:T(8,128)S(1)}, f32[256,256]{1,0:T(8,128)S(1)}, u32[]{:S(2)}, u32[]{:S(2)}) %collective-permute-start.12) | collective-permute-done | bytes 262176 | tf_op jit(solution)/shard_map/ppermute | solution.py:618
  63.2 0.9 %shard_map.66.refs_0_ = f32[512,2,256]{2,1,0:T(2,128)} custom-call(s32[1]{0:T(128)} %bitcast.column_ref.refs_1_, f32[512,256]{1,0:T(8,128)S(1)} %shard_map.65.mine_ref, f32[256,256]{1,0:T(8,128)S(1)} %collective-permute-done.12.theirs_ref), custom_call_target="tpu_custom_call" | custom-call | bytes 1835012 | tf_op jit(solution)/shard_map/pallas_call | solution.py:31
  64.1 4.7 %collective-permute-done.11.theirs_ref = f32[256,256]{1,0:T(8,128)S(1)} collective-permute-done((f32[256,256]{1,0:T(8,128)S(1)}, f32[256,256]{1,0:T(8,128)S(1)}, u32[]{:S(2)}, u32[]{:S(2)}) %collective-permute-start.11) | collective-permute-done | bytes 262176 | tf_op jit(solution)/shard_map/ppermute | solution.py:618
  68.8 0.9 %shard_map.67 = f32[512,2,256]{2,1,0:T(2,128)} custom-call(s32[1]{0:T(128)} %bitcast.column_ref.refs_1_, f32[512,256]{1,0:T(8,128)S(1)} %shard_map.65.mine_ref, f32[256,256]{1,0:T(8,128)S(1)} %collective-permute-done.11.theirs_ref, f32[512,2,256]{2,1,0:T(2,128)} %shard_map.66.refs_0_), custom_call_target="tpu_custom_call", output_to_operand_aliasing={{}: (3, {})} | custom-call | bytes 2883588 | tf_op jit(solution)/shard_map/pallas_call | solution.py:31
  (17 shorter events, 0.0 us)
Async XLA Ops:
  0.0 1.2 %copy-start = (f32[512,2,256]{2,1,0:T(2,128)S(1)}, f32[512,2,256]{2,1,0:T(2,128)}, u32[]{:S(2)}) copy-start(f32[512,2,256]{2,1,0:T(2,128)} %state_ref.1) | copy-start | bytes 3145732
  1.2 0.8 %copy-start.1 = (s32[32,2,64]{2,1,0:T(2,128)S(1)}, s32[32,2,64]{2,1,0:T(2,128)}, u32[]{:S(2)}) copy-start(s32[32,2,64]{2,1,0:T(2,128)} %cells_ref.3) | copy-start | bytes 49156
  2.0 13.3 %copy-start.2 = (f32[32,2,64]{2,1,0:T(2,128)S(1)}, f32[32,2,64]{2,1,0:T(2,128)}, u32[]{:S(2)}) copy-start(f32[32,2,64]{2,1,0:T(2,128)} %values_hbm.1) | copy-start | bytes 49156
  2.0 13.3 %copy-start.3 = (f32[32,2,64]{2,1,0:T(2,128)S(1)}, f32[32,2,64]{2,1,0:T(2,128)}, u32[]{:S(2)}) copy-start(f32[32,2,64]{2,1,0:T(2,128)} %var_hbm.1) | copy-start | bytes 49156
  2.6 9.3 %collective-permute-start = (f32[2,64,512]{2,1,0:T(8,128)S(1)}, f32[2,64,512]{2,1,0:T(8,128)S(1)}, u32[]{:S(2)}, u32[]{:S(2)}) collective-permute-start(f32[2,64,512]{2,1,0:T(8,128)S(1)} %shard_map.56.refs_5_.refs_1_), channel_id=1, source_target_pairs={{0,1},{1,0},{2,3},{3,2},{4,5},{5,4},{6,7},{7,6},{8,9},{9,8},{10,11... | collective-permute-start | bytes 786440 | tf_op jit(solution)/shard_map/ppermute | solution.py:618
  5.6 12.7 %collective-permute-start.2 = (f32[2,64,512]{2,1,0:T(8,128)S(1)}, f32[2,64,512]{2,1,0:T(8,128)S(1)}, u32[]{:S(2)}, u32[]{:S(2)}) collective-permute-start(f32[2,64,512]{2,1,0:T(8,128)S(1)} %shard_map.56.refs_5_.refs_1_), channel_id=1, source_target_pairs={{0,30},{1,31},{2,4},{3,5},{4,2},{5,3},{6,8},{7,9},{8,6},{9,7},{10,... | collective-permute-start | bytes 786440 | tf_op jit(solution)/shard_map/ppermute | solution.py:618
  9.3 9.0 %collective-permute-start.1 = (f32[2,64,512]{2,1,0:T(8,128)S(1)}, f32[2,64,512]{2,1,0:T(8,128)S(1)}, u32[]{:S(2)}, u32[]{:S(2)}) collective-permute-start(f32[2,64,512]{2,1,0:T(8,128)S(1)} %shard_map.56.refs_5_.refs_1_), channel_id=1, source_target_pairs={{0,2},{1,3},{2,0},{3,1},{4,6},{5,7},{6,4},{7,5},{8,10},{9,11},{10,... | collective-permute-start | bytes 786440 | tf_op jit(solution)/shard_map/ppermute | solution.py:618
  11.9 8.6 %collective-permute-start.4 = (f32[2,64,512]{2,1,0:T(8,128)S(1)}, f32[2,64,512]{2,1,0:T(8,128)S(1)}, u32[]{:S(2)}, u32[]{:S(2)}) collective-permute-start(f32[2,64,512]{2,1,0:T(8,128)S(1)} %collective-permute-done.after_ref.refs_6_.refs_4_), channel_id=1, source_target_pairs={{0,30},{1,31},{2,4},{3,5},{4,2},{5,3},{6,8},{7,9},{8,6},{9,7},{10,... | collective-permute-start | bytes 786440 | tf_op jit(solution)/shard_map/ppermute | solution.py:618
  15.3 5.3 %collective-permute-start.3 = (f32[2,64,512]{2,1,0:T(8,128)S(1)}, f32[2,64,512]{2,1,0:T(8,128)S(1)}, u32[]{:S(2)}, u32[]{:S(2)}) collective-permute-start(f32[2,64,512]{2,1,0:T(8,128)S(1)} %collective-permute-done.after_ref.refs_6_.refs_4_), channel_id=1, source_target_pairs={{0,2},{1,3},{2,0},{3,1},{4,6},{5,7},{6,4},{7,5},{8,10},{9,11},{10,... | collective-permute-start | bytes 786440 | tf_op jit(solution)/shard_map/ppermute | solution.py:618
  15.4 1.6 %copy-start.4 = (s32[32,5]{0,1:T(8,128)S(1)}, s32[32,5]{0,1:T(8,128)}, u32[]{:S(2)}) copy-start(s32[32,5]{0,1:T(8,128)} %param.6) | copy-start | bytes 1924
  15.4 14.4 %collective-permute-start.5 = (f32[512,256]{1,0:T(8,128)S(1)}, f32[512,256]{1,0:T(8,128)S(1)}, u32[]{:S(2)}, u32[]{:S(2)}) collective-permute-start(f32[512,256]{1,0:T(8,128)S(1)} %get-tuple-element.61), channel_id=1, source_target_pairs={{0,1},{1,0},{2,3},{3,2},{4,5},{5,4},{6,7},{7,6},{8,9},{9,8},{10,11... | collective-permute-start | bytes 1572872 | tf_op jit(solution)/shard_map/ppermute | solution.py:618
  33.9 8.4 %collective-permute-start.8 = (f32[64,1024]{1,0:T(8,128)S(1)}, f32[64,1024]{1,0:T(8,128)S(1)}, u32[]{:S(2)}, u32[]{:S(2)}) collective-permute-start(f32[64,1024]{1,0:T(8,128)S(1)} %get-tuple-element.65.refs_7_.refs_1_), channel_id=1, source_target_pairs={{0,1},{1,0},{2,3},{3,2},{4,5},{5,4},{6,7},{7,6},{8,9},{9,8},{10,11... | collective-permute-start | bytes 786440 | tf_op jit(solution)/shard_map/ppermute | solution.py:618
  35.5 8.6 %collective-permute-start.7 = (f32[64,1024]{1,0:T(8,128)S(1)}, f32[64,1024]{1,0:T(8,128)S(1)}, u32[]{:S(2)}, u32[]{:S(2)}) collective-permute-start(f32[64,1024]{1,0:T(8,128)S(1)} %get-tuple-element.65.refs_7_.refs_1_), channel_id=1, source_target_pairs={{0,30},{1,31},{2,4},{3,5},{4,2},{5,3},{6,8},{7,9},{8,6},{9,7},{10,... | collective-permute-start | bytes 786440 | tf_op jit(solution)/shard_map/ppermute | solution.py:618
  35.6 8.5 %collective-permute-start.6 = (f32[64,1024]{1,0:T(8,128)S(1)}, f32[64,1024]{1,0:T(8,128)S(1)}, u32[]{:S(2)}, u32[]{:S(2)}) collective-permute-start(f32[64,1024]{1,0:T(8,128)S(1)} %get-tuple-element.65.refs_7_.refs_1_), channel_id=1, source_target_pairs={{0,2},{1,3},{2,0},{3,1},{4,6},{5,7},{6,4},{7,5},{8,10},{9,11},{10,... | collective-permute-start | bytes 786440 | tf_op jit(solution)/shard_map/ppermute | solution.py:618
  35.6 11.2 %collective-permute-start.10 = (f32[64,1024]{1,0:T(8,128)S(1)}, f32[64,1024]{1,0:T(8,128)S(1)}, u32[]{:S(2)}, u32[]{:S(2)}) collective-permute-start(f32[64,1024]{1,0:T(8,128)S(1)} %get-tuple-element.65.refs_7_.refs_1_), channel_id=1, source_target_pairs={{0,31},{1,30},{2,5},{3,4},{4,3},{5,2},{6,9},{7,8},{8,7},{9,6},{10,... | collective-permute-start | bytes 786440 | tf_op jit(solution)/shard_map/ppermute | solution.py:618
  42.3 4.6 %collective-permute-start.9 = (f32[64,1024]{1,0:T(8,128)S(1)}, f32[64,1024]{1,0:T(8,128)S(1)}, u32[]{:S(2)}, u32[]{:S(2)}) collective-permute-start(f32[64,1024]{1,0:T(8,128)S(1)} %collective-permute-done.8.refs_10_.refs_4_), channel_id=1, source_target_pairs={{0,2},{1,3},{2,0},{3,1},{4,6},{5,7},{6,4},{7,5},{8,10},{9,11},{10,... | collective-permute-start | bytes 786440 | tf_op jit(solution)/shard_map/ppermute | solution.py:618
  55.3 7.9 %collective-permute-start.12 = (f32[256,256]{1,0:T(8,128)S(1)}, f32[256,256]{1,0:T(8,128)S(1)}, u32[]{:S(2)}, u32[]{:S(2)}) collective-permute-start(f32[256,256]{1,0:T(8,128)S(1)} %get-tuple-element.84), channel_id=1, source_target_pairs={{0,1},{1,0},{2,3},{3,2},{4,5},{5,4},{6,7},{7,6},{8,9},{9,8},{10,11... | collective-permute-start | bytes 786440 | tf_op jit(solution)/shard_map/ppermute | solution.py:618
  56.9 11.9 %collective-permute-start.11 = (f32[256,256]{1,0:T(8,128)S(1)}, f32[256,256]{1,0:T(8,128)S(1)}, u32[]{:S(2)}, u32[]{:S(2)}) collective-permute-start(f32[256,256]{1,0:T(8,128)S(1)} %get-tuple-element.83), channel_id=1, source_target_pairs={{0,1},{1,0},{2,3},{3,2},{4,5},{5,4},{6,7},{7,6},{8,9},{9,8},{10,11... | collective-permute-start | bytes 786440 | tf_op jit(solution)/shard_map/ppermute | solution.py:618

commit v5 on v4

--- a/solution.py
+++ b/solution.py
@@ -557,7 +557,7 @@
     kernel = functools.partial(
         factor_kernel, pieces, batch, members, chunk, patches_of, len(place), ready, crossing
     )
-    flops = 6 * n * n * members + 60 * n * n * n
+    flops = 6 * n * n * members + (30 if crossing else 20) * n * n * n
     return call(kernel, outs, ins, args, scratch, flops, FACTOR_LIMIT, aliases)
 
 
@@ -666,7 +666,7 @@
         gate_kernel,
         [((half, cells), F32, anywhere), (obs_values.shape, F32, VMEM), (obs_var.shape, F32, VMEM)],
         [anywhere] * 4,
-        [obs_values, obs_var, send, other],
+        [obs_values, obs_var, send, rows],
         [pltpu.SemaphoreType.DMA((2,))],
         aliases={2: 0},
     )

time: 70.8 us -> 69 us (0.975)
  the two profiles are of different devices: /device:TPU:0 before, /device:TPU:1 now
where the time goes in v5:
time: 69 us; the launch traced here: 68.7 us
  Pallas kernels  27 us (39%)
  waiting for transfers between devices  22.6 us (33%)
  starting transfers between devices  17.5 us (25%)
  local copies, waits for them, and re-layouts  1.41 us (2%)
    pallas_call x13, Pallas kernels, call(): pl.pallas_call(kernel, out_shape=shapes, in_specs=ins, out_specs=[space f...  27 us
    ppermute x13, waiting for transfers between devices, permute(): return lax.ppermute(x, BOTH, table)  22.6 us
    ppermute x13, starting transfers between devices, permute(): return lax.ppermute(x, BOTH, table)  17.5 us
    unnamed x10, local copies, waits for them, and re-layouts  1.41 us
  transfers between devices with their start and end apart: 13, of which 7 were waited for; matrix products, arithmetic and copies ran while one was open for 0% of the time, Pallas kernels for 18%

profile of v5, /device:TPU:1, one launch (start us, length us, event | category | flops | bytes accessed | tf_op | source)
XLA Modules:
  0.0 68.7 jit_solution(8518494731883690591)
XLA Ops:
  0.0 1.2 %copy-done = f32[512,2,256]{2,1,0:T(2,128)S(1)} copy-done((f32[512,2,256]{2,1,0:T(2,128)S(1)}, f32[512,2,256]{2,1,0:T(2,128)}, u32[]{:S(2)}) %copy-start) | copy-done | bytes 1048600
  1.2 0.6 shard_map.55
  1.8 0.2 copy-done.1
  2.0 0.6 shard_map.56.after_ref.refs_5_.refs_1_
  2.6 2.1 %collective-permute-start = (f32[2,64,512]{2,1,0:T(8,128)S(1)}, f32[2,64,512]{2,1,0:T(8,128)S(1)}, u32[]{:S(2)}, u32[]{:S(2)}) collective-permute-start(f32[2,64,512]{2,1,0:T(8,128)S(1)} %shard_map.56.after_ref.refs_5_.refs_1_), channel_id=1, source_target_pairs={{0,1},{1,0},{2,3},{3,2},{4,5},{5,4},{6,7},{7,6},{8,9},{9,8},{10,11... | collective-permute-start | bytes 786440 | tf_op jit(solution)/shard_map/ppermute | solution.py:618
  5.0 2.5 %collective-permute-start.2 = (f32[2,64,512]{2,1,0:T(8,128)S(1)}, f32[2,64,512]{2,1,0:T(8,128)S(1)}, u32[]{:S(2)}, u32[]{:S(2)}) collective-permute-start(f32[2,64,512]{2,1,0:T(8,128)S(1)} %shard_map.56.after_ref.refs_5_.refs_1_), channel_id=1, source_target_pairs={{0,30},{1,31},{2,4},{3,5},{4,2},{5,3},{6,8},{7,9},{8,6},{9,7},{10,... | collective-permute-start | bytes 786440 | tf_op jit(solution)/shard_map/ppermute | solution.py:618
  7.5 2.3 %collective-permute-start.1 = (f32[2,64,512]{2,1,0:T(8,128)S(1)}, f32[2,64,512]{2,1,0:T(8,128)S(1)}, u32[]{:S(2)}, u32[]{:S(2)}) collective-permute-start(f32[2,64,512]{2,1,0:T(8,128)S(1)} %shard_map.56.after_ref.refs_5_.refs_1_), channel_id=1, source_target_pairs={{0,2},{1,3},{2,0},{3,1},{4,6},{5,7},{6,4},{7,5},{8,10},{9,11},{10,... | collective-permute-start | bytes 786440 | tf_op jit(solution)/shard_map/ppermute | solution.py:618
  9.8 1.0 %collective-permute-done.refs_6_.refs_4_ = f32[2,64,512]{2,1,0:T(8,128)S(1)} collective-permute-done((f32[2,64,512]{2,1,0:T(8,128)S(1)}, f32[2,64,512]{2,1,0:T(8,128)S(1)}, u32[]{:S(2)}, u32[]{:S(2)}) %collective-permute-start) | collective-permute-done | bytes 262176 | tf_op jit(solution)/shard_map/ppermute | solution.py:618
  10.8 3.7 %collective-permute-start.4 = (f32[2,64,512]{2,1,0:T(8,128)S(1)}, f32[2,64,512]{2,1,0:T(8,128)S(1)}, u32[]{:S(2)}, u32[]{:S(2)}) collective-permute-start(f32[2,64,512]{2,1,0:T(8,128)S(1)} %collective-permute-done.refs_6_.refs_4_), channel_id=1, source_target_pairs={{0,30},{1,31},{2,4},{3,5},{4,2},{5,3},{6,8},{7,9},{8,6},{9,7},{10,... | collective-permute-start | bytes 786440 | tf_op jit(solution)/shard_map/ppermute | solution.py:618
  14.5 0.9 %collective-permute-start.3 = (f32[2,64,512]{2,1,0:T(8,128)S(1)}, f32[2,64,512]{2,1,0:T(8,128)S(1)}, u32[]{:S(2)}, u32[]{:S(2)}) collective-permute-start(f32[2,64,512]{2,1,0:T(8,128)S(1)} %collective-permute-done.refs_6_.refs_4_), channel_id=1, source_target_pairs={{0,2},{1,3},{2,0},{3,1},{4,6},{5,7},{6,4},{7,5},{8,10},{9,11},{10,... | collective-permute-start | bytes 786440 | tf_op jit(solution)/shard_map/ppermute | solution.py:618
  15.3 1.3 %shard_map.58 = (bf16[384,1024]{1,0:T(8,128)(2,1)S(1)}, bf16[384,1024]{1,0:T(8,128)(2,1)S(1)}, f32[384,128]{1,0:T(8,128)S(1)}, f32[384,384]{1,0:T(8,128)S(1)}, f32[64,128]{1,0:T(8,128)S(1)}) custom-call(s32[1]{0:T(128)} %bitcast.1.region_ref.refs_0_, s32[1]{0:T(128)} %bitcast.column_ref.refs_1_, s32[5,32]{1,0:T(8,128)S(1)} %bitcast.3, ...), custom_call_target="tpu_custom_call" | custom-call | flops 301989888 | bytes 2949768 | tf_op jit(solution)/shard_map/pallas_call | solution.py:31
  16.6 5.0 %collective-permute-done.4.refs_6_ = f32[2,64,512]{2,1,0:T(8,128)S(1)} collective-permute-done((f32[2,64,512]{2,1,0:T(8,128)S(1)}, f32[2,64,512]{2,1,0:T(8,128)S(1)}, u32[]{:S(2)}, u32[]{:S(2)}) %collective-permute-start.4) | collective-permute-done | bytes 262176 | tf_op jit(solution)/shard_map/ppermute | solution.py:618
  21.6 6.2 %shard_map.59 = (bf16[384,1024]{1,0:T(8,128)(2,1)S(1)}, bf16[384,1024]{1,0:T(8,128)(2,1)S(1)}, f32[384,128]{1,0:T(8,128)S(1)}, f32[384,384]{1,0:T(8,128)S(1)}, b...) custom-call(f32[64,128]{1,0:T(8,128)S(1)} %get-tuple-element.49.refs, ...), custom_call_target="tpu_custom_call", output_to_operand_aliasing={{0}: (7, {}), {1}: (8, {}), {2}: (9, {}), {3}: (10, {})} | custom-call | flops 2038431744 | bytes 6914052 | tf_op jit(solution)/shard_map/pallas_call | solution.py:31
  27.8 4.1 %shard_map.60 = (f32[384,256]{1,0:T(8,128)S(1)}, f32[64,1024]{1,0:T(8,128)S(1)}) custom-call(s32[1]{0:T(128)} %bitcast.1.region_ref.refs_0_, s32[1]{0:T(128)} %bitcast.column_ref.refs_1_, s32[1]{0:T(128)} %get-tuple-element.57.n_ref, s32[32,2,64]{2,1,0:T(2,128)S(1)} %copy-done.1, bf16[384,1024]{1,0:T(8,128)(2,1)S(1)} %get-tuple-element.54.sh_ref, ...), custom_call_target="tpu_custom_call" | custom-call | flops 805306368 | bytes 4669452 | tf_op jit(solution)/shard_map/pallas_call | solution.py:31
  32.0 1.3 %collective-permute-start.8 = (f32[64,1024]{1,0:T(8,128)S(1)}, f32[64,1024]{1,0:T(8,128)S(1)}, u32[]{:S(2)}, u32[]{:S(2)}) collective-permute-start(f32[64,1024]{1,0:T(8,128)S(1)} %get-tuple-element.65.refs_7_.refs_1_), channel_id=1, source_target_pairs={{0,1},{1,0},{2,3},{3,2},{4,5},{5,4},{6,7},{7,6},{8,9},{9,8},{10,11... | collective-permute-start | bytes 786440 | tf_op jit(solution)/shard_map/ppermute | solution.py:618
  33.3 1.7 %collective-permute-start.7 = (f32[64,1024]{1,0:T(8,128)S(1)}, f32[64,1024]{1,0:T(8,128)S(1)}, u32[]{:S(2)}, u32[]{:S(2)}) collective-permute-start(f32[64,1024]{1,0:T(8,128)S(1)} %get-tuple-element.65.refs_7_.refs_1_), channel_id=1, source_target_pairs={{0,30},{1,31},{2,4},{3,5},{4,2},{5,3},{6,8},{7,9},{8,6},{9,7},{10,... | collective-permute-start | bytes 786440 | tf_op jit(solution)/shard_map/ppermute | solution.py:618
  35.0 0.6 collective-permute-start.6
  35.6 4.5 %collective-permute-done.8.refs_10_.refs_4_ = f32[64,1024]{1,0:T(8,128)S(1)} collective-permute-done((f32[64,1024]{1,0:T(8,128)S(1)}, f32[64,1024]{1,0:T(8,128)S(1)}, u32[]{:S(2)}, u32[]{:S(2)}) %collective-permute-start.8) | collective-permute-done | bytes 262176 | tf_op jit(solution)/shard_map/ppermute | solution.py:618
  40.1 0.7 %collective-permute-start.9 = (f32[64,1024]{1,0:T(8,128)S(1)}, f32[64,1024]{1,0:T(8,128)S(1)}, u32[]{:S(2)}, u32[]{:S(2)}) collective-permute-start(f32[64,1024]{1,0:T(8,128)S(1)} %collective-permute-done.8.refs_10_.refs_4_), channel_id=1, source_target_pairs={{0,2},{1,3},{2,0},{3,1},{4,6},{5,7},{6,4},{7,5},{8,10},{9,11},{10,... | collective-permute-start | bytes 786440 | tf_op jit(solution)/shard_map/ppermute | solution.py:618
  40.8 1.2 %shard_map.61 = (f32[512,256]{1,0:T(8,128)S(1)}, f32[512,256]{1,0:T(8,128)S(1)}, bf16[1024,256]{1,0:T(8,128)(2,1)S(1)}, bf16[1024,256]{1,0:T(8,128)(2,1)S(1)}) custom-call(bf16[384,1024]{1,0:T(8,128)(2,1)S(1)} %get-tuple-element.54.sh_ref, bf16[384,1024]{1,0:T(8,128)(2,1)S(1)} %get-tuple-element.55.sl_ref, f32[384,128]{1,0:T(8,128)S(1)} %get-tuple-element.56.d_ref, ...), custom_call_target="tpu_custom_call" | custom-call | flops 603979776 | bytes 5308416 | tf_op jit(solution)/shard_map/pallas_call | solution.py:31
  42.0 2.7 %collective-permute-done.7.refs_9_.refs_3_ = f32[64,1024]{1,0:T(8,128)S(1)} collective-permute-done((f32[64,1024]{1,0:T(8,128)S(1)}, f32[64,1024]{1,0:T(8,128)S(1)}, u32[]{:S(2)}, u32[]{:S(2)}) %collective-permute-start.7) | collective-permute-done | bytes 262176 | tf_op jit(solution)/shard_map/ppermute | solution.py:618
  44.7 2.1 %shard_map.62 = (bf16[384,1024]{1,0:T(8,128)(2,1)S(1)}, bf16[384,1024]{1,0:T(8,128)(2,1)S(1)}, f32[384,128]{1,0:T(8,128)S(1)}, f32[384,384]{1,0:T(8,128)S(1)}, f...) custom-call(s32[1]{0:T(128)} %bitcast.1.region_ref.refs_0_, s32[1]{0:T(128)} %bitcast.column_ref.refs_1_, ...), custom_call_target="tpu_custom_call" | custom-call | flops 905969664 | bytes 4915848 | tf_op jit(solution)/shard_map/pallas_call | solution.py:31
  46.8 0.7 %collective-permute-done.10.refs_6_ = f32[64,1024]{1,0:T(8,128)S(1)} collective-permute-done((f32[64,1024]{1,0:T(8,128)S(1)}, f32[64,1024]{1,0:T(8,128)S(1)}, u32[]{:S(2)}, u32[]{:S(2)}) %collective-permute-start.10) | collective-permute-done | bytes 262176 | tf_op jit(solution)/shard_map/ppermute | solution.py:618
  47.4 5.8 %shard_map.63 = (bf16[384,1024]{1,0:T(8,128)(2,1)S(1)}, bf16[384,1024]{1,0:T(8,128)(2,1)S(1)}, f32[384,128]{1,0:T(8,128)S(1)}, f32[384,384]{1,0:T(8,128)S(1)}, b...) custom-call(f32[64,128]{1,0:T(8,128)S(1)} %get-tuple-element.66.refs, ...), custom_call_target="tpu_custom_call", output_to_operand_aliasing={{0}: (9, {}), {1}: (10, {}), {2}: (11, {}), {3}: (12, {}), ... | custom-call | flops 2604662784 | bytes 8749060 | tf_op jit(solution)/shard_map/pallas_call | solution.py:31
  53.2 2.6 %shard_map.64 = (f32[384,256]{1,0:T(8,128)S(1)}, f32[256,256]{1,0:T(8,128)S(1)}, f32[256,256]{1,0:T(8,128)S(1)}) custom-call(s32[1]{0:T(128)} %get-tuple-element.75.n_ref, bf16[384,1024]{1,0:T(8,128)(2,1)S(1)} %get-tuple-element.72.sh_ref, bf16[384,1024]{1,0:T(8,128)(2,1)S(1)} %get-tuple-element.73.sl_ref, f32[384,128]{1,0:T(8,128)S(1)} %get-tuple-element.74.d_ref, ...), custom_call_target="tpu_custom_call" | custom-call | flops 1207959552 | bytes 4784132 | tf_op jit(solution)/shard_map/pallas_call | solution.py:31
  55.9 1.3 %collective-permute-start.12 = (f32[256,256]{1,0:T(8,128)S(1)}, f32[256,256]{1,0:T(8,128)S(1)}, u32[]{:S(2)}, u32[]{:S(2)}) collective-permute-start(f32[256,256]{1,0:T(8,128)S(1)} %get-tuple-element.84), channel_id=1, source_target_pairs={{0,1},{1,0},{2,3},{3,2},{4,5},{5,4},{6,7},{7,6},{8,9},{9,8},{10,11... | collective-permute-start | bytes 786440 | tf_op jit(solution)/shard_map/ppermute | solution.py:618
  57.2 0.2 collective-permute-start.11
  57.4 0.6 shard_map.65.mine_ref
  58.0 6.4 %collective-permute-done.12.theirs_ref = f32[256,256]{1,0:T(8,128)S(1)} collective-permute-done((f32[256,256]{1,0:T(8,128)S(1)}, f32[256,256]{1,0:T(8,128)S(1)}, u32[]{:S(2)}, u32[]{:S(2)}) %collective-permute-start.12) | collective-permute-done | bytes 262176 | tf_op jit(solution)/shard_map/ppermute | solution.py:618
  64.3 0.9 %shard_map.66.refs_0_ = f32[512,2,256]{2,1,0:T(2,128)} custom-call(s32[1]{0:T(128)} %bitcast.column_ref.refs_1_, f32[512,256]{1,0:T(8,128)S(1)} %shard_map.65.mine_ref, f32[256,256]{1,0:T(8,128)S(1)} %collective-permute-done.12.theirs_ref), custom_call_target="tpu_custom_call" | custom-call | bytes 1835012 | tf_op jit(solution)/shard_map/pallas_call | solution.py:31
  65.2 2.4 %collective-permute-done.11.theirs_ref = f32[256,256]{1,0:T(8,128)S(1)} collective-permute-done((f32[256,256]{1,0:T(8,128)S(1)}, f32[256,256]{1,0:T(8,128)S(1)}, u32[]{:S(2)}, u32[]{:S(2)}) %collective-permute-start.11) | collective-permute-done | bytes 262176 | tf_op jit(solution)/shard_map/ppermute | solution.py:618
  67.7 0.9 %shard_map.67 = f32[512,2,256]{2,1,0:T(2,128)} custom-call(s32[1]{0:T(128)} %bitcast.column_ref.refs_1_, f32[512,256]{1,0:T(8,128)S(1)} %shard_map.65.mine_ref, f32[256,256]{1,0:T(8,128)S(1)} %collective-permute-done.11.theirs_ref, f32[512,2,256]{2,1,0:T(2,128)} %shard_map.66.refs_0_), custom_call_target="tpu_custom_call", output_to_operand_aliasing={{}: (3, {})} | custom-call | bytes 2883588 | tf_op jit(solution)/shard_map/pallas_call | solution.py:31
  (17 shorter events, 0.3 us)
Async XLA Ops:
  0.0 1.2 %copy-start = (f32[512,2,256]{2,1,0:T(2,128)S(1)}, f32[512,2,256]{2,1,0:T(2,128)}, u32[]{:S(2)}) copy-start(f32[512,2,256]{2,1,0:T(2,128)} %state_ref.1) | copy-start | bytes 3145732
  1.2 0.8 %copy-start.1 = (s32[32,2,64]{2,1,0:T(2,128)S(1)}, s32[32,2,64]{2,1,0:T(2,128)}, u32[]{:S(2)}) copy-start(s32[32,2,64]{2,1,0:T(2,128)} %cells_ref.3) | copy-start | bytes 49156
  2.0 2.8 %copy-start.2 = (f32[32,2,64]{2,1,0:T(2,128)S(1)}, f32[32,2,64]{2,1,0:T(2,128)}, u32[]{:S(2)}) copy-start(f32[32,2,64]{2,1,0:T(2,128)} %values_hbm.1) | copy-start | bytes 49156
  2.0 2.8 %copy-start.3 = (f32[32,2,64]{2,1,0:T(2,128)S(1)}, f32[32,2,64]{2,1,0:T(2,128)}, u32[]{:S(2)}) copy-start(f32[32,2,64]{2,1,0:T(2,128)} %var_hbm.1) | copy-start | bytes 49156
  2.6 8.2 %collective-permute-start = (f32[2,64,512]{2,1,0:T(8,128)S(1)}, f32[2,64,512]{2,1,0:T(8,128)S(1)}, u32[]{:S(2)}, u32[]{:S(2)}) collective-permute-start(f32[2,64,512]{2,1,0:T(8,128)S(1)} %shard_map.56.after_ref.refs_5_.refs_1_), channel_id=1, source_target_pairs={{0,1},{1,0},{2,3},{3,2},{4,5},{5,4},{6,7},{7,6},{8,9},{9,8},{10,11... | collective-permute-start | bytes 786440 | tf_op jit(solution)/shard_map/ppermute | solution.py:618
  4.8 10.5 %copy-start.4 = (s32[32,5]{0,1:T(8,128)S(1)}, s32[32,5]{0,1:T(8,128)}, u32[]{:S(2)}) copy-start(s32[32,5]{0,1:T(8,128)} %param.6) | copy-start | bytes 1924
  4.9 23.0 %collective-permute-start.5 = (f32[512,256]{1,0:T(8,128)S(1)}, f32[512,256]{1,0:T(8,128)S(1)}, u32[]{:S(2)}, u32[]{:S(2)}) collective-permute-start(f32[512,256]{1,0:T(8,128)S(1)} %get-tuple-element.61), channel_id=1, source_target_pairs={{0,1},{1,0},{2,3},{3,2},{4,5},{5,4},{6,7},{7,6},{8,9},{9,8},{10,11... | collective-permute-start | bytes 1572872 | tf_op jit(solution)/shard_map/ppermute | solution.py:618
  5.0 11.6 %collective-permute-start.2 = (f32[2,64,512]{2,1,0:T(8,128)S(1)}, f32[2,64,512]{2,1,0:T(8,128)S(1)}, u32[]{:S(2)}, u32[]{:S(2)}) collective-permute-start(f32[2,64,512]{2,1,0:T(8,128)S(1)} %shard_map.56.after_ref.refs_5_.refs_1_), channel_id=1, source_target_pairs={{0,30},{1,31},{2,4},{3,5},{4,2},{5,3},{6,8},{7,9},{8,6},{9,7},{10,... | collective-permute-start | bytes 786440 | tf_op jit(solution)/shard_map/ppermute | solution.py:618
  7.5 9.2 %collective-permute-start.1 = (f32[2,64,512]{2,1,0:T(8,128)S(1)}, f32[2,64,512]{2,1,0:T(8,128)S(1)}, u32[]{:S(2)}, u32[]{:S(2)}) collective-permute-start(f32[2,64,512]{2,1,0:T(8,128)S(1)} %shard_map.56.after_ref.refs_5_.refs_1_), channel_id=1, source_target_pairs={{0,2},{1,3},{2,0},{3,1},{4,6},{5,7},{6,4},{7,5},{8,10},{9,11},{10,... | collective-permute-start | bytes 786440 | tf_op jit(solution)/shard_map/ppermute | solution.py:618
  10.8 10.8 %collective-permute-start.4 = (f32[2,64,512]{2,1,0:T(8,128)S(1)}, f32[2,64,512]{2,1,0:T(8,128)S(1)}, u32[]{:S(2)}, u32[]{:S(2)}) collective-permute-start(f32[2,64,512]{2,1,0:T(8,128)S(1)} %collective-permute-done.refs_6_.refs_4_), channel_id=1, source_target_pairs={{0,30},{1,31},{2,4},{3,5},{4,2},{5,3},{6,8},{7,9},{8,6},{9,7},{10,... | collective-permute-start | bytes 786440 | tf_op jit(solution)/shard_map/ppermute | solution.py:618
  14.5 7.2 %collective-permute-start.3 = (f32[2,64,512]{2,1,0:T(8,128)S(1)}, f32[2,64,512]{2,1,0:T(8,128)S(1)}, u32[]{:S(2)}, u32[]{:S(2)}) collective-permute-start(f32[2,64,512]{2,1,0:T(8,128)S(1)} %collective-permute-done.refs_6_.refs_4_), channel_id=1, source_target_pairs={{0,2},{1,3},{2,0},{3,1},{4,6},{5,7},{6,4},{7,5},{8,10},{9,11},{10,... | collective-permute-start | bytes 786440 | tf_op jit(solution)/shard_map/ppermute | solution.py:618
  32.0 8.1 %collective-permute-start.8 = (f32[64,1024]{1,0:T(8,128)S(1)}, f32[64,1024]{1,0:T(8,128)S(1)}, u32[]{:S(2)}, u32[]{:S(2)}) collective-permute-start(f32[64,1024]{1,0:T(8,128)S(1)} %get-tuple-element.65.refs_7_.refs_1_), channel_id=1, source_target_pairs={{0,1},{1,0},{2,3},{3,2},{4,5},{5,4},{6,7},{7,6},{8,9},{9,8},{10,11... | collective-permute-start | bytes 786440 | tf_op jit(solution)/shard_map/ppermute | solution.py:618
  33.3 11.4 %collective-permute-start.7 = (f32[64,1024]{1,0:T(8,128)S(1)}, f32[64,1024]{1,0:T(8,128)S(1)}, u32[]{:S(2)}, u32[]{:S(2)}) collective-permute-start(f32[64,1024]{1,0:T(8,128)S(1)} %get-tuple-element.65.refs_7_.refs_1_), channel_id=1, source_target_pairs={{0,30},{1,31},{2,4},{3,5},{4,2},{5,3},{6,8},{7,9},{8,6},{9,7},{10,... | collective-permute-start | bytes 786440 | tf_op jit(solution)/shard_map/ppermute | solution.py:618
  35.0 9.7 %collective-permute-start.6 = (f32[64,1024]{1,0:T(8,128)S(1)}, f32[64,1024]{1,0:T(8,128)S(1)}, u32[]{:S(2)}, u32[]{:S(2)}) collective-permute-start(f32[64,1024]{1,0:T(8,128)S(1)} %get-tuple-element.65.refs_7_.refs_1_), channel_id=1, source_target_pairs={{0,2},{1,3},{2,0},{3,1},{4,6},{5,7},{6,4},{7,5},{8,10},{9,11},{10,... | collective-permute-start | bytes 786440 | tf_op jit(solution)/shard_map/ppermute | solution.py:618
  35.6 11.9 %collective-permute-start.10 = (f32[64,1024]{1,0:T(8,128)S(1)}, f32[64,1024]{1,0:T(8,128)S(1)}, u32[]{:S(2)}, u32[]{:S(2)}) collective-permute-start(f32[64,1024]{1,0:T(8,128)S(1)} %get-tuple-element.65.refs_7_.refs_1_), channel_id=1, source_target_pairs={{0,31},{1,30},{2,5},{3,4},{4,3},{5,2},{6,9},{7,8},{8,7},{9,6},{10,... | collective-permute-start | bytes 786440 | tf_op jit(solution)/shard_map/ppermute | solution.py:618
  40.1 7.4 %collective-permute-start.9 = (f32[64,1024]{1,0:T(8,128)S(1)}, f32[64,1024]{1,0:T(8,128)S(1)}, u32[]{:S(2)}, u32[]{:S(2)}) collective-permute-start(f32[64,1024]{1,0:T(8,128)S(1)} %collective-permute-done.8.refs_10_.refs_4_), channel_id=1, source_target_pairs={{0,2},{1,3},{2,0},{3,1},{4,6},{5,7},{6,4},{7,5},{8,10},{9,11},{10,... | collective-permute-start | bytes 786440 | tf_op jit(solution)/shard_map/ppermute | solution.py:618
  55.9 8.5 %collective-permute-start.12 = (f32[256,256]{1,0:T(8,128)S(1)}, f32[256,256]{1,0:T(8,128)S(1)}, u32[]{:S(2)}, u32[]{:S(2)}) collective-permute-start(f32[256,256]{1,0:T(8,128)S(1)} %get-tuple-element.84), channel_id=1, source_target_pairs={{0,1},{1,0},{2,3},{3,2},{4,5},{5,4},{6,7},{7,6},{8,9},{9,8},{10,11... | collective-permute-start | bytes 786440 | tf_op jit(solution)/shard_map/ppermute | solution.py:618
  57.2 10.5 %collective-permute-start.11 = (f32[256,256]{1,0:T(8,128)S(1)}, f32[256,256]{1,0:T(8,128)S(1)}, u32[]{:S(2)}, u32[]{:S(2)}) collective-permute-start(f32[256,256]{1,0:T(8,128)S(1)} %get-tuple-element.83), channel_id=1, source_target_pairs={{0,1},{1,0},{2,3},{3,2},{4,5},{5,4},{6,7},{7,6},{8,9},{9,8},{10,11... | collective-permute-start | bytes 786440 | tf_op jit(solution)/shard_map/ppermute | solution.py:618

commit v6 on v5

--- a/solution.py
+++ b/solution.py
@@ -289,6 +289,14 @@
             for target, part in zip(targets, split(jnp.transpose(block[low - span[0] :]))):
                 target[0:head, start + low : start + span[1]] = part
 
+    def less_diagonal(block, keep, span):
+        low, high = span[0], min(span[1], head)
+        if low >= high:
+            return block
+        middle = block[:, low:high] - keep * eye_ref[low : span[1], low:high]
+        pieces = [block[:, 0:low], middle, block[:, high:head]]
+        return jnp.concatenate([piece for piece in pieces if piece.shape[1]], axis=1)
+
     def put_corner(targets, start, block):
         for target, part in zip(targets, split(block)):
             target[head:n, start + head : start + n] = part
@@ -322,7 +330,7 @@
         x = []
         for k, span in enumerate(chunks):
             x.append(dot3(sides(source, span), first))
-            put(both, 0, span, weight * r[k] - keep * eye_ref[span[0] : span[1], 0:head])
+            put(both, 0, span, less_diagonal(weight * r[k], keep, span))
         put_corner(both, 0, weight * corners[:, 0:tail] - keep * eye_ref[head:n, head:n])
         waiting = (weight, x, corners[:, tail : 2 * tail])
         rho2 = keep * keep
@@ -477,9 +485,11 @@
     shift, zs = shift_of(z, d_ref), split(z)
     start = sh_ref.shape[1] - state_ref.shape[0]
     s = (sh_ref[...], sl_ref[...])
-    count = out_refs[0].shape[0]
-    for i, out_ref in enumerate(out_refs):
-        out_ref[...] = updated(state_ref[i * count : (i + 1) * count], start + i * count, s, shift, zs)
+    first = 0
+    for out_ref in out_refs:
+        stop = first + out_ref.shape[0]
+        out_ref[...] = updated(state_ref[first:stop], start + first, s, shift, zs)
+        first = stop
 
 
 def join_kernel(first, column_ref, mine_ref, theirs_ref, *refs):
@@ -589,10 +599,10 @@
     return call(kernel, outs, [VMEM] * (4 + len(states)), [sh, sl, d, z, *states], (), flops)
 
 
-def last(factored, state, parts=1):
+def last(factored, state, counts=None):
     sh, sl, d, g, xh, xl, more, *cross = factored
     n, width = sh.shape[0], state.shape[1]
-    outs = [((n, width), F32, VMEM)] + [((state.shape[0] // parts, width), F32, VMEM)] * parts
+    outs = [((n, width), F32, VMEM)] + [((count, width), F32, VMEM) for count in counts or state.shape[:1]]
     args = [more, sh, sl, d, g, xh, xl, state, *cross]
     flops = 12 * sh.shape[0] * sh.shape[1] * width
     ins = [SMEM] + [VMEM] * (len(args) - 1)
@@ -693,14 +703,15 @@
         factored = factor(
             pieces, batch, members, CHUNK, patches_next, *given, sources, early, [*anomaly, *done]
         )
-    z, *theirs = last(factored, states[1], 2)
+    most = half - half // 4
+    z, *theirs = last(factored, states[1], (most, half - most))
     theirs = [across(part) for part in theirs]
     (mine,) = update(factored, z, states[:1], (0,))
     joined = []
-    for part, other in enumerate(theirs):
+    for first, other in zip((0, most), theirs):
         count = other.shape[0]
         (out,) = call(
-            functools.partial(join_kernel, part * count),
+            functools.partial(join_kernel, first),
             [(state.shape, F32, anywhere)],
             [SMEM, VMEM, VMEM] + [anywhere] * len(joined),
             [place[1], mine, other, *joined],

time: 69 us -> 68.8 us (level)
  no operation moved by 1% of the time
where the time goes in v6:
time: 68.8 us; the launch traced here: 68.6 us
  Pallas kernels  26.9 us (39%)
  waiting for transfers between devices  22.5 us (33%)
  starting transfers between devices  17.5 us (25%)
  local copies, waits for them, and re-layouts  1.41 us (2%)
    pallas_call x13, Pallas kernels, call(): pl.pallas_call(kernel, out_shape=shapes, in_specs=ins, out_specs=[space f...  26.9 us
    ppermute x13, waiting for transfers between devices, permute(): return lax.ppermute(x, BOTH, table)  22.5 us
    ppermute x13, starting transfers between devices, permute(): return lax.ppermute(x, BOTH, table)  17.5 us
    unnamed x10, local copies, waits for them, and re-layouts  1.41 us
  transfers between devices with their start and end apart: 13, of which 7 were waited for; matrix products, arithmetic and copies ran while one was open for 0% of the time, Pallas kernels for 18%

profile of v6, /device:TPU:1, one launch (start us, length us, event | category | flops | bytes accessed | tf_op | source)
XLA Modules:
  0.0 68.6 jit_solution(11910616585339517191)
XLA Ops:
  0.0 1.2 %copy-done = f32[512,2,256]{2,1,0:T(2,128)S(1)} copy-done((f32[512,2,256]{2,1,0:T(2,128)S(1)}, f32[512,2,256]{2,1,0:T(2,128)}, u32[]{:S(2)}) %copy-start) | copy-done | bytes 1048600
  1.2 0.6 shard_map.55
  1.8 0.2 copy-done.1
  2.0 0.6 shard_map.56.after_ref.refs_5_.refs_1_
  2.6 2.1 %collective-permute-start = (f32[2,64,512]{2,1,0:T(8,128)S(1)}, f32[2,64,512]{2,1,0:T(8,128)S(1)}, u32[]{:S(2)}, u32[]{:S(2)}) collective-permute-start(f32[2,64,512]{2,1,0:T(8,128)S(1)} %shard_map.56.after_ref.refs_5_.refs_1_), channel_id=1, source_target_pairs={{0,1},{1,0},{2,3},{3,2},{4,5},{5,4},{6,7},{7,6},{8,9},{9,8},{10,11... | collective-permute-start | bytes 786440 | tf_op jit(solution)/shard_map/ppermute | solution.py:628
  5.0 2.5 %collective-permute-start.2 = (f32[2,64,512]{2,1,0:T(8,128)S(1)}, f32[2,64,512]{2,1,0:T(8,128)S(1)}, u32[]{:S(2)}, u32[]{:S(2)}) collective-permute-start(f32[2,64,512]{2,1,0:T(8,128)S(1)} %shard_map.56.after_ref.refs_5_.refs_1_), channel_id=1, source_target_pairs={{0,30},{1,31},{2,4},{3,5},{4,2},{5,3},{6,8},{7,9},{8,6},{9,7},{10,... | collective-permute-start | bytes 786440 | tf_op jit(solution)/shard_map/ppermute | solution.py:628
  7.5 2.3 %collective-permute-start.1 = (f32[2,64,512]{2,1,0:T(8,128)S(1)}, f32[2,64,512]{2,1,0:T(8,128)S(1)}, u32[]{:S(2)}, u32[]{:S(2)}) collective-permute-start(f32[2,64,512]{2,1,0:T(8,128)S(1)} %shard_map.56.after_ref.refs_5_.refs_1_), channel_id=1, source_target_pairs={{0,2},{1,3},{2,0},{3,1},{4,6},{5,7},{6,4},{7,5},{8,10},{9,11},{10,... | collective-permute-start | bytes 786440 | tf_op jit(solution)/shard_map/ppermute | solution.py:628
  9.8 1.0 %collective-permute-done.refs_6_.refs_4_ = f32[2,64,512]{2,1,0:T(8,128)S(1)} collective-permute-done((f32[2,64,512]{2,1,0:T(8,128)S(1)}, f32[2,64,512]{2,1,0:T(8,128)S(1)}, u32[]{:S(2)}, u32[]{:S(2)}) %collective-permute-start) | collective-permute-done | bytes 262176 | tf_op jit(solution)/shard_map/ppermute | solution.py:628
  10.8 3.7 %collective-permute-start.4 = (f32[2,64,512]{2,1,0:T(8,128)S(1)}, f32[2,64,512]{2,1,0:T(8,128)S(1)}, u32[]{:S(2)}, u32[]{:S(2)}) collective-permute-start(f32[2,64,512]{2,1,0:T(8,128)S(1)} %collective-permute-done.refs_6_.refs_4_), channel_id=1, source_target_pairs={{0,30},{1,31},{2,4},{3,5},{4,2},{5,3},{6,8},{7,9},{8,6},{9,7},{10,... | collective-permute-start | bytes 786440 | tf_op jit(solution)/shard_map/ppermute | solution.py:628
  14.5 0.9 %collective-permute-start.3 = (f32[2,64,512]{2,1,0:T(8,128)S(1)}, f32[2,64,512]{2,1,0:T(8,128)S(1)}, u32[]{:S(2)}, u32[]{:S(2)}) collective-permute-start(f32[2,64,512]{2,1,0:T(8,128)S(1)} %collective-permute-done.refs_6_.refs_4_), channel_id=1, source_target_pairs={{0,2},{1,3},{2,0},{3,1},{4,6},{5,7},{6,4},{7,5},{8,10},{9,11},{10,... | collective-permute-start | bytes 786440 | tf_op jit(solution)/shard_map/ppermute | solution.py:628
  15.3 1.3 %shard_map.58 = (bf16[384,1024]{1,0:T(8,128)(2,1)S(1)}, bf16[384,1024]{1,0:T(8,128)(2,1)S(1)}, f32[384,128]{1,0:T(8,128)S(1)}, f32[384,384]{1,0:T(8,128)S(1)}, f32[64,128]{1,0:T(8,128)S(1)}) custom-call(s32[1]{0:T(128)} %bitcast.1.region_ref.refs_0_, s32[1]{0:T(128)} %bitcast.column_ref.refs_1_, s32[5,32]{1,0:T(8,128)S(1)} %bitcast.3, ...), custom_call_target="tpu_custom_call" | custom-call | flops 301989888 | bytes 2949768 | tf_op jit(solution)/shard_map/pallas_call | solution.py:31
  16.6 5.0 %collective-permute-done.4.refs_6_ = f32[2,64,512]{2,1,0:T(8,128)S(1)} collective-permute-done((f32[2,64,512]{2,1,0:T(8,128)S(1)}, f32[2,64,512]{2,1,0:T(8,128)S(1)}, u32[]{:S(2)}, u32[]{:S(2)}) %collective-permute-start.4) | collective-permute-done | bytes 262176 | tf_op jit(solution)/shard_map/ppermute | solution.py:628
  21.6 6.2 %shard_map.59 = (bf16[384,1024]{1,0:T(8,128)(2,1)S(1)}, bf16[384,1024]{1,0:T(8,128)(2,1)S(1)}, f32[384,128]{1,0:T(8,128)S(1)}, f32[384,384]{1,0:T(8,128)S(1)}, b...) custom-call(f32[64,128]{1,0:T(8,128)S(1)} %get-tuple-element.49.refs, ...), custom_call_target="tpu_custom_call", output_to_operand_aliasing={{0}: (7, {}), {1}: (8, {}), {2}: (9, {}), {3}: (10, {})} | custom-call | flops 2038431744 | bytes 6914052 | tf_op jit(solution)/shard_map/pallas_call | solution.py:31
  27.8 4.1 %shard_map.60 = (f32[384,256]{1,0:T(8,128)S(1)}, f32[64,1024]{1,0:T(8,128)S(1)}) custom-call(s32[1]{0:T(128)} %bitcast.1.region_ref.refs_0_, s32[1]{0:T(128)} %bitcast.column_ref.refs_1_, s32[1]{0:T(128)} %get-tuple-element.57.n_ref, s32[32,2,64]{2,1,0:T(2,128)S(1)} %copy-done.1, bf16[384,1024]{1,0:T(8,128)(2,1)S(1)} %get-tuple-element.54.sh_ref, ...), custom_call_target="tpu_custom_call" | custom-call | flops 805306368 | bytes 4669452 | tf_op jit(solution)/shard_map/pallas_call | solution.py:31
  32.0 1.3 %collective-permute-start.8 = (f32[64,1024]{1,0:T(8,128)S(1)}, f32[64,1024]{1,0:T(8,128)S(1)}, u32[]{:S(2)}, u32[]{:S(2)}) collective-permute-start(f32[64,1024]{1,0:T(8,128)S(1)} %get-tuple-element.65.refs_7_.refs_1_), channel_id=1, source_target_pairs={{0,1},{1,0},{2,3},{3,2},{4,5},{5,4},{6,7},{7,6},{8,9},{9,8},{10,11... | collective-permute-start | bytes 786440 | tf_op jit(solution)/shard_map/ppermute | solution.py:628
  33.3 1.7 %collective-permute-start.7 = (f32[64,1024]{1,0:T(8,128)S(1)}, f32[64,1024]{1,0:T(8,128)S(1)}, u32[]{:S(2)}, u32[]{:S(2)}) collective-permute-start(f32[64,1024]{1,0:T(8,128)S(1)} %get-tuple-element.65.refs_7_.refs_1_), channel_id=1, source_target_pairs={{0,30},{1,31},{2,4},{3,5},{4,2},{5,3},{6,8},{7,9},{8,6},{9,7},{10,... | collective-permute-start | bytes 786440 | tf_op jit(solution)/shard_map/ppermute | solution.py:628
  35.0 0.6 collective-permute-start.6
  35.6 4.5 %collective-permute-done.8.refs_10_.refs_4_ = f32[64,1024]{1,0:T(8,128)S(1)} collective-permute-done((f32[64,1024]{1,0:T(8,128)S(1)}, f32[64,1024]{1,0:T(8,128)S(1)}, u32[]{:S(2)}, u32[]{:S(2)}) %collective-permute-start.8) | collective-permute-done | bytes 262176 | tf_op jit(solution)/shard_map/ppermute | solution.py:628
  40.0 0.7 %collective-permute-start.9 = (f32[64,1024]{1,0:T(8,128)S(1)}, f32[64,1024]{1,0:T(8,128)S(1)}, u32[]{:S(2)}, u32[]{:S(2)}) collective-permute-start(f32[64,1024]{1,0:T(8,128)S(1)} %collective-permute-done.8.refs_10_.refs_4_), channel_id=1, source_target_pairs={{0,2},{1,3},{2,0},{3,1},{4,6},{5,7},{6,4},{7,5},{8,10},{9,11},{10,... | collective-permute-start | bytes 786440 | tf_op jit(solution)/shard_map/ppermute | solution.py:628
  40.7 1.2 %shard_map.61 = (f32[512,256]{1,0:T(8,128)S(1)}, f32[512,256]{1,0:T(8,128)S(1)}, bf16[1024,256]{1,0:T(8,128)(2,1)S(1)}, bf16[1024,256]{1,0:T(8,128)(2,1)S(1)}) custom-call(bf16[384,1024]{1,0:T(8,128)(2,1)S(1)} %get-tuple-element.54.sh_ref, bf16[384,1024]{1,0:T(8,128)(2,1)S(1)} %get-tuple-element.55.sl_ref, f32[384,128]{1,0:T(8,128)S(1)} %get-tuple-element.56.d_ref, ...), custom_call_target="tpu_custom_call" | custom-call | flops 603979776 | bytes 5308416 | tf_op jit(solution)/shard_map/pallas_call | solution.py:31
  42.0 2.7 %collective-permute-done.7.refs_9_.refs_3_ = f32[64,1024]{1,0:T(8,128)S(1)} collective-permute-done((f32[64,1024]{1,0:T(8,128)S(1)}, f32[64,1024]{1,0:T(8,128)S(1)}, u32[]{:S(2)}, u32[]{:S(2)}) %collective-permute-start.7) | collective-permute-done | bytes 262176 | tf_op jit(solution)/shard_map/ppermute | solution.py:628
  44.7 2.1 %shard_map.62 = (bf16[384,1024]{1,0:T(8,128)(2,1)S(1)}, bf16[384,1024]{1,0:T(8,128)(2,1)S(1)}, f32[384,128]{1,0:T(8,128)S(1)}, f32[384,384]{1,0:T(8,128)S(1)}, f...) custom-call(s32[1]{0:T(128)} %bitcast.1.region_ref.refs_0_, s32[1]{0:T(128)} %bitcast.column_ref.refs_1_, ...), custom_call_target="tpu_custom_call" | custom-call | flops 905969664 | bytes 4915848 | tf_op jit(solution)/shard_map/pallas_call | solution.py:31
  46.7 0.7 %collective-permute-done.10.refs_6_ = f32[64,1024]{1,0:T(8,128)S(1)} collective-permute-done((f32[64,1024]{1,0:T(8,128)S(1)}, f32[64,1024]{1,0:T(8,128)S(1)}, u32[]{:S(2)}, u32[]{:S(2)}) %collective-permute-start.10) | collective-permute-done | bytes 262176 | tf_op jit(solution)/shard_map/ppermute | solution.py:628
  47.4 5.8 %shard_map.63 = (bf16[384,1024]{1,0:T(8,128)(2,1)S(1)}, bf16[384,1024]{1,0:T(8,128)(2,1)S(1)}, f32[384,128]{1,0:T(8,128)S(1)}, f32[384,384]{1,0:T(8,128)S(1)}, b...) custom-call(f32[64,128]{1,0:T(8,128)S(1)} %get-tuple-element.66.refs, ...), custom_call_target="tpu_custom_call", output_to_operand_aliasing={{0}: (9, {}), {1}: (10, {}), {2}: (11, {}), {3}: (12, {}), ... | custom-call | flops 2604662784 | bytes 8749060 | tf_op jit(solution)/shard_map/pallas_call | solution.py:31
  53.2 2.6 %shard_map.64 = (f32[384,256]{1,0:T(8,128)S(1)}, f32[384,256]{1,0:T(8,128)S(1)}, f32[128,256]{1,0:T(8,128)S(1)}) custom-call(s32[1]{0:T(128)} %get-tuple-element.75.n_ref, bf16[384,1024]{1,0:T(8,128)(2,1)S(1)} %get-tuple-element.72.sh_ref, bf16[384,1024]{1,0:T(8,128)(2,1)S(1)} %get-tuple-element.73.sl_ref, f32[384,128]{1,0:T(8,128)S(1)} %get-tuple-element.74.d_ref, ...), custom_call_target="tpu_custom_call" | custom-call | flops 1207959552 | bytes 4784132 | tf_op jit(solution)/shard_map/pallas_call | solution.py:31
  55.9 1.3 %collective-permute-start.12 = (f32[384,256]{1,0:T(8,128)S(1)}, f32[384,256]{1,0:T(8,128)S(1)}, u32[]{:S(2)}, u32[]{:S(2)}) collective-permute-start(f32[384,256]{1,0:T(8,128)S(1)} %get-tuple-element.84), channel_id=1, source_target_pairs={{0,1},{1,0},{2,3},{3,2},{4,5},{5,4},{6,7},{7,6},{8,9},{9,8},{10,11... | collective-permute-start | bytes 1179656 | tf_op jit(solution)/shard_map/ppermute | solution.py:628
  57.2 0.2 collective-permute-start.11
  57.4 0.6 shard_map.65.mine_ref
  58.0 8.3 %collective-permute-done.12.theirs_ref = f32[384,256]{1,0:T(8,128)S(1)} collective-permute-done((f32[384,256]{1,0:T(8,128)S(1)}, f32[384,256]{1,0:T(8,128)S(1)}, u32[]{:S(2)}, u32[]{:S(2)}) %collective-permute-start.12) | collective-permute-done | bytes 393248 | tf_op jit(solution)/shard_map/ppermute | solution.py:628
  66.2 1.0 %shard_map.66.refs_0_ = f32[512,2,256]{2,1,0:T(2,128)} custom-call(s32[1]{0:T(128)} %bitcast.column_ref.refs_1_, f32[512,256]{1,0:T(8,128)S(1)} %shard_map.65.mine_ref, f32[384,256]{1,0:T(8,128)S(1)} %collective-permute-done.12.theirs_ref), custom_call_target="tpu_custom_call" | custom-call | bytes 1966084 | tf_op jit(solution)/shard_map/pallas_call | solution.py:31
  67.3 0.4 collective-permute-done.11.theirs_ref
  67.6 0.8 %shard_map.67 = f32[512,2,256]{2,1,0:T(2,128)} custom-call(s32[1]{0:T(128)} %bitcast.column_ref.refs_1_, f32[512,256]{1,0:T(8,128)S(1)} %shard_map.65.mine_ref, f32[128,256]{1,0:T(8,128)S(1)} %collective-permute-done.11.theirs_ref, f32[512,2,256]{2,1,0:T(2,128)} %shard_map.66.refs_0_), custom_call_target="tpu_custom_call", output_to_operand_aliasing={{}: (3, {})} | custom-call | bytes 2752516 | tf_op jit(solution)/shard_map/pallas_call | solution.py:31
  (17 shorter events, 0.3 us)
Async XLA Ops:
  0.0 1.2 %copy-start = (f32[512,2,256]{2,1,0:T(2,128)S(1)}, f32[512,2,256]{2,1,0:T(2,128)}, u32[]{:S(2)}) copy-start(f32[512,2,256]{2,1,0:T(2,128)} %state_ref.1) | copy-start | bytes 3145732
  1.2 0.8 %copy-start.1 = (s32[32,2,64]{2,1,0:T(2,128)S(1)}, s32[32,2,64]{2,1,0:T(2,128)}, u32[]{:S(2)}) copy-start(s32[32,2,64]{2,1,0:T(2,128)} %cells_ref.3) | copy-start | bytes 49156
  2.0 2.8 %copy-start.2 = (f32[32,2,64]{2,1,0:T(2,128)S(1)}, f32[32,2,64]{2,1,0:T(2,128)}, u32[]{:S(2)}) copy-start(f32[32,2,64]{2,1,0:T(2,128)} %values_hbm.1) | copy-start | bytes 49156
  2.0 2.8 %copy-start.3 = (f32[32,2,64]{2,1,0:T(2,128)S(1)}, f32[32,2,64]{2,1,0:T(2,128)}, u32[]{:S(2)}) copy-start(f32[32,2,64]{2,1,0:T(2,128)} %var_hbm.1) | copy-start | bytes 49156
  2.6 8.2 %collective-permute-start = (f32[2,64,512]{2,1,0:T(8,128)S(1)}, f32[2,64,512]{2,1,0:T(8,128)S(1)}, u32[]{:S(2)}, u32[]{:S(2)}) collective-permute-start(f32[2,64,512]{2,1,0:T(8,128)S(1)} %shard_map.56.after_ref.refs_5_.refs_1_), channel_id=1, source_target_pairs={{0,1},{1,0},{2,3},{3,2},{4,5},{5,4},{6,7},{7,6},{8,9},{9,8},{10,11... | collective-permute-start | bytes 786440 | tf_op jit(solution)/shard_map/ppermute | solution.py:628
  4.8 10.5 %copy-start.4 = (s32[32,5]{0,1:T(8,128)S(1)}, s32[32,5]{0,1:T(8,128)}, u32[]{:S(2)}) copy-start(s32[32,5]{0,1:T(8,128)} %param.6) | copy-start | bytes 1924
  4.9 23.0 %collective-permute-start.5 = (f32[512,256]{1,0:T(8,128)S(1)}, f32[512,256]{1,0:T(8,128)S(1)}, u32[]{:S(2)}, u32[]{:S(2)}) collective-permute-start(f32[512,256]{1,0:T(8,128)S(1)} %get-tuple-element.61), channel_id=1, source_target_pairs={{0,1},{1,0},{2,3},{3,2},{4,5},{5,4},{6,7},{7,6},{8,9},{9,8},{10,11... | collective-permute-start | bytes 1572872 | tf_op jit(solution)/shard_map/ppermute | solution.py:628
  5.0 11.6 %collective-permute-start.2 = (f32[2,64,512]{2,1,0:T(8,128)S(1)}, f32[2,64,512]{2,1,0:T(8,128)S(1)}, u32[]{:S(2)}, u32[]{:S(2)}) collective-permute-start(f32[2,64,512]{2,1,0:T(8,128)S(1)} %shard_map.56.after_ref.refs_5_.refs_1_), channel_id=1, source_target_pairs={{0,30},{1,31},{2,4},{3,5},{4,2},{5,3},{6,8},{7,9},{8,6},{9,7},{10,... | collective-permute-start | bytes 786440 | tf_op jit(solution)/shard_map/ppermute | solution.py:628
  7.5 9.2 %collective-permute-start.1 = (f32[2,64,512]{2,1,0:T(8,128)S(1)}, f32[2,64,512]{2,1,0:T(8,128)S(1)}, u32[]{:S(2)}, u32[]{:S(2)}) collective-permute-start(f32[2,64,512]{2,1,0:T(8,128)S(1)} %shard_map.56.after_ref.refs_5_.refs_1_), channel_id=1, source_target_pairs={{0,2},{1,3},{2,0},{3,1},{4,6},{5,7},{6,4},{7,5},{8,10},{9,11},{10,... | collective-permute-start | bytes 786440 | tf_op jit(solution)/shard_map/ppermute | solution.py:628
  10.8 10.8 %collective-permute-start.4 = (f32[2,64,512]{2,1,0:T(8,128)S(1)}, f32[2,64,512]{2,1,0:T(8,128)S(1)}, u32[]{:S(2)}, u32[]{:S(2)}) collective-permute-start(f32[2,64,512]{2,1,0:T(8,128)S(1)} %collective-permute-done.refs_6_.refs_4_), channel_id=1, source_target_pairs={{0,30},{1,31},{2,4},{3,5},{4,2},{5,3},{6,8},{7,9},{8,6},{9,7},{10,... | collective-permute-start | bytes 786440 | tf_op jit(solution)/shard_map/ppermute | solution.py:628
  14.5 7.2 %collective-permute-start.3 = (f32[2,64,512]{2,1,0:T(8,128)S(1)}, f32[2,64,512]{2,1,0:T(8,128)S(1)}, u32[]{:S(2)}, u32[]{:S(2)}) collective-permute-start(f32[2,64,512]{2,1,0:T(8,128)S(1)} %collective-permute-done.refs_6_.refs_4_), channel_id=1, source_target_pairs={{0,2},{1,3},{2,0},{3,1},{4,6},{5,7},{6,4},{7,5},{8,10},{9,11},{10,... | collective-permute-start | bytes 786440 | tf_op jit(solution)/shard_map/ppermute | solution.py:628
  32.0 8.1 %collective-permute-start.8 = (f32[64,1024]{1,0:T(8,128)S(1)}, f32[64,1024]{1,0:T(8,128)S(1)}, u32[]{:S(2)}, u32[]{:S(2)}) collective-permute-start(f32[64,1024]{1,0:T(8,128)S(1)} %get-tuple-element.65.refs_7_.refs_1_), channel_id=1, source_target_pairs={{0,1},{1,0},{2,3},{3,2},{4,5},{5,4},{6,7},{7,6},{8,9},{9,8},{10,11... | collective-permute-start | bytes 786440 | tf_op jit(solution)/shard_map/ppermute | solution.py:628
  33.3 11.4 %collective-permute-start.7 = (f32[64,1024]{1,0:T(8,128)S(1)}, f32[64,1024]{1,0:T(8,128)S(1)}, u32[]{:S(2)}, u32[]{:S(2)}) collective-permute-start(f32[64,1024]{1,0:T(8,128)S(1)} %get-tuple-element.65.refs_7_.refs_1_), channel_id=1, source_target_pairs={{0,30},{1,31},{2,4},{3,5},{4,2},{5,3},{6,8},{7,9},{8,6},{9,7},{10,... | collective-permute-start | bytes 786440 | tf_op jit(solution)/shard_map/ppermute | solution.py:628
  35.0 9.7 %collective-permute-start.6 = (f32[64,1024]{1,0:T(8,128)S(1)}, f32[64,1024]{1,0:T(8,128)S(1)}, u32[]{:S(2)}, u32[]{:S(2)}) collective-permute-start(f32[64,1024]{1,0:T(8,128)S(1)} %get-tuple-element.65.refs_7_.refs_1_), channel_id=1, source_target_pairs={{0,2},{1,3},{2,0},{3,1},{4,6},{5,7},{6,4},{7,5},{8,10},{9,11},{10,... | collective-permute-start | bytes 786440 | tf_op jit(solution)/shard_map/ppermute | solution.py:628
  35.6 11.9 %collective-permute-start.10 = (f32[64,1024]{1,0:T(8,128)S(1)}, f32[64,1024]{1,0:T(8,128)S(1)}, u32[]{:S(2)}, u32[]{:S(2)}) collective-permute-start(f32[64,1024]{1,0:T(8,128)S(1)} %get-tuple-element.65.refs_7_.refs_1_), channel_id=1, source_target_pairs={{0,31},{1,30},{2,5},{3,4},{4,3},{5,2},{6,9},{7,8},{8,7},{9,6},{10,... | collective-permute-start | bytes 786440 | tf_op jit(solution)/shard_map/ppermute | solution.py:628
  40.0 7.4 %collective-permute-start.9 = (f32[64,1024]{1,0:T(8,128)S(1)}, f32[64,1024]{1,0:T(8,128)S(1)}, u32[]{:S(2)}, u32[]{:S(2)}) collective-permute-start(f32[64,1024]{1,0:T(8,128)S(1)} %collective-permute-done.8.refs_10_.refs_4_), channel_id=1, source_target_pairs={{0,2},{1,3},{2,0},{3,1},{4,6},{5,7},{6,4},{7,5},{8,10},{9,11},{10,... | collective-permute-start | bytes 786440 | tf_op jit(solution)/shard_map/ppermute | solution.py:628
  55.9 10.4 %collective-permute-start.12 = (f32[384,256]{1,0:T(8,128)S(1)}, f32[384,256]{1,0:T(8,128)S(1)}, u32[]{:S(2)}, u32[]{:S(2)}) collective-permute-start(f32[384,256]{1,0:T(8,128)S(1)} %get-tuple-element.84), channel_id=1, source_target_pairs={{0,1},{1,0},{2,3},{3,2},{4,5},{5,4},{6,7},{7,6},{8,9},{9,8},{10,11... | collective-permute-start | bytes 1179656 | tf_op jit(solution)/shard_map/ppermute | solution.py:628
  57.2 10.5 %collective-permute-start.11 = (f32[128,256]{1,0:T(8,128)S(1)}, f32[128,256]{1,0:T(8,128)S(1)}, u32[]{:S(2)}, u32[]{:S(2)}) collective-permute-start(f32[128,256]{1,0:T(8,128)S(1)} %get-tuple-element.83), channel_id=1, source_target_pairs={{0,1},{1,0},{2,3},{3,2},{4,5},{5,4},{6,7},{7,6},{8,9},{9,8},{10,11... | collective-permute-start | bytes 393224 | tf_op jit(solution)/shard_map/ppermute | solution.py:628

commit v7 on v6

--- a/solution.py
+++ b/solution.py
@@ -22,6 +22,7 @@
 MOST_STEPS = 15
 TILE = 256
 CHUNK = 128
+SOLVE_CHUNK = 192
 
 
 def call(kernel, outs, ins, args, scratch=(), flops=0, limit=16, aliases=None):
@@ -362,8 +363,8 @@
 
 def in_chunks(count, product, work):
     waiting = None
-    for start in range(0, count, CHUNK):
-        span = slice(start, min(start + CHUNK, count))
+    for start in range(0, count, SOLVE_CHUNK):
+        span = slice(start, min(start + SOLVE_CHUNK, count))
         result = product(span)
         if waiting is not None:
             work(*waiting)

time: 68.8 us -> 68.3 us (level)
  no operation moved by 1% of the time
where the time goes in v7:
time: 68.3 us; the launch traced here: 68.1 us
  Pallas kernels  26.5 us (39%)
  waiting for transfers between devices  22.5 us (33%)
  starting transfers between devices  17.5 us (26%)
  local copies, waits for them, and re-layouts  1.41 us (2%)
    pallas_call x13, Pallas kernels, call(): pl.pallas_call(kernel, out_shape=shapes, in_specs=ins, out_specs=[space f...  26.5 us
    ppermute x13, waiting for transfers between devices, permute(): return lax.ppermute(x, BOTH, table)  22.5 us
    ppermute x13, starting transfers between devices, permute(): return lax.ppermute(x, BOTH, table)  17.5 us
    unnamed x10, local copies, waits for them, and re-layouts  1.41 us
  transfers between devices with their start and end apart: 13, of which 7 were waited for; matrix products, arithmetic and copies ran while one was open for 0% of the time, Pallas kernels for 18%

profile of v7, /device:TPU:1, one launch (start us, length us, event | category | flops | bytes accessed | tf_op | source)
XLA Modules:
  0.0 68.1 jit_solution(14705695872686180861)
XLA Ops:
  0.0 1.2 %copy-done = f32[512,2,256]{2,1,0:T(2,128)S(1)} copy-done((f32[512,2,256]{2,1,0:T(2,128)S(1)}, f32[512,2,256]{2,1,0:T(2,128)}, u32[]{:S(2)}) %copy-start) | copy-done | bytes 1048600
  1.2 0.6 shard_map.55
  1.8 0.2 copy-done.1
  2.0 0.6 shard_map.56.after_ref.refs_5_.refs_1_
  2.6 2.1 %collective-permute-start = (f32[2,64,512]{2,1,0:T(8,128)S(1)}, f32[2,64,512]{2,1,0:T(8,128)S(1)}, u32[]{:S(2)}, u32[]{:S(2)}) collective-permute-start(f32[2,64,512]{2,1,0:T(8,128)S(1)} %shard_map.56.after_ref.refs_5_.refs_1_), channel_id=1, source_target_pairs={{0,1},{1,0},{2,3},{3,2},{4,5},{5,4},{6,7},{7,6},{8,9},{9,8},{10,11... | collective-permute-start | bytes 786440 | tf_op jit(solution)/shard_map/ppermute | solution.py:629
  5.0 2.5 %collective-permute-start.2 = (f32[2,64,512]{2,1,0:T(8,128)S(1)}, f32[2,64,512]{2,1,0:T(8,128)S(1)}, u32[]{:S(2)}, u32[]{:S(2)}) collective-permute-start(f32[2,64,512]{2,1,0:T(8,128)S(1)} %shard_map.56.after_ref.refs_5_.refs_1_), channel_id=1, source_target_pairs={{0,30},{1,31},{2,4},{3,5},{4,2},{5,3},{6,8},{7,9},{8,6},{9,7},{10,... | collective-permute-start | bytes 786440 | tf_op jit(solution)/shard_map/ppermute | solution.py:629
  7.5 2.3 %collective-permute-start.1 = (f32[2,64,512]{2,1,0:T(8,128)S(1)}, f32[2,64,512]{2,1,0:T(8,128)S(1)}, u32[]{:S(2)}, u32[]{:S(2)}) collective-permute-start(f32[2,64,512]{2,1,0:T(8,128)S(1)} %shard_map.56.after_ref.refs_5_.refs_1_), channel_id=1, source_target_pairs={{0,2},{1,3},{2,0},{3,1},{4,6},{5,7},{6,4},{7,5},{8,10},{9,11},{10,... | collective-permute-start | bytes 786440 | tf_op jit(solution)/shard_map/ppermute | solution.py:629
  9.8 1.0 %collective-permute-done.refs_6_.refs_4_ = f32[2,64,512]{2,1,0:T(8,128)S(1)} collective-permute-done((f32[2,64,512]{2,1,0:T(8,128)S(1)}, f32[2,64,512]{2,1,0:T(8,128)S(1)}, u32[]{:S(2)}, u32[]{:S(2)}) %collective-permute-start) | collective-permute-done | bytes 262176 | tf_op jit(solution)/shard_map/ppermute | solution.py:629
  10.8 3.7 %collective-permute-start.4 = (f32[2,64,512]{2,1,0:T(8,128)S(1)}, f32[2,64,512]{2,1,0:T(8,128)S(1)}, u32[]{:S(2)}, u32[]{:S(2)}) collective-permute-start(f32[2,64,512]{2,1,0:T(8,128)S(1)} %collective-permute-done.refs_6_.refs_4_), channel_id=1, source_target_pairs={{0,30},{1,31},{2,4},{3,5},{4,2},{5,3},{6,8},{7,9},{8,6},{9,7},{10,... | collective-permute-start | bytes 786440 | tf_op jit(solution)/shard_map/ppermute | solution.py:629
  14.5 0.9 %collective-permute-start.3 = (f32[2,64,512]{2,1,0:T(8,128)S(1)}, f32[2,64,512]{2,1,0:T(8,128)S(1)}, u32[]{:S(2)}, u32[]{:S(2)}) collective-permute-start(f32[2,64,512]{2,1,0:T(8,128)S(1)} %collective-permute-done.refs_6_.refs_4_), channel_id=1, source_target_pairs={{0,2},{1,3},{2,0},{3,1},{4,6},{5,7},{6,4},{7,5},{8,10},{9,11},{10,... | collective-permute-start | bytes 786440 | tf_op jit(solution)/shard_map/ppermute | solution.py:629
  15.3 1.3 %shard_map.58 = (bf16[384,1024]{1,0:T(8,128)(2,1)S(1)}, bf16[384,1024]{1,0:T(8,128)(2,1)S(1)}, f32[384,128]{1,0:T(8,128)S(1)}, f32[384,384]{1,0:T(8,128)S(1)}, f32[64,128]{1,0:T(8,128)S(1)}) custom-call(s32[1]{0:T(128)} %bitcast.1.region_ref.refs_0_, s32[1]{0:T(128)} %bitcast.column_ref.refs_1_, s32[5,32]{1,0:T(8,128)S(1)} %bitcast.3, ...), custom_call_target="tpu_custom_call" | custom-call | flops 301989888 | bytes 2949768 | tf_op jit(solution)/shard_map/pallas_call | solution.py:32
  16.6 5.0 %collective-permute-done.4.refs_6_ = f32[2,64,512]{2,1,0:T(8,128)S(1)} collective-permute-done((f32[2,64,512]{2,1,0:T(8,128)S(1)}, f32[2,64,512]{2,1,0:T(8,128)S(1)}, u32[]{:S(2)}, u32[]{:S(2)}) %collective-permute-start.4) | collective-permute-done | bytes 262176 | tf_op jit(solution)/shard_map/ppermute | solution.py:629
  21.6 6.2 %shard_map.59 = (bf16[384,1024]{1,0:T(8,128)(2,1)S(1)}, bf16[384,1024]{1,0:T(8,128)(2,1)S(1)}, f32[384,128]{1,0:T(8,128)S(1)}, f32[384,384]{1,0:T(8,128)S(1)}, b...) custom-call(f32[64,128]{1,0:T(8,128)S(1)} %get-tuple-element.49.refs, ...), custom_call_target="tpu_custom_call", output_to_operand_aliasing={{0}: (7, {}), {1}: (8, {}), {2}: (9, {}), {3}: (10, {})} | custom-call | flops 2038431744 | bytes 6914052 | tf_op jit(solution)/shard_map/pallas_call | solution.py:32
  27.8 3.8 %shard_map.60 = (f32[384,256]{1,0:T(8,128)S(1)}, f32[64,1024]{1,0:T(8,128)S(1)}) custom-call(s32[1]{0:T(128)} %bitcast.1.region_ref.refs_0_, s32[1]{0:T(128)} %bitcast.column_ref.refs_1_, s32[1]{0:T(128)} %get-tuple-element.57.n_ref, s32[32,2,64]{2,1,0:T(2,128)S(1)} %copy-done.1, bf16[384,1024]{1,0:T(8,128)(2,1)S(1)} %get-tuple-element.54.sh_ref, ...), custom_call_target="tpu_custom_call" | custom-call | flops 805306368 | bytes 4669452 | tf_op jit(solution)/shard_map/pallas_call | solution.py:32
  31.6 1.3 %collective-permute-start.8 = (f32[64,1024]{1,0:T(8,128)S(1)}, f32[64,1024]{1,0:T(8,128)S(1)}, u32[]{:S(2)}, u32[]{:S(2)}) collective-permute-start(f32[64,1024]{1,0:T(8,128)S(1)} %get-tuple-element.65.refs_7_.refs_1_), channel_id=1, source_target_pairs={{0,1},{1,0},{2,3},{3,2},{4,5},{5,4},{6,7},{7,6},{8,9},{9,8},{10,11... | collective-permute-start | bytes 786440 | tf_op jit(solution)/shard_map/ppermute | solution.py:629
  32.9 1.7 %collective-permute-start.7 = (f32[64,1024]{1,0:T(8,128)S(1)}, f32[64,1024]{1,0:T(8,128)S(1)}, u32[]{:S(2)}, u32[]{:S(2)}) collective-permute-start(f32[64,1024]{1,0:T(8,128)S(1)} %get-tuple-element.65.refs_7_.refs_1_), channel_id=1, source_target_pairs={{0,30},{1,31},{2,4},{3,5},{4,2},{5,3},{6,8},{7,9},{8,6},{9,7},{10,... | collective-permute-start | bytes 786440 | tf_op jit(solution)/shard_map/ppermute | solution.py:629
  34.7 0.6 collective-permute-start.6
  35.3 4.5 %collective-permute-done.8.refs_10_.refs_4_ = f32[64,1024]{1,0:T(8,128)S(1)} collective-permute-done((f32[64,1024]{1,0:T(8,128)S(1)}, f32[64,1024]{1,0:T(8,128)S(1)}, u32[]{:S(2)}, u32[]{:S(2)}) %collective-permute-start.8) | collective-permute-done | bytes 262176 | tf_op jit(solution)/shard_map/ppermute | solution.py:629
  39.7 0.7 %collective-permute-start.9 = (f32[64,1024]{1,0:T(8,128)S(1)}, f32[64,1024]{1,0:T(8,128)S(1)}, u32[]{:S(2)}, u32[]{:S(2)}) collective-permute-start(f32[64,1024]{1,0:T(8,128)S(1)} %collective-permute-done.8.refs_10_.refs_4_), channel_id=1, source_target_pairs={{0,2},{1,3},{2,0},{3,1},{4,6},{5,7},{6,4},{7,5},{8,10},{9,11},{10,... | collective-permute-start | bytes 786440 | tf_op jit(solution)/shard_map/ppermute | solution.py:629
  40.4 1.2 %shard_map.61 = (f32[512,256]{1,0:T(8,128)S(1)}, f32[512,256]{1,0:T(8,128)S(1)}, bf16[1024,256]{1,0:T(8,128)(2,1)S(1)}, bf16[1024,256]{1,0:T(8,128)(2,1)S(1)}) custom-call(bf16[384,1024]{1,0:T(8,128)(2,1)S(1)} %get-tuple-element.54.sh_ref, bf16[384,1024]{1,0:T(8,128)(2,1)S(1)} %get-tuple-element.55.sl_ref, f32[384,128]{1,0:T(8,128)S(1)} %get-tuple-element.56.d_ref, ...), custom_call_target="tpu_custom_call" | custom-call | flops 603979776 | bytes 5308416 | tf_op jit(solution)/shard_map/pallas_call | solution.py:32
  41.7 2.7 %collective-permute-done.7.refs_9_.refs_3_ = f32[64,1024]{1,0:T(8,128)S(1)} collective-permute-done((f32[64,1024]{1,0:T(8,128)S(1)}, f32[64,1024]{1,0:T(8,128)S(1)}, u32[]{:S(2)}, u32[]{:S(2)}) %collective-permute-start.7) | collective-permute-done | bytes 262176 | tf_op jit(solution)/shard_map/ppermute | solution.py:629
  44.4 2.1 %shard_map.62 = (bf16[384,1024]{1,0:T(8,128)(2,1)S(1)}, bf16[384,1024]{1,0:T(8,128)(2,1)S(1)}, f32[384,128]{1,0:T(8,128)S(1)}, f32[384,384]{1,0:T(8,128)S(1)}, f...) custom-call(s32[1]{0:T(128)} %bitcast.1.region_ref.refs_0_, s32[1]{0:T(128)} %bitcast.column_ref.refs_1_, ...), custom_call_target="tpu_custom_call" | custom-call | flops 905969664 | bytes 4915848 | tf_op jit(solution)/shard_map/pallas_call | solution.py:32
  46.4 0.7 %collective-permute-done.10.refs_6_ = f32[64,1024]{1,0:T(8,128)S(1)} collective-permute-done((f32[64,1024]{1,0:T(8,128)S(1)}, f32[64,1024]{1,0:T(8,128)S(1)}, u32[]{:S(2)}, u32[]{:S(2)}) %collective-permute-start.10) | collective-permute-done | bytes 262176 | tf_op jit(solution)/shard_map/ppermute | solution.py:629
  47.1 5.8 %shard_map.63 = (bf16[384,1024]{1,0:T(8,128)(2,1)S(1)}, bf16[384,1024]{1,0:T(8,128)(2,1)S(1)}, f32[384,128]{1,0:T(8,128)S(1)}, f32[384,384]{1,0:T(8,128)S(1)}, b...) custom-call(f32[64,128]{1,0:T(8,128)S(1)} %get-tuple-element.66.refs, ...), custom_call_target="tpu_custom_call", output_to_operand_aliasing={{0}: (9, {}), {1}: (10, {}), {2}: (11, {}), {3}: (12, {}), ... | custom-call | flops 2604662784 | bytes 8749060 | tf_op jit(solution)/shard_map/pallas_call | solution.py:32
  52.9 2.5 %shard_map.64 = (f32[384,256]{1,0:T(8,128)S(1)}, f32[384,256]{1,0:T(8,128)S(1)}, f32[128,256]{1,0:T(8,128)S(1)}) custom-call(s32[1]{0:T(128)} %get-tuple-element.75.n_ref, bf16[384,1024]{1,0:T(8,128)(2,1)S(1)} %get-tuple-element.72.sh_ref, bf16[384,1024]{1,0:T(8,128)(2,1)S(1)} %get-tuple-element.73.sl_ref, f32[384,128]{1,0:T(8,128)S(1)} %get-tuple-element.74.d_ref, ...), custom_call_target="tpu_custom_call" | custom-call | flops 1207959552 | bytes 4784132 | tf_op jit(solution)/shard_map/pallas_call | solution.py:32
  55.4 1.3 %collective-permute-start.12 = (f32[384,256]{1,0:T(8,128)S(1)}, f32[384,256]{1,0:T(8,128)S(1)}, u32[]{:S(2)}, u32[]{:S(2)}) collective-permute-start(f32[384,256]{1,0:T(8,128)S(1)} %get-tuple-element.84), channel_id=1, source_target_pairs={{0,1},{1,0},{2,3},{3,2},{4,5},{5,4},{6,7},{7,6},{8,9},{9,8},{10,11... | collective-permute-start | bytes 1179656 | tf_op jit(solution)/shard_map/ppermute | solution.py:629
  56.7 0.2 collective-permute-start.11
  56.9 0.6 shard_map.65.mine_ref
  57.5 8.3 %collective-permute-done.12.theirs_ref = f32[384,256]{1,0:T(8,128)S(1)} collective-permute-done((f32[384,256]{1,0:T(8,128)S(1)}, f32[384,256]{1,0:T(8,128)S(1)}, u32[]{:S(2)}, u32[]{:S(2)}) %collective-permute-start.12) | collective-permute-done | bytes 393248 | tf_op jit(solution)/shard_map/ppermute | solution.py:629
  65.7 1.0 %shard_map.66.refs_0_ = f32[512,2,256]{2,1,0:T(2,128)} custom-call(s32[1]{0:T(128)} %bitcast.column_ref.refs_1_, f32[512,256]{1,0:T(8,128)S(1)} %shard_map.65.mine_ref, f32[384,256]{1,0:T(8,128)S(1)} %collective-permute-done.12.theirs_ref), custom_call_target="tpu_custom_call" | custom-call | bytes 1966084 | tf_op jit(solution)/shard_map/pallas_call | solution.py:32
  66.8 0.4 collective-permute-done.11.theirs_ref
  67.1 0.8 %shard_map.67 = f32[512,2,256]{2,1,0:T(2,128)} custom-call(s32[1]{0:T(128)} %bitcast.column_ref.refs_1_, f32[512,256]{1,0:T(8,128)S(1)} %shard_map.65.mine_ref, f32[128,256]{1,0:T(8,128)S(1)} %collective-permute-done.11.theirs_ref, f32[512,2,256]{2,1,0:T(2,128)} %shard_map.66.refs_0_), custom_call_target="tpu_custom_call", output_to_operand_aliasing={{}: (3, {})} | custom-call | bytes 2752516 | tf_op jit(solution)/shard_map/pallas_call | solution.py:32
  (17 shorter events, 0.3 us)
Async XLA Ops:
  0.0 1.2 %copy-start = (f32[512,2,256]{2,1,0:T(2,128)S(1)}, f32[512,2,256]{2,1,0:T(2,128)}, u32[]{:S(2)}) copy-start(f32[512,2,256]{2,1,0:T(2,128)} %state_ref.1) | copy-start | bytes 3145732
  1.2 0.8 %copy-start.1 = (s32[32,2,64]{2,1,0:T(2,128)S(1)}, s32[32,2,64]{2,1,0:T(2,128)}, u32[]{:S(2)}) copy-start(s32[32,2,64]{2,1,0:T(2,128)} %cells_ref.3) | copy-start | bytes 49156
  2.0 2.8 %copy-start.2 = (f32[32,2,64]{2,1,0:T(2,128)S(1)}, f32[32,2,64]{2,1,0:T(2,128)}, u32[]{:S(2)}) copy-start(f32[32,2,64]{2,1,0:T(2,128)} %values_hbm.1) | copy-start | bytes 49156
  2.0 2.8 %copy-start.3 = (f32[32,2,64]{2,1,0:T(2,128)S(1)}, f32[32,2,64]{2,1,0:T(2,128)}, u32[]{:S(2)}) copy-start(f32[32,2,64]{2,1,0:T(2,128)} %var_hbm.1) | copy-start | bytes 49156
  2.6 8.2 %collective-permute-start = (f32[2,64,512]{2,1,0:T(8,128)S(1)}, f32[2,64,512]{2,1,0:T(8,128)S(1)}, u32[]{:S(2)}, u32[]{:S(2)}) collective-permute-start(f32[2,64,512]{2,1,0:T(8,128)S(1)} %shard_map.56.after_ref.refs_5_.refs_1_), channel_id=1, source_target_pairs={{0,1},{1,0},{2,3},{3,2},{4,5},{5,4},{6,7},{7,6},{8,9},{9,8},{10,11... | collective-permute-start | bytes 786440 | tf_op jit(solution)/shard_map/ppermute | solution.py:629
  4.8 10.5 %copy-start.4 = (s32[32,5]{0,1:T(8,128)S(1)}, s32[32,5]{0,1:T(8,128)}, u32[]{:S(2)}) copy-start(s32[32,5]{0,1:T(8,128)} %param.6) | copy-start | bytes 1924
  4.9 23.0 %collective-permute-start.5 = (f32[512,256]{1,0:T(8,128)S(1)}, f32[512,256]{1,0:T(8,128)S(1)}, u32[]{:S(2)}, u32[]{:S(2)}) collective-permute-start(f32[512,256]{1,0:T(8,128)S(1)} %get-tuple-element.61), channel_id=1, source_target_pairs={{0,1},{1,0},{2,3},{3,2},{4,5},{5,4},{6,7},{7,6},{8,9},{9,8},{10,11... | collective-permute-start | bytes 1572872 | tf_op jit(solution)/shard_map/ppermute | solution.py:629
  5.0 11.6 %collective-permute-start.2 = (f32[2,64,512]{2,1,0:T(8,128)S(1)}, f32[2,64,512]{2,1,0:T(8,128)S(1)}, u32[]{:S(2)}, u32[]{:S(2)}) collective-permute-start(f32[2,64,512]{2,1,0:T(8,128)S(1)} %shard_map.56.after_ref.refs_5_.refs_1_), channel_id=1, source_target_pairs={{0,30},{1,31},{2,4},{3,5},{4,2},{5,3},{6,8},{7,9},{8,6},{9,7},{10,... | collective-permute-start | bytes 786440 | tf_op jit(solution)/shard_map/ppermute | solution.py:629
  7.5 9.2 %collective-permute-start.1 = (f32[2,64,512]{2,1,0:T(8,128)S(1)}, f32[2,64,512]{2,1,0:T(8,128)S(1)}, u32[]{:S(2)}, u32[]{:S(2)}) collective-permute-start(f32[2,64,512]{2,1,0:T(8,128)S(1)} %shard_map.56.after_ref.refs_5_.refs_1_), channel_id=1, source_target_pairs={{0,2},{1,3},{2,0},{3,1},{4,6},{5,7},{6,4},{7,5},{8,10},{9,11},{10,... | collective-permute-start | bytes 786440 | tf_op jit(solution)/shard_map/ppermute | solution.py:629
  10.8 10.8 %collective-permute-start.4 = (f32[2,64,512]{2,1,0:T(8,128)S(1)}, f32[2,64,512]{2,1,0:T(8,128)S(1)}, u32[]{:S(2)}, u32[]{:S(2)}) collective-permute-start(f32[2,64,512]{2,1,0:T(8,128)S(1)} %collective-permute-done.refs_6_.refs_4_), channel_id=1, source_target_pairs={{0,30},{1,31},{2,4},{3,5},{4,2},{5,3},{6,8},{7,9},{8,6},{9,7},{10,... | collective-permute-start | bytes 786440 | tf_op jit(solution)/shard_map/ppermute | solution.py:629
  14.5 7.2 %collective-permute-start.3 = (f32[2,64,512]{2,1,0:T(8,128)S(1)}, f32[2,64,512]{2,1,0:T(8,128)S(1)}, u32[]{:S(2)}, u32[]{:S(2)}) collective-permute-start(f32[2,64,512]{2,1,0:T(8,128)S(1)} %collective-permute-done.refs_6_.refs_4_), channel_id=1, source_target_pairs={{0,2},{1,3},{2,0},{3,1},{4,6},{5,7},{6,4},{7,5},{8,10},{9,11},{10,... | collective-permute-start | bytes 786440 | tf_op jit(solution)/shard_map/ppermute | solution.py:629
  31.6 8.1 %collective-permute-start.8 = (f32[64,1024]{1,0:T(8,128)S(1)}, f32[64,1024]{1,0:T(8,128)S(1)}, u32[]{:S(2)}, u32[]{:S(2)}) collective-permute-start(f32[64,1024]{1,0:T(8,128)S(1)} %get-tuple-element.65.refs_7_.refs_1_), channel_id=1, source_target_pairs={{0,1},{1,0},{2,3},{3,2},{4,5},{5,4},{6,7},{7,6},{8,9},{9,8},{10,11... | collective-permute-start | bytes 786440 | tf_op jit(solution)/shard_map/ppermute | solution.py:629
  32.9 11.4 %collective-permute-start.7 = (f32[64,1024]{1,0:T(8,128)S(1)}, f32[64,1024]{1,0:T(8,128)S(1)}, u32[]{:S(2)}, u32[]{:S(2)}) collective-permute-start(f32[64,1024]{1,0:T(8,128)S(1)} %get-tuple-element.65.refs_7_.refs_1_), channel_id=1, source_target_pairs={{0,30},{1,31},{2,4},{3,5},{4,2},{5,3},{6,8},{7,9},{8,6},{9,7},{10,... | collective-permute-start | bytes 786440 | tf_op jit(solution)/shard_map/ppermute | solution.py:629
  34.7 9.7 %collective-permute-start.6 = (f32[64,1024]{1,0:T(8,128)S(1)}, f32[64,1024]{1,0:T(8,128)S(1)}, u32[]{:S(2)}, u32[]{:S(2)}) collective-permute-start(f32[64,1024]{1,0:T(8,128)S(1)} %get-tuple-element.65.refs_7_.refs_1_), channel_id=1, source_target_pairs={{0,2},{1,3},{2,0},{3,1},{4,6},{5,7},{6,4},{7,5},{8,10},{9,11},{10,... | collective-permute-start | bytes 786440 | tf_op jit(solution)/shard_map/ppermute | solution.py:629
  35.2 11.9 %collective-permute-start.10 = (f32[64,1024]{1,0:T(8,128)S(1)}, f32[64,1024]{1,0:T(8,128)S(1)}, u32[]{:S(2)}, u32[]{:S(2)}) collective-permute-start(f32[64,1024]{1,0:T(8,128)S(1)} %get-tuple-element.65.refs_7_.refs_1_), channel_id=1, source_target_pairs={{0,31},{1,30},{2,5},{3,4},{4,3},{5,2},{6,9},{7,8},{8,7},{9,6},{10,... | collective-permute-start | bytes 786440 | tf_op jit(solution)/shard_map/ppermute | solution.py:629
  39.7 7.4 %collective-permute-start.9 = (f32[64,1024]{1,0:T(8,128)S(1)}, f32[64,1024]{1,0:T(8,128)S(1)}, u32[]{:S(2)}, u32[]{:S(2)}) collective-permute-start(f32[64,1024]{1,0:T(8,128)S(1)} %collective-permute-done.8.refs_10_.refs_4_), channel_id=1, source_target_pairs={{0,2},{1,3},{2,0},{3,1},{4,6},{5,7},{6,4},{7,5},{8,10},{9,11},{10,... | collective-permute-start | bytes 786440 | tf_op jit(solution)/shard_map/ppermute | solution.py:629
  55.4 10.4 %collective-permute-start.12 = (f32[384,256]{1,0:T(8,128)S(1)}, f32[384,256]{1,0:T(8,128)S(1)}, u32[]{:S(2)}, u32[]{:S(2)}) collective-permute-start(f32[384,256]{1,0:T(8,128)S(1)} %get-tuple-element.84), channel_id=1, source_target_pairs={{0,1},{1,0},{2,3},{3,2},{4,5},{5,4},{6,7},{7,6},{8,9},{9,8},{10,11... | collective-permute-start | bytes 1179656 | tf_op jit(solution)/shard_map/ppermute | solution.py:629
  56.7 10.5 %collective-permute-start.11 = (f32[128,256]{1,0:T(8,128)S(1)}, f32[128,256]{1,0:T(8,128)S(1)}, u32[]{:S(2)}, u32[]{:S(2)}) collective-permute-start(f32[128,256]{1,0:T(8,128)S(1)} %get-tuple-element.83), channel_id=1, source_target_pairs={{0,1},{1,0},{2,3},{3,2},{4,5},{5,4},{6,7},{7,6},{8,9},{9,8},{10,11... | collective-permute-start | bytes 393224 | tf_op jit(solution)/shard_map/ppermute | solution.py:629

commit v8 on v7

--- a/solution.py
+++ b/solution.py
@@ -702,7 +702,7 @@
         states = [mine, theirs]
         done = prepare(pieces[:early], batch, members, patches_next, *given, anomaly, sources[:early], n)
         factored = factor(
-            pieces, batch, members, CHUNK, patches_next, *given, sources, early, [*anomaly, *done]
+            pieces, batch, members, SOLVE_CHUNK, patches_next, *given, sources, early, [*anomaly, *done]
         )
     most = half - half // 4
     z, *theirs = last(factored, states[1], (most, half - most))

time: 68.3 us -> 68.5 us (level)
  no operation moved by 1% of the time
where the time goes in v8:
time: 68.5 us; the launch traced here: 68.3 us
  Pallas kernels  26.6 us (39%)
  waiting for transfers between devices  22.5 us (33%)
  starting transfers between devices  17.5 us (26%)
  local copies, waits for them, and re-layouts  1.41 us (2%)
    pallas_call x13, Pallas kernels, call(): pl.pallas_call(kernel, out_shape=shapes, in_specs=ins, out_specs=[space f...  26.6 us
    ppermute x13, waiting for transfers between devices, permute(): return lax.ppermute(x, BOTH, table)  22.5 us
    ppermute x13, starting transfers between devices, permute(): return lax.ppermute(x, BOTH, table)  17.5 us
    unnamed x10, local copies, waits for them, and re-layouts  1.41 us
  transfers between devices with their start and end apart: 13, of which 7 were waited for; matrix products, arithmetic and copies ran while one was open for 0% of the time, Pallas kernels for 18%

profile of v8, /device:TPU:1, one launch (start us, length us, event | category | flops | bytes accessed | tf_op | source)
XLA Modules:
  0.0 68.3 jit_solution(18324200322320907422)
XLA Ops:
  0.0 1.2 %copy-done = f32[512,2,256]{2,1,0:T(2,128)S(1)} copy-done((f32[512,2,256]{2,1,0:T(2,128)S(1)}, f32[512,2,256]{2,1,0:T(2,128)}, u32[]{:S(2)}) %copy-start) | copy-done | bytes 1048600
  1.2 0.6 shard_map.55
  1.8 0.2 copy-done.1
  2.0 0.6 shard_map.56.after_ref.refs_5_.refs_1_
  2.6 2.1 %collective-permute-start = (f32[2,64,512]{2,1,0:T(8,128)S(1)}, f32[2,64,512]{2,1,0:T(8,128)S(1)}, u32[]{:S(2)}, u32[]{:S(2)}) collective-permute-start(f32[2,64,512]{2,1,0:T(8,128)S(1)} %shard_map.56.after_ref.refs_5_.refs_1_), channel_id=1, source_target_pairs={{0,1},{1,0},{2,3},{3,2},{4,5},{5,4},{6,7},{7,6},{8,9},{9,8},{10,11... | collective-permute-start | bytes 786440 | tf_op jit(solution)/shard_map/ppermute | solution.py:629
  5.0 2.5 %collective-permute-start.2 = (f32[2,64,512]{2,1,0:T(8,128)S(1)}, f32[2,64,512]{2,1,0:T(8,128)S(1)}, u32[]{:S(2)}, u32[]{:S(2)}) collective-permute-start(f32[2,64,512]{2,1,0:T(8,128)S(1)} %shard_map.56.after_ref.refs_5_.refs_1_), channel_id=1, source_target_pairs={{0,30},{1,31},{2,4},{3,5},{4,2},{5,3},{6,8},{7,9},{8,6},{9,7},{10,... | collective-permute-start | bytes 786440 | tf_op jit(solution)/shard_map/ppermute | solution.py:629
  7.5 2.3 %collective-permute-start.1 = (f32[2,64,512]{2,1,0:T(8,128)S(1)}, f32[2,64,512]{2,1,0:T(8,128)S(1)}, u32[]{:S(2)}, u32[]{:S(2)}) collective-permute-start(f32[2,64,512]{2,1,0:T(8,128)S(1)} %shard_map.56.after_ref.refs_5_.refs_1_), channel_id=1, source_target_pairs={{0,2},{1,3},{2,0},{3,1},{4,6},{5,7},{6,4},{7,5},{8,10},{9,11},{10,... | collective-permute-start | bytes 786440 | tf_op jit(solution)/shard_map/ppermute | solution.py:629
  9.8 1.0 %collective-permute-done.refs_6_.refs_4_ = f32[2,64,512]{2,1,0:T(8,128)S(1)} collective-permute-done((f32[2,64,512]{2,1,0:T(8,128)S(1)}, f32[2,64,512]{2,1,0:T(8,128)S(1)}, u32[]{:S(2)}, u32[]{:S(2)}) %collective-permute-start) | collective-permute-done | bytes 262176 | tf_op jit(solution)/shard_map/ppermute | solution.py:629
  10.8 3.7 %collective-permute-start.4 = (f32[2,64,512]{2,1,0:T(8,128)S(1)}, f32[2,64,512]{2,1,0:T(8,128)S(1)}, u32[]{:S(2)}, u32[]{:S(2)}) collective-permute-start(f32[2,64,512]{2,1,0:T(8,128)S(1)} %collective-permute-done.refs_6_.refs_4_), channel_id=1, source_target_pairs={{0,30},{1,31},{2,4},{3,5},{4,2},{5,3},{6,8},{7,9},{8,6},{9,7},{10,... | collective-permute-start | bytes 786440 | tf_op jit(solution)/shard_map/ppermute | solution.py:629
  14.5 0.9 %collective-permute-start.3 = (f32[2,64,512]{2,1,0:T(8,128)S(1)}, f32[2,64,512]{2,1,0:T(8,128)S(1)}, u32[]{:S(2)}, u32[]{:S(2)}) collective-permute-start(f32[2,64,512]{2,1,0:T(8,128)S(1)} %collective-permute-done.refs_6_.refs_4_), channel_id=1, source_target_pairs={{0,2},{1,3},{2,0},{3,1},{4,6},{5,7},{6,4},{7,5},{8,10},{9,11},{10,... | collective-permute-start | bytes 786440 | tf_op jit(solution)/shard_map/ppermute | solution.py:629
  15.3 1.3 %shard_map.58 = (bf16[384,1024]{1,0:T(8,128)(2,1)S(1)}, bf16[384,1024]{1,0:T(8,128)(2,1)S(1)}, f32[384,128]{1,0:T(8,128)S(1)}, f32[384,384]{1,0:T(8,128)S(1)}, f32[64,128]{1,0:T(8,128)S(1)}) custom-call(s32[1]{0:T(128)} %bitcast.1.region_ref.refs_0_, s32[1]{0:T(128)} %bitcast.column_ref.refs_1_, s32[5,32]{1,0:T(8,128)S(1)} %bitcast.3, ...), custom_call_target="tpu_custom_call" | custom-call | flops 301989888 | bytes 2949768 | tf_op jit(solution)/shard_map/pallas_call | solution.py:32
  16.6 5.0 %collective-permute-done.4.refs_6_ = f32[2,64,512]{2,1,0:T(8,128)S(1)} collective-permute-done((f32[2,64,512]{2,1,0:T(8,128)S(1)}, f32[2,64,512]{2,1,0:T(8,128)S(1)}, u32[]{:S(2)}, u32[]{:S(2)}) %collective-permute-start.4) | collective-permute-done | bytes 262176 | tf_op jit(solution)/shard_map/ppermute | solution.py:629
  21.6 6.2 %shard_map.59 = (bf16[384,1024]{1,0:T(8,128)(2,1)S(1)}, bf16[384,1024]{1,0:T(8,128)(2,1)S(1)}, f32[384,128]{1,0:T(8,128)S(1)}, f32[384,384]{1,0:T(8,128)S(1)}, b...) custom-call(f32[64,128]{1,0:T(8,128)S(1)} %get-tuple-element.49.refs, ...), custom_call_target="tpu_custom_call", output_to_operand_aliasing={{0}: (7, {}), {1}: (8, {}), {2}: (9, {}), {3}: (10, {})} | custom-call | flops 2038431744 | bytes 6914052 | tf_op jit(solution)/shard_map/pallas_call | solution.py:32
  27.8 3.8 %shard_map.60 = (f32[384,256]{1,0:T(8,128)S(1)}, f32[64,1024]{1,0:T(8,128)S(1)}) custom-call(s32[1]{0:T(128)} %bitcast.1.region_ref.refs_0_, s32[1]{0:T(128)} %bitcast.column_ref.refs_1_, s32[1]{0:T(128)} %get-tuple-element.57.n_ref, s32[32,2,64]{2,1,0:T(2,128)S(1)} %copy-done.1, bf16[384,1024]{1,0:T(8,128)(2,1)S(1)} %get-tuple-element.54.sh_ref, ...), custom_call_target="tpu_custom_call" | custom-call | flops 805306368 | bytes 4669452 | tf_op jit(solution)/shard_map/pallas_call | solution.py:32
  31.6 1.3 %collective-permute-start.8 = (f32[64,1024]{1,0:T(8,128)S(1)}, f32[64,1024]{1,0:T(8,128)S(1)}, u32[]{:S(2)}, u32[]{:S(2)}) collective-permute-start(f32[64,1024]{1,0:T(8,128)S(1)} %get-tuple-element.65.refs_7_.refs_1_), channel_id=1, source_target_pairs={{0,1},{1,0},{2,3},{3,2},{4,5},{5,4},{6,7},{7,6},{8,9},{9,8},{10,11... | collective-permute-start | bytes 786440 | tf_op jit(solution)/shard_map/ppermute | solution.py:629
  32.9 1.7 %collective-permute-start.7 = (f32[64,1024]{1,0:T(8,128)S(1)}, f32[64,1024]{1,0:T(8,128)S(1)}, u32[]{:S(2)}, u32[]{:S(2)}) collective-permute-start(f32[64,1024]{1,0:T(8,128)S(1)} %get-tuple-element.65.refs_7_.refs_1_), channel_id=1, source_target_pairs={{0,30},{1,31},{2,4},{3,5},{4,2},{5,3},{6,8},{7,9},{8,6},{9,7},{10,... | collective-permute-start | bytes 786440 | tf_op jit(solution)/shard_map/ppermute | solution.py:629
  34.7 0.6 collective-permute-start.6
  35.3 4.5 %collective-permute-done.8.refs_10_.refs_4_ = f32[64,1024]{1,0:T(8,128)S(1)} collective-permute-done((f32[64,1024]{1,0:T(8,128)S(1)}, f32[64,1024]{1,0:T(8,128)S(1)}, u32[]{:S(2)}, u32[]{:S(2)}) %collective-permute-start.8) | collective-permute-done | bytes 262176 | tf_op jit(solution)/shard_map/ppermute | solution.py:629
  39.7 0.7 %collective-permute-start.9 = (f32[64,1024]{1,0:T(8,128)S(1)}, f32[64,1024]{1,0:T(8,128)S(1)}, u32[]{:S(2)}, u32[]{:S(2)}) collective-permute-start(f32[64,1024]{1,0:T(8,128)S(1)} %collective-permute-done.8.refs_10_.refs_4_), channel_id=1, source_target_pairs={{0,2},{1,3},{2,0},{3,1},{4,6},{5,7},{6,4},{7,5},{8,10},{9,11},{10,... | collective-permute-start | bytes 786440 | tf_op jit(solution)/shard_map/ppermute | solution.py:629
  40.4 1.2 %shard_map.61 = (f32[512,256]{1,0:T(8,128)S(1)}, f32[512,256]{1,0:T(8,128)S(1)}, bf16[1024,256]{1,0:T(8,128)(2,1)S(1)}, bf16[1024,256]{1,0:T(8,128)(2,1)S(1)}) custom-call(bf16[384,1024]{1,0:T(8,128)(2,1)S(1)} %get-tuple-element.54.sh_ref, bf16[384,1024]{1,0:T(8,128)(2,1)S(1)} %get-tuple-element.55.sl_ref, f32[384,128]{1,0:T(8,128)S(1)} %get-tuple-element.56.d_ref, ...), custom_call_target="tpu_custom_call" | custom-call | flops 603979776 | bytes 5308416 | tf_op jit(solution)/shard_map/pallas_call | solution.py:32
  41.7 2.7 %collective-permute-done.7.refs_9_.refs_3_ = f32[64,1024]{1,0:T(8,128)S(1)} collective-permute-done((f32[64,1024]{1,0:T(8,128)S(1)}, f32[64,1024]{1,0:T(8,128)S(1)}, u32[]{:S(2)}, u32[]{:S(2)}) %collective-permute-start.7) | collective-permute-done | bytes 262176 | tf_op jit(solution)/shard_map/ppermute | solution.py:629
  44.4 2.1 %shard_map.62 = (bf16[384,1024]{1,0:T(8,128)(2,1)S(1)}, bf16[384,1024]{1,0:T(8,128)(2,1)S(1)}, f32[384,128]{1,0:T(8,128)S(1)}, f32[384,384]{1,0:T(8,128)S(1)}, f...) custom-call(s32[1]{0:T(128)} %bitcast.1.region_ref.refs_0_, s32[1]{0:T(128)} %bitcast.column_ref.refs_1_, ...), custom_call_target="tpu_custom_call" | custom-call | flops 905969664 | bytes 4915848 | tf_op jit(solution)/shard_map/pallas_call | solution.py:32
  46.4 0.7 %collective-permute-done.10.refs_6_ = f32[64,1024]{1,0:T(8,128)S(1)} collective-permute-done((f32[64,1024]{1,0:T(8,128)S(1)}, f32[64,1024]{1,0:T(8,128)S(1)}, u32[]{:S(2)}, u32[]{:S(2)}) %collective-permute-start.10) | collective-permute-done | bytes 262176 | tf_op jit(solution)/shard_map/ppermute | solution.py:629
  47.1 6.0 %shard_map.63 = (bf16[384,1024]{1,0:T(8,128)(2,1)S(1)}, bf16[384,1024]{1,0:T(8,128)(2,1)S(1)}, f32[384,128]{1,0:T(8,128)S(1)}, f32[384,384]{1,0:T(8,128)S(1)}, b...) custom-call(f32[64,128]{1,0:T(8,128)S(1)} %get-tuple-element.66.refs, ...), custom_call_target="tpu_custom_call", output_to_operand_aliasing={{0}: (9, {}), {1}: (10, {}), {2}: (11, {}), {3}: (12, {}), ... | custom-call | flops 2604662784 | bytes 8749060 | tf_op jit(solution)/shard_map/pallas_call | solution.py:32
  53.1 2.5 %shard_map.64 = (f32[384,256]{1,0:T(8,128)S(1)}, f32[384,256]{1,0:T(8,128)S(1)}, f32[128,256]{1,0:T(8,128)S(1)}) custom-call(s32[1]{0:T(128)} %get-tuple-element.75.n_ref, bf16[384,1024]{1,0:T(8,128)(2,1)S(1)} %get-tuple-element.72.sh_ref, bf16[384,1024]{1,0:T(8,128)(2,1)S(1)} %get-tuple-element.73.sl_ref, f32[384,128]{1,0:T(8,128)S(1)} %get-tuple-element.74.d_ref, ...), custom_call_target="tpu_custom_call" | custom-call | flops 1207959552 | bytes 4784132 | tf_op jit(solution)/shard_map/pallas_call | solution.py:32
  55.6 1.3 %collective-permute-start.12 = (f32[384,256]{1,0:T(8,128)S(1)}, f32[384,256]{1,0:T(8,128)S(1)}, u32[]{:S(2)}, u32[]{:S(2)}) collective-permute-start(f32[384,256]{1,0:T(8,128)S(1)} %get-tuple-element.84), channel_id=1, source_target_pairs={{0,1},{1,0},{2,3},{3,2},{4,5},{5,4},{6,7},{7,6},{8,9},{9,8},{10,11... | collective-permute-start | bytes 1179656 | tf_op jit(solution)/shard_map/ppermute | solution.py:629
  56.9 0.2 collective-permute-start.11
  57.1 0.6 shard_map.65.mine_ref
  57.7 8.3 %collective-permute-done.12.theirs_ref = f32[384,256]{1,0:T(8,128)S(1)} collective-permute-done((f32[384,256]{1,0:T(8,128)S(1)}, f32[384,256]{1,0:T(8,128)S(1)}, u32[]{:S(2)}, u32[]{:S(2)}) %collective-permute-start.12) | collective-permute-done | bytes 393248 | tf_op jit(solution)/shard_map/ppermute | solution.py:629
  65.9 1.0 %shard_map.66.refs_0_ = f32[512,2,256]{2,1,0:T(2,128)} custom-call(s32[1]{0:T(128)} %bitcast.column_ref.refs_1_, f32[512,256]{1,0:T(8,128)S(1)} %shard_map.65.mine_ref, f32[384,256]{1,0:T(8,128)S(1)} %collective-permute-done.12.theirs_ref), custom_call_target="tpu_custom_call" | custom-call | bytes 1966084 | tf_op jit(solution)/shard_map/pallas_call | solution.py:32
  67.0 0.4 collective-permute-done.11.theirs_ref
  67.4 0.8 %shard_map.67 = f32[512,2,256]{2,1,0:T(2,128)} custom-call(s32[1]{0:T(128)} %bitcast.column_ref.refs_1_, f32[512,256]{1,0:T(8,128)S(1)} %shard_map.65.mine_ref, f32[128,256]{1,0:T(8,128)S(1)} %collective-permute-done.11.theirs_ref, f32[512,2,256]{2,1,0:T(2,128)} %shard_map.66.refs_0_), custom_call_target="tpu_custom_call", output_to_operand_aliasing={{}: (3, {})} | custom-call | bytes 2752516 | tf_op jit(solution)/shard_map/pallas_call | solution.py:32
  (17 shorter events, 0.3 us)
Async XLA Ops:
  0.0 1.2 %copy-start = (f32[512,2,256]{2,1,0:T(2,128)S(1)}, f32[512,2,256]{2,1,0:T(2,128)}, u32[]{:S(2)}) copy-start(f32[512,2,256]{2,1,0:T(2,128)} %state_ref.1) | copy-start | bytes 3145732
  1.2 0.8 %copy-start.1 = (s32[32,2,64]{2,1,0:T(2,128)S(1)}, s32[32,2,64]{2,1,0:T(2,128)}, u32[]{:S(2)}) copy-start(s32[32,2,64]{2,1,0:T(2,128)} %cells_ref.3) | copy-start | bytes 49156
  2.0 2.8 %copy-start.2 = (f32[32,2,64]{2,1,0:T(2,128)S(1)}, f32[32,2,64]{2,1,0:T(2,128)}, u32[]{:S(2)}) copy-start(f32[32,2,64]{2,1,0:T(2,128)} %values_hbm.1) | copy-start | bytes 49156
  2.0 2.8 %copy-start.3 = (f32[32,2,64]{2,1,0:T(2,128)S(1)}, f32[32,2,64]{2,1,0:T(2,128)}, u32[]{:S(2)}) copy-start(f32[32,2,64]{2,1,0:T(2,128)} %var_hbm.1) | copy-start | bytes 49156
  2.6 8.2 %collective-permute-start = (f32[2,64,512]{2,1,0:T(8,128)S(1)}, f32[2,64,512]{2,1,0:T(8,128)S(1)}, u32[]{:S(2)}, u32[]{:S(2)}) collective-permute-start(f32[2,64,512]{2,1,0:T(8,128)S(1)} %shard_map.56.after_ref.refs_5_.refs_1_), channel_id=1, source_target_pairs={{0,1},{1,0},{2,3},{3,2},{4,5},{5,4},{6,7},{7,6},{8,9},{9,8},{10,11... | collective-permute-start | bytes 786440 | tf_op jit(solution)/shard_map/ppermute | solution.py:629
  4.8 10.5 %copy-start.4 = (s32[32,5]{0,1:T(8,128)S(1)}, s32[32,5]{0,1:T(8,128)}, u32[]{:S(2)}) copy-start(s32[32,5]{0,1:T(8,128)} %param.6) | copy-start | bytes 1924
  4.9 23.0 %collective-permute-start.5 = (f32[512,256]{1,0:T(8,128)S(1)}, f32[512,256]{1,0:T(8,128)S(1)}, u32[]{:S(2)}, u32[]{:S(2)}) collective-permute-start(f32[512,256]{1,0:T(8,128)S(1)} %get-tuple-element.61), channel_id=1, source_target_pairs={{0,1},{1,0},{2,3},{3,2},{4,5},{5,4},{6,7},{7,6},{8,9},{9,8},{10,11... | collective-permute-start | bytes 1572872 | tf_op jit(solution)/shard_map/ppermute | solution.py:629
  5.0 11.6 %collective-permute-start.2 = (f32[2,64,512]{2,1,0:T(8,128)S(1)}, f32[2,64,512]{2,1,0:T(8,128)S(1)}, u32[]{:S(2)}, u32[]{:S(2)}) collective-permute-start(f32[2,64,512]{2,1,0:T(8,128)S(1)} %shard_map.56.after_ref.refs_5_.refs_1_), channel_id=1, source_target_pairs={{0,30},{1,31},{2,4},{3,5},{4,2},{5,3},{6,8},{7,9},{8,6},{9,7},{10,... | collective-permute-start | bytes 786440 | tf_op jit(solution)/shard_map/ppermute | solution.py:629
  7.5 9.2 %collective-permute-start.1 = (f32[2,64,512]{2,1,0:T(8,128)S(1)}, f32[2,64,512]{2,1,0:T(8,128)S(1)}, u32[]{:S(2)}, u32[]{:S(2)}) collective-permute-start(f32[2,64,512]{2,1,0:T(8,128)S(1)} %shard_map.56.after_ref.refs_5_.refs_1_), channel_id=1, source_target_pairs={{0,2},{1,3},{2,0},{3,1},{4,6},{5,7},{6,4},{7,5},{8,10},{9,11},{10,... | collective-permute-start | bytes 786440 | tf_op jit(solution)/shard_map/ppermute | solution.py:629
  10.8 10.8 %collective-permute-start.4 = (f32[2,64,512]{2,1,0:T(8,128)S(1)}, f32[2,64,512]{2,1,0:T(8,128)S(1)}, u32[]{:S(2)}, u32[]{:S(2)}) collective-permute-start(f32[2,64,512]{2,1,0:T(8,128)S(1)} %collective-permute-done.refs_6_.refs_4_), channel_id=1, source_target_pairs={{0,30},{1,31},{2,4},{3,5},{4,2},{5,3},{6,8},{7,9},{8,6},{9,7},{10,... | collective-permute-start | bytes 786440 | tf_op jit(solution)/shard_map/ppermute | solution.py:629
  14.5 7.2 %collective-permute-start.3 = (f32[2,64,512]{2,1,0:T(8,128)S(1)}, f32[2,64,512]{2,1,0:T(8,128)S(1)}, u32[]{:S(2)}, u32[]{:S(2)}) collective-permute-start(f32[2,64,512]{2,1,0:T(8,128)S(1)} %collective-permute-done.refs_6_.refs_4_), channel_id=1, source_target_pairs={{0,2},{1,3},{2,0},{3,1},{4,6},{5,7},{6,4},{7,5},{8,10},{9,11},{10,... | collective-permute-start | bytes 786440 | tf_op jit(solution)/shard_map/ppermute | solution.py:629
  31.6 8.1 %collective-permute-start.8 = (f32[64,1024]{1,0:T(8,128)S(1)}, f32[64,1024]{1,0:T(8,128)S(1)}, u32[]{:S(2)}, u32[]{:S(2)}) collective-permute-start(f32[64,1024]{1,0:T(8,128)S(1)} %get-tuple-element.65.refs_7_.refs_1_), channel_id=1, source_target_pairs={{0,1},{1,0},{2,3},{3,2},{4,5},{5,4},{6,7},{7,6},{8,9},{9,8},{10,11... | collective-permute-start | bytes 786440 | tf_op jit(solution)/shard_map/ppermute | solution.py:629
  32.9 11.4 %collective-permute-start.7 = (f32[64,1024]{1,0:T(8,128)S(1)}, f32[64,1024]{1,0:T(8,128)S(1)}, u32[]{:S(2)}, u32[]{:S(2)}) collective-permute-start(f32[64,1024]{1,0:T(8,128)S(1)} %get-tuple-element.65.refs_7_.refs_1_), channel_id=1, source_target_pairs={{0,30},{1,31},{2,4},{3,5},{4,2},{5,3},{6,8},{7,9},{8,6},{9,7},{10,... | collective-permute-start | bytes 786440 | tf_op jit(solution)/shard_map/ppermute | solution.py:629
  34.7 9.7 %collective-permute-start.6 = (f32[64,1024]{1,0:T(8,128)S(1)}, f32[64,1024]{1,0:T(8,128)S(1)}, u32[]{:S(2)}, u32[]{:S(2)}) collective-permute-start(f32[64,1024]{1,0:T(8,128)S(1)} %get-tuple-element.65.refs_7_.refs_1_), channel_id=1, source_target_pairs={{0,2},{1,3},{2,0},{3,1},{4,6},{5,7},{6,4},{7,5},{8,10},{9,11},{10,... | collective-permute-start | bytes 786440 | tf_op jit(solution)/shard_map/ppermute | solution.py:629
  35.2 11.9 %collective-permute-start.10 = (f32[64,1024]{1,0:T(8,128)S(1)}, f32[64,1024]{1,0:T(8,128)S(1)}, u32[]{:S(2)}, u32[]{:S(2)}) collective-permute-start(f32[64,1024]{1,0:T(8,128)S(1)} %get-tuple-element.65.refs_7_.refs_1_), channel_id=1, source_target_pairs={{0,31},{1,30},{2,5},{3,4},{4,3},{5,2},{6,9},{7,8},{8,7},{9,6},{10,... | collective-permute-start | bytes 786440 | tf_op jit(solution)/shard_map/ppermute | solution.py:629
  39.7 7.4 %collective-permute-start.9 = (f32[64,1024]{1,0:T(8,128)S(1)}, f32[64,1024]{1,0:T(8,128)S(1)}, u32[]{:S(2)}, u32[]{:S(2)}) collective-permute-start(f32[64,1024]{1,0:T(8,128)S(1)} %collective-permute-done.8.refs_10_.refs_4_), channel_id=1, source_target_pairs={{0,2},{1,3},{2,0},{3,1},{4,6},{5,7},{6,4},{7,5},{8,10},{9,11},{10,... | collective-permute-start | bytes 786440 | tf_op jit(solution)/shard_map/ppermute | solution.py:629
  55.6 10.4 %collective-permute-start.12 = (f32[384,256]{1,0:T(8,128)S(1)}, f32[384,256]{1,0:T(8,128)S(1)}, u32[]{:S(2)}, u32[]{:S(2)}) collective-permute-start(f32[384,256]{1,0:T(8,128)S(1)} %get-tuple-element.84), channel_id=1, source_target_pairs={{0,1},{1,0},{2,3},{3,2},{4,5},{5,4},{6,7},{7,6},{8,9},{9,8},{10,11... | collective-permute-start | bytes 1179656 | tf_op jit(solution)/shard_map/ppermute | solution.py:629
  56.9 10.5 %collective-permute-start.11 = (f32[128,256]{1,0:T(8,128)S(1)}, f32[128,256]{1,0:T(8,128)S(1)}, u32[]{:S(2)}, u32[]{:S(2)}) collective-permute-start(f32[128,256]{1,0:T(8,128)S(1)} %get-tuple-element.83), channel_id=1, source_target_pairs={{0,1},{1,0},{2,3},{3,2},{4,5},{5,4},{6,7},{7,6},{8,9},{9,8},{10,11... | collective-permute-start | bytes 393224 | tf_op jit(solution)/shard_map/ppermute | solution.py:629
